TPU v7x, 128 devices: a whole 4x4x4 slice. The times are simulated.
128 devices in a mesh: clus: 32 (over y, x, core), rhs: 4 (over z).
Axes of the slice: x: 4, y: 4, z: 4, core: 2. Of those that a mesh axis runs over, the one named last changes fastest.
Arguments:
- sources: bfloat16 [128, 131072], P(None, 'clus'), may hold values from -6 to 6
- leaf_basis: bfloat16 [1024, 128, 64], P('clus'), may hold values from -0.5 to 0.5
- transfer: bfloat16 [1024, 64, 64], P('clus'), may hold values from -0.375 to 0.375
- far_leaf: int32 [1024, 8], P('clus'), may hold values from 0 to 1023
- leaf_coupling: bfloat16 [1024, 8, 64, 64], P('clus'), may hold values from -0.25 to 0.25
- far_par: int32 [256, 8], P('clus'), may hold values from 0 to 255
- par_coupling: bfloat16 [256, 8, 64, 64], P('clus'), may hold values from -0.25 to 0.25
- near_list: int32 [1024, 8], P('clus', 'rhs'), may hold values from 0 to 1023, as said below
- near_count: int32 [1024], P('clus'), may hold values from 3 to 8, as said below
- near_block: bfloat16 [1024, 8, 128, 128], P('clus', 'rhs'), may hold values from -0.25 to 0.25
Outputs:
- potential: bfloat16 [128, 131072], P('rhs', 'clus')
Inputs may be any that keep to these rules, and one draw needn't show every extreme that they name: `near_list`: slot 0 of leaf t is t itself; every entry of leaf t names a leaf held by the same index of clus as t or by one of the two beside it (leaves are split in order, 32 to an index). Slot 1 names a leaf of the index before and slot 2 one of the index after, where those exist. `near_count`: slots at or past the count are not used; some leaf uses all 8; the count varies strongly between indices of clus.
All inputs are finite; a program needn't handle non-finite values.
Results may differ from a plain program's by a relative error of at most 0.0046.
Values may be sent and summed in bfloat16 or wider, within the bound.
No kernel may reach another device: no remote copies, remote signals or barrier semaphores. Data moves between devices by JAX's collectives and lax.ppermute only.
A program may use at most 128 MiB of HBM per device.

v0:
```python
import jax
import jax.numpy as jnp
from jax import lax
from jax.sharding import PartitionSpec as P


def extended(cells, sides, width):
    for axis, dim in sides:
        count = lax.axis_size(axis)
        ends = count - 1
        head = lax.slice_in_dim(cells, 0, width, axis=dim)
        tail = lax.slice_in_dim(cells, cells.shape[dim] - width, cells.shape[dim], axis=dim)
        cells = jnp.concatenate(
            [
                lax.ppermute(tail, axis, [(i, (i + 1) % count) for i in range(ends)]),
                cells,
                lax.ppermute(head, axis, [((i + 1) % count, i) for i in range(ends)]),
            ],
            axis=dim,
        )
    return cells


def collect_rows(running, fragment, indices, first_row, active):
    amount = fragment.shape[1]
    offset = indices - first_row
    inside = (offset >= 0) & (offset < amount) & active
    chosen = jnp.take(fragment, jnp.clip(offset, 0, amount - 1), axis=1)
    return jnp.where(inside[None, :, :, None], chosen, running)


def per_device(
    sources,
    leaf_basis,
    transfer,
    far_leaf,
    leaf_coupling,
    far_par,
    par_coupling,
    near_list,
    near_count,
    near_block,
):
    full_cols, col_span = sources.shape
    leaf_count, leaf_size, basis_rank = leaf_basis.shape
    slot_count = near_list.shape[1]
    col_count = full_cols // lax.axis_size("rhs")
    blocks = sources.reshape(full_cols, leaf_count, leaf_size)
    own_cols = lax.dynamic_slice_in_dim(blocks, lax.axis_index("rhs") * col_count, col_count, 0)
    leaf_coef = jnp.einsum(
        "rlp,lpk->rlk", own_cols, leaf_basis, preferred_element_type=jnp.float32
    ).astype(jnp.bfloat16)
    lifted = jnp.einsum("rlj,ljk->rlk", leaf_coef, transfer, preferred_element_type=jnp.float32)
    parent_count = leaf_count // 4
    par_coef = (
        lifted.reshape(col_count, parent_count, 4, basis_rank).sum(axis=2).astype(jnp.bfloat16)
    )
    every_leaf = jnp.ones(far_leaf.shape, dtype=bool)
    leaf_start = jnp.zeros((col_count, leaf_count, far_leaf.shape[1], basis_rank), jnp.bfloat16)
    leaf_source = collect_rows(
        leaf_start,
        lax.all_gather(leaf_coef, "clus", axis=1, tiled=True),
        far_leaf,
        jnp.int32(0),
        every_leaf,
    )
    leaf_field = jnp.einsum(
        "tjab,rtjb->rta", leaf_coupling, leaf_source, preferred_element_type=jnp.float32
    )
    every_parent = jnp.ones(far_par.shape, dtype=bool)
    parent_start = jnp.zeros((col_count, parent_count, far_par.shape[1], basis_rank), jnp.bfloat16)
    par_source = collect_rows(
        parent_start,
        lax.all_gather(par_coef, "clus", axis=1, tiled=True),
        far_par,
        jnp.int32(0),
        every_parent,
    )
    par_field = jnp.einsum(
        "qjab,rqjb->rqa", par_coupling, par_source, preferred_element_type=jnp.float32
    ).astype(jnp.bfloat16)
    spread = jnp.repeat(par_field, 4, axis=1)
    downward = (
        leaf_field
        + jnp.einsum("ljk,rlk->rlj", transfer, spread, preferred_element_type=jnp.float32)
    ).astype(jnp.bfloat16)
    far_out = jnp.einsum("lpk,rlk->rlp", leaf_basis, downward, preferred_element_type=jnp.float32)
    first_row = (lax.axis_index("clus") - 1) * leaf_count
    slot_ids = lax.axis_index("rhs") * slot_count + jnp.arange(slot_count, dtype=jnp.int32)
    active = slot_ids[None, :] < near_count[:, None]
    widened = extended(blocks, (("clus", 1),), leaf_count)
    near_start = jnp.zeros((full_cols, leaf_count, slot_count, leaf_size), jnp.bfloat16)
    near_source = collect_rows(near_start, widened, near_list, first_row, active)
    partial_near = jnp.einsum(
        "tjpq,rtjq->rtp", near_block, near_source, preferred_element_type=jnp.float32
    )
    near_out = lax.psum_scatter(partial_near, "rhs", scatter_dimension=0, tiled=True)
    return (far_out + near_out).reshape(col_count, col_span).astype(jnp.bfloat16)


def solution(mesh):
    in_specs = (
        P(None, "clus"),
        P("clus", None, None),
        P("clus", None, None),
        P("clus", None),
        P("clus", None, None, None),
        P("clus", None),
        P("clus", None, None, None),
        P("clus", "rhs"),
        P("clus"),
        P("clus", "rhs", None, None),
    )
    out_specs = P("rhs", "clus")
    return jax.shard_map(
        per_device, mesh=mesh, in_specs=in_specs, out_specs=out_specs, check_vma=False
    )
```

profile of v0, /device:TPU:6, one launch (start us, length us, event | category | flops | bytes accessed | tf_op | source)
XLA Modules:
  0.0 137.2 jit_solution(16481694197329578423)
XLA Ops:
  7.4 1.8 %copy.30 = bf16[128,4096]{0,1:T(8,128)(2,1)S(1)} copy(bf16[128,4096]{1,0:T(8,128)(2,1)} %param.10) | data formatting | bytes 2097152 | tf_op args[0]
  9.2 2.0 %fusion.21 = bf16[32,32,64]{2,0,1:T(8,128)(2,1)S(1)} fusion(bf16[32,128,64]{1,2,0:T(8,128)(2,1)} %param.11, bf16[128,32,128]{0,2,1:T(8,128)(2,1)S(1)} %bitcast.67, s32[]{:T(128)S(6)} %select_n.43), kind=kOutput, calls=%fused_computation.24 | convolution fusion | flops 16842752 | bytes 1703940 | tf_op jit(solution)/shard_map/rlp,lpk->rlk/dot_general | solution.py:50
  11.2 2.1 %bitcast_reduce_fusion = bf16[32,8,64]{2,0,1:T(8,128)(2,1)} fusion(bf16[32,32,64]{2,0,1:T(8,128)(2,1)S(1)} %fusion.21, bf16[32,64,64]{2,1,0:T(8,128)(2,1)} %param.12), kind=kOutput, calls=%fused_computation.35 | convolution fusion | flops 8437760 | bytes 425984 | tf_op jit(solution)/shard_map/rlj,ljk->rlk/dot_general | solution.py:53
  13.3 0.7 all-gather.3.cloned.1.call-update
  14.0 1.9 %collective-permute-start = (bf16[128,32,128]{0,2,1:T(8,128)(2,1)S(1)}, bf16[128,32,128]{0,2,1:T(8,128)(2,1)}, u32[]{:S(2)}, u32[]{:S(2)}) collective-permute-start(bf16[128,32,128]{0,2,1:T(8,128)(2,1)S(1)} %bitcast.68), channel_id=1, source_target_pairs={{0,4},{4,8},{8,12},{12,16},{16,20},{20,24},{24,28},{28,32},{32,36}... | collective-permute-start | bytes 3145736 | tf_op jit(solution)/shard_map/ppermute | solution.py:15
  16.0 3.6 %collective-permute-start.1 = (bf16[128,32,128]{0,2,1:T(8,128)(2,1)S(1)}, bf16[128,32,128]{0,2,1:T(8,128)(2,1)}, u32[]{:S(2)}, u32[]{:S(2)}) collective-permute-start(bf16[128,32,128]{0,2,1:T(8,128)(2,1)S(1)} %bitcast.69), channel_id=1, source_target_pairs={{4,0},{8,4},{12,8},{16,12},{20,16},{24,20},{28,24},{32,28},{36,32}... | collective-permute-start | bytes 3145736 | tf_op jit(solution)/shard_map/ppermute | solution.py:17
  19.8 0.1 reshape.55
  19.9 0.1 copy.33
  20.0 0.1 copy.34
  20.1 10.6 %collective-permute-done = bf16[128,32,128]{0,2,1:T(8,128)(2,1)} collective-permute-done((bf16[128,32,128]{0,2,1:T(8,128)(2,1)S(1)}, bf16[128,32,128]{0,2,1:T(8,128)(2,1)}, u32[]{:S(2)}, u32[]{:S(2)}) %collective-permute-start) | collective-permute-done | bytes 1048608 | tf_op jit(solution)/shard_map/ppermute | solution.py:15
  30.7 2.0 %collective-permute-done.1 = bf16[128,32,128]{0,2,1:T(8,128)(2,1)} collective-permute-done((bf16[128,32,128]{0,2,1:T(8,128)(2,1)S(1)}, bf16[128,32,128]{0,2,1:T(8,128)(2,1)}, u32[]{:S(2)}, u32[]{:S(2)}) %collective-permute-start.1) | collective-permute-done | bytes 1048608 | tf_op jit(solution)/shard_map/ppermute | solution.py:17
  32.7 3.1 %pad_maximum_fusion = bf16[128,96,128]{0,2,1:T(8,128)(2,1)} fusion(bf16[128,32,128]{0,2,1:T(8,128)(2,1)} %collective-permute-done.1, bf16[128,32,128]{0,2,1:T(8,128)(2,1)S(1)} %bitcast.70, bf16[128,32,128]{0,2,1:T(8,128)(2,1)} %collective-permute-done), kind=kLoop, calls=%fused_computation.3 | loop fusion | flops 3145728 | bytes 6291456 | tf_op jit(solution)/shard_map/concatenate | solution.py:13
  35.8 4.0 %gather_fusion.2 = bf16[64,128,128]{1,2,0:T(8,128)(2,1)} fusion(bf16[128,96,128]{0,2,1:T(8,128)(2,1)} %pad_maximum_fusion, s32[1024]{0:T(1024)S(1)} %pad_clamp_fusion), kind=kCustom, calls=%fused_computation.2 | custom fusion | bytes 4194560 | tf_op jit(solution)/shard_map/jit(_take)/gather | solution.py:28
  39.8 4.1 %copy.36 = bf16[32,2,128,128]{3,2,1,0:T(8,128)(2,1)} copy(bf16[32,2,128,128]{2,3,1,0:T(8,128)(2,1)} %bitcast.71) | data formatting | bytes 4194304 | tf_op jit(solution)/shard_map/jit(_take)/gather | solution.py:28
  43.8 3.7 %fusion.12 = f32[128,32,128]{2,0,1:T(8,128)} fusion(bf16[32,2,128,128]{3,2,1,0:T(8,128)(2,1)S(1)} %copy-done, bf16[32,2,128,128]{3,2,1,0:T(8,128)(2,1)} %copy.36, pred[32,2]{1,0:T(8,128)(4,1)S(1)} %copy.33, pred[32,2]{1,0:T(8,128)(4,1)S(1)} %copy.34), kind=kOutput, calls=%fused_computation.16 | convolution fusion | flops 270532608 | bytes 6291584 | tf_op jit(solution)/shard_map/tjpq,rtjq->rtp/dot_general | solution.py:94
  47.6 0.7 copy-done.4
  48.8 11.2 %all-gather.5.cloned.1.call-done = bf16[32,256,64]{2,0,1:T(8,128)(2,1)} async-done(((bf16[32,8,64]{2,0,1:T(8,128)(2,1)}), bf16[32,256,64]{2,0,1:T(8,128)(2,1)}) %all-gather.5.cloned.1.call-update) | async-done | bytes 1048592 | tf_op jit(solution)/shard_map/all_gather | solution.py:74
  59.9 2.2 %gather_fusion.1 = bf16[64,32,64]{2,1,0:T(8,128)(2,1)S(1)} fusion(bf16[32,256,64]{2,0,1:T(8,128)(2,1)} %all-gather.5.cloned.1.call-done, s32[1024]{0:T(1024)S(1)} %pad_clamp_fusion.1), kind=kCustom, calls=%fused_computation.1 | custom fusion | bytes 524544 | tf_op jit(solution)/shard_map/jit(_take)/gather | solution.py:28
  62.2 1.8 %fusion.25 = bf16[32,8,64]{2,0,1:T(8,128)(2,1)S(1)} fusion(bf16[8,8,64,64]{3,2,1,0:T(8,128)(2,1)} %param.16, bf16[8,8,32,64]{3,2,1,0:T(8,128)(2,1)S(1)} %bitcast.74, pred[8,8]{1,0:T(8,128)(4,1)S(1)} %get-tuple-element.8, pred[8,8]{1,0:T(8,128)(4,1)S(1)} %get-tuple-element.7), kind=kOutput, calls=%fused_computation.29 | convolution fusion | flops 17055744 | bytes 819328 | tf_op jit(solution)/shard_map/qjab,rqjb->rqa/dot_general | solution.py:79
  63.9 51.0 %all-gather.3.cloned.1.call-done = bf16[32,1024,64]{2,0,1:T(8,128)(2,1)} async-done(((bf16[32,32,64]{2,0,1:T(8,128)(2,1)}), bf16[32,1024,64]{2,0,1:T(8,128)(2,1)}) %all-gather.3.cloned.1.call-update) | async-done | bytes 4194320 | tf_op jit(solution)/shard_map/all_gather | solution.py:62
  114.9 5.6 %gather_fusion = bf16[256,32,64]{2,1,0:T(8,128)(2,1)} fusion(bf16[32,1024,64]{2,0,1:T(8,128)(2,1)} %all-gather.3.cloned.1.call-done, s32[1024]{0:T(1024)S(1)} %pad_clamp_fusion.2), kind=kCustom, calls=%fused_computation | custom fusion | bytes 2098176 | tf_op jit(solution)/shard_map/jit(_take)/gather | solution.py:28
  120.5 5.1 %fusion.15 = f32[32,32,64]{2,1,0:T(8,128)} fusion(bf16[32,8,64,64]{3,2,1,0:T(8,128)(2,1)} %param.14, bf16[32,8,32,64]{3,2,1,0:T(8,128)(2,1)} %bitcast.72, pred[32,8]{1,0:T(8,128)(4,1)S(1)} %copy.28, pred[32,8]{1,0:T(8,128)(4,1)S(1)} %copy.29), kind=kOutput, calls=%fused_computation.17 | convolution fusion | flops 68157440 | bytes 3408384 | tf_op jit(solution)/shard_map/tjab,rtjb->rta/dot_general | solution.py:67
  125.6 2.4 %fusion.22 = bf16[32,4,8,128]{3,2,1,0:T(8,128)(2,1)} fusion(f32[32,32,128]{2,0,1:T(8,128)} %reduce-scatter.2.cloned.1.call-done, bf16[32,128,64]{1,2,0:T(8,128)(2,1)S(1)} %copy-done.3, f32[32,32,64]{2,1,0:T(8,128)} %fusion.15, bf16[32,32,64]{2,0,1:T(8,128)(2,1)S(1)} %bitcast.73, bf16[32,64,64]{2,1,0:T(8,128)(2,1)S(1)} %copy-done.2), kind=kOutput, calls=%fused_computation.25 | convolution fusion | flops 25559040 | bytes 1966080 | tf_op jit(solution)/shard_map/lpk,rlk->rlp/dot_general | solution.py:87
  128.1 1.7 %copy.44 = bf16[32,4,8,128]{3,2,0,1:T(8,128)(2,1)} copy(bf16[32,4,8,128]{3,2,1,0:T(8,128)(2,1)} %fusion.22) | data formatting | bytes 524288 | tf_op jit(solution)/shard_map/convert_element_type | solution.py:98
  (37 shorter events, 0.8 us)
Async XLA Ops:
  7.4 36.5 %copy-start = (bf16[32,2,128,128]{3,2,1,0:T(8,128)(2,1)S(1)}, bf16[32,2,128,128]{3,2,1,0:T(8,128)(2,1)}, u32[]{:S(2)}) copy-start(bf16[32,2,128,128]{3,2,1,0:T(8,128)(2,1)} %param.19) | copy-start | bytes 6291460
  7.4 52.5 %all-gather.5.cloned.1.call-start = ((), (), s32[]{:S(2)}) async-start(), calls=%async_computation.2 | async-start | bytes 2162688 | tf_op jit(solution)/shard_map/all_gather | solution.py:74
  7.4 12.3 %copy-start.6 = (s32[32,2]{0,1:T(2,128)S(1)}, s32[32,2]{0,1:T(2,128)}, u32[]{:S(2)}) copy-start(s32[32,2]{0,1:T(2,128)} %param.17) | copy-start | bytes 772
  7.4 12.3 %copy-start.7 = (s32[32]{0:T(128)S(1)}, s32[32]{0:T(128)}, u32[]{:S(2)}) copy-start(s32[32]{0:T(128)} %param.18) | copy-start | bytes 388
  11.2 2.1 %copy-start.1 = (bf16[32,32,64]{2,0,1:T(8,128)(2,1)}, bf16[32,32,64]{2,0,1:T(8,128)(2,1)S(1)}, u32[]{:S(2)}) copy-start(bf16[32,32,64]{2,0,1:T(8,128)(2,1)S(1)} %fusion.21) | copy-start | bytes 393220
  13.2 101.7 %all-gather.3.cloned.1.call-start = ((), (), s32[]{:S(2)}) async-start(), calls=%async_computation.1 | async-start | bytes 8650752 | tf_op jit(solution)/shard_map/all_gather | solution.py:62
  14.0 111.6 %reduce-scatter.2.cloned.1.call-start = ((), (), s32[]{:S(2)}) async-start(), calls=%async_computation.3 | async-start | bytes 2621440 | tf_op jit(solution)/shard_map/reduce_scatter | solution.py:97
  14.0 16.7 %collective-permute-start = (bf16[128,32,128]{0,2,1:T(8,128)(2,1)S(1)}, bf16[128,32,128]{0,2,1:T(8,128)(2,1)}, u32[]{:S(2)}, u32[]{:S(2)}) collective-permute-start(bf16[128,32,128]{0,2,1:T(8,128)(2,1)S(1)} %bitcast.68), channel_id=1, source_target_pairs={{0,4},{4,8},{8,12},{12,16},{16,20},{20,24},{24,28},{28,32},{32,36}... | collective-permute-start | bytes 3145736 | tf_op jit(solution)/shard_map/ppermute | solution.py:15
  16.0 16.7 %collective-permute-start.1 = (bf16[128,32,128]{0,2,1:T(8,128)(2,1)S(1)}, bf16[128,32,128]{0,2,1:T(8,128)(2,1)}, u32[]{:S(2)}, u32[]{:S(2)}) collective-permute-start(bf16[128,32,128]{0,2,1:T(8,128)(2,1)S(1)} %bitcast.69), channel_id=1, source_target_pairs={{4,0},{8,4},{12,8},{16,12},{20,16},{24,20},{28,24},{32,28},{36,32}... | collective-permute-start | bytes 3145736 | tf_op jit(solution)/shard_map/ppermute | solution.py:17
  47.6 0.7 copy-start.4
  47.6 1.1 copy-start.5
  120.5 5.1 %copy-start.2 = (bf16[32,64,64]{2,1,0:T(8,128)(2,1)S(1)}, bf16[32,64,64]{2,1,0:T(8,128)(2,1)}, u32[]{:S(2)}) copy-start(bf16[32,64,64]{2,1,0:T(8,128)(2,1)} %param.12) | copy-start | bytes 786436
  120.5 5.1 %copy-start.3 = (bf16[32,128,64]{1,2,0:T(8,128)(2,1)S(1)}, bf16[32,128,64]{1,2,0:T(8,128)(2,1)}, u32[]{:S(2)}) copy-start(bf16[32,128,64]{1,2,0:T(8,128)(2,1)} %param.11) | copy-start | bytes 1572868
Sparse Core Ops, SparseCore 0:
  13.4 46.5 all-gather.4
  62.4 52.4 all-gather.2
Sparse Core Ops, SparseCore 1:
  47.7 35.6 reduce-scatter.1
where the time goes:
time: 139 us; the launch traced here: 137 us
  waiting for transfers between devices  75.4 us (54%)
  local copies, waits for them, and re-layouts  20.9 us (15%)
  matrix products  17 us (12%)
  between operations  15 us (11%)
  starting transfers between devices  5.65 us (4%)
  other arithmetic  3.22 us (2%)
    all_gather x1, waiting for transfers between devices, per_device(): lax.all_gather(leaf_coef, 'clus', axis=1, tiled=True)  51 us
    gather x4, local copies, waits for them, and re-layouts, collect_rows(): chosen = jnp.take(fragment, jnp.clip(offset, 0, amount - 1), axis=1)  15.9 us
    all_gather x1, waiting for transfers between devices, per_device(): lax.all_gather(par_coef, 'clus', axis=1, tiled=True)  11.2 us
    ppermute x1, waiting for transfers between devices, extended(): lax.ppermute(tail, axis, [(i, (i + 1) % count) for i in range(ends)])  10.6 us
    dot_general x1, matrix products, per_device(): jnp.einsum('tjab,rtjb->rta', leaf_coupling, leaf_source, preferred_elemen...  5.06 us
    dot_general x1, matrix products, per_device(): jnp.einsum('tjpq,rtjq->rtp', near_block, near_source, preferred_element_t...  3.72 us
    ppermute x1, starting transfers between devices, extended(): lax.ppermute(head, axis, [((i + 1) % count, i) for i in range(ends)])  3.64 us
    concatenate x1, other arithmetic, extended(): jnp.concatenate([lax.ppermute(tail, axis, [(i, (i + 1) % count) for i in...  3.1 us
  transfers between devices with their start and end apart: 5, of which 4 were waited for; matrix products, arithmetic and copies ran while one was open for 22% of the time, Pallas kernels for 0%

commit v1 on v0

v1 whole, which is shorter than its diff:
```python
import jax
import jax.numpy as jnp
from jax import lax
from jax.experimental import pallas as pl
from jax.experimental.pallas import tpu as pltpu
from jax.sharding import PartitionSpec as P

BF16 = jnp.bfloat16
F32 = jnp.float32
LEAVES = 32
PARENTS = 8
ROWS = 640
SIDE = 4
STEP_PARENTS = 2
NT = (((1,), (1,)), ((), ()))


def dot_nt(a, b):
    return lax.dot_general(a, b, NT, preferred_element_type=F32)


def side_by_side(a, b):
    return jnp.concatenate([a, b], axis=1)


def diagonal(a, b):
    zeros = jnp.zeros_like(a)
    return jnp.concatenate([side_by_side(a, zeros), side_by_side(zeros, b)], axis=0)


def coef_kernel(meta, sources, basis, transfer, out):
    pairs = []
    for m in range(LEAVES // 2):
        weights = diagonal(basis[2 * m], basis[2 * m + 1])
        pair = dot_nt(sources[:, 256 * m : 256 * (m + 1)], weights).astype(BF16)
        out[32 * m : 32 * (m + 1), :] = pair
        pairs.append(pair)
    for n in range(PARENTS // 2):
        halves = []
        for q in (2 * n, 2 * n + 1):
            children = side_by_side(pairs[2 * q], pairs[2 * q + 1])
            weights = transfer[4 * q : 4 * q + 4].reshape(256, 64)
            halves.append(jnp.dot(children, weights, preferred_element_type=F32))
        out[512 + 32 * n : 512 + 32 * (n + 1), :] = side_by_side(*halves).astype(BF16)


def coefficients(meta, sources, basis, transfer):
    return pl.pallas_call(
        coef_kernel,
        out_shape=jax.ShapeDtypeStruct((ROWS, 128), BF16),
        grid_spec=pltpu.PrefetchScalarGridSpec(
            num_scalar_prefetch=1,
            grid=(1,),
            in_specs=[
                pl.BlockSpec((32, 4096), lambda i, meta: (meta[0], 0)),
                pl.BlockSpec((LEAVES, 64, 128), lambda i, meta: (0, 0, 0)),
                pl.BlockSpec((LEAVES, 64, 64), lambda i, meta: (0, 0, 0)),
            ],
            out_specs=pl.BlockSpec((ROWS, 128), lambda i, meta: (0, 0)),
        ),
        compiler_params=pltpu.CompilerParams(vmem_limit_bytes=32 << 20),
    )(meta, sources, basis, transfer)


def near_kernel(meta, near_list, near_count, own, before, after, near_block, *rest):
    outs, window, sems = rest[:4], rest[4], rest[5]
    copies = [
        pltpu.make_async_copy(part, window.at[:, pl.ds(4096 * k, 4096)], sems.at[k])
        for k, part in enumerate((before, own, after))
    ]
    for copy in copies:
        copy.start()
    for copy in copies:
        copy.wait()
    z = meta[0]
    first = (meta[1] - 1) * LEAVES

    def body(t, carry):
        parts = []
        for i in range(2):
            place = jnp.clip(near_list[i, t] - first, 0, 3 * LEAVES - 1)
            columns = pl.ds(pl.multiple_of(place * 128, 128), 128)
            active = z * 2 + i < near_count[t]
            rows = [
                window[pl.ds(pl.multiple_of(((z + d) % 4) * 32, 32), 32), columns]
                for d in range(4)
            ]
            block = jnp.concatenate(rows, axis=0)
            parts.append(lax.select(active, block, jnp.zeros_like(block)))
        weights = side_by_side(near_block[t, 0], near_block[t, 1])
        result = dot_nt(side_by_side(*parts), weights).astype(BF16)
        here = pl.ds(pl.multiple_of(t * 128, 128), 128)
        for d in range(4):
            outs[d][:, here] = result[32 * d : 32 * (d + 1)]
        return carry

    lax.fori_loop(0, LEAVES, body, 0, unroll=4)


def near_partials(meta, near_list, near_count, own, before, after, near_block):
    smem = pl.BlockSpec(memory_space=pltpu.SMEM)
    anywhere = pl.BlockSpec(memory_space=pl.ANY)
    return pl.pallas_call(
        near_kernel,
        out_shape=[jax.ShapeDtypeStruct((32, 4096), BF16)] * 4,
        in_specs=[smem] * 3 + [anywhere] * 3 + [pl.BlockSpec(memory_space=pltpu.VMEM)],
        out_specs=[pl.BlockSpec(memory_space=pltpu.VMEM)] * 4,
        scratch_shapes=[
            pltpu.VMEM((128, 3 * 4096), BF16),
            pltpu.SemaphoreType.DMA((3,)),
        ],
        compiler_params=pltpu.CompilerParams(vmem_limit_bytes=32 << 20),
    )(meta, near_list, near_count, own, before, after, near_block)


def chunk_places(y, x, alongx):
    def chip(first, second):
        dy, dx = (second, first) if alongx else (first, second)
        return ((y + dy + SIDE) % SIDE) * SIDE + (x + dx + SIDE) % SIDE

    order = (0, -1, 1, 2)
    own = [chip(s, 0) for s in order]
    sides = [chip(s, d) for d in (-1, 1) for s in order]
    far = [chip(s, 2) for s in order]
    return own, sides, far


def far_kernel(meta, far_leaf, far_par, *rest):
    (own, sides_b, sides_a, far_b, far_a, own2, sides2, far2) = rest[:8]
    coupling, par_coupling, transfer, basis, near0, near1, near2, near3, out, held, sems = rest[8:]
    step = pl.program_id(0)

    def copies(y, x, core):
        mine = chunk_places(y, x, core == 0)
        other = chunk_places(y, x, core == 1)
        pieces = []
        for k in range(4):
            pieces.append((own, k, mine[0][k], core))
            pieces.append((sides_b, k, mine[1][k], core))
            pieces.append((sides_a, k, mine[1][4 + k], core))
            pieces.append((far_b if k < 2 else far_a, k % 2, mine[2][k], core))
            pieces.append((own2, k, other[0][k], 1 - core))
            pieces.append((sides2, k, other[1][k], 1 - core))
            pieces.append((sides2, 4 + k, other[1][4 + k], 1 - core))
            pieces.append((far2, k, other[2][k], 1 - core))
        return [
            pltpu.make_async_copy(
                ref.at[pl.ds(ROWS * k, ROWS)], held.at[chip * 2 + c], sems.at[n]
            )
            for n, (ref, k, chip, c) in enumerate(pieces)
        ]

    @pl.when(step == 0)
    def _():
        y, x, core = meta[2], meta[3], meta[4]
        for which in range(2):

            @pl.when(core == which)
            def _():
                started = copies(y, x, which)
                for copy in started:
                    copy.start()
                for copy in started:
                    copy.wait()

    lane = lax.broadcasted_iota(jnp.int32, (1, 128), 1)
    low = (lane < 64).astype(F32).astype(BF16)
    high = (lane >= 64).astype(F32).astype(BF16)

    def leaf_pair(index):
        rows = pl.ds(pl.multiple_of((index % 32) // 2 * 32, 32), 32)
        return held[index // 32, rows, :] * lax.select(index % 2 == 0, low, high)

    def par_pair(index):
        rows = pl.ds(pl.multiple_of(512 + (index % 8) // 2 * 32, 32), 32)
        return held[index // 8, rows, :] * lax.select(index % 2 == 0, low, high)

    def couple(pick, indices, blocks):
        total = None
        for i in range(0, 8, 2):
            terms = side_by_side(pick(indices[i]), pick(indices[i + 1]))
            weights = jnp.concatenate(
                [blocks(i), blocks(i), blocks(i + 1), blocks(i + 1)], axis=1
            )
            term = dot_nt(terms, weights)
            total = term if total is None else total + term
        return total

    for p in range(STEP_PARENTS):
        q = step * STEP_PARENTS + p
        field = couple(
            par_pair, [far_par[q, i] for i in range(8)], lambda i: par_coupling[p, i]
        ).astype(BF16)
        spread = dot_nt(field, transfer[4 * p : 4 * p + 4].reshape(256, 64))
        for m in range(2):
            downs = []
            for c in (2 * m, 2 * m + 1):
                leaf = 4 * p + c
                local = couple(
                    leaf_pair,
                    [far_leaf[i, 4 * q + c] for i in range(8)],
                    lambda i: coupling[leaf, i],
                )
                downs.append(local + spread[:, 64 * c : 64 * (c + 1)])
            down = side_by_side(*downs).astype(BF16)
            leaf = 4 * p + 2 * m
            result = jnp.dot(
                down, diagonal(basis[leaf], basis[leaf + 1]), preferred_element_type=F32
            )
            here = slice(128 * leaf, 128 * (leaf + 2))
            near = near0[:, here].astype(F32) + near1[:, here].astype(F32)
            near += near2[:, here].astype(F32) + near3[:, here].astype(F32)
            out[:, here] = (result + near).astype(BF16)


def far_and_sum(meta, far_leaf, far_par, gathered, coupling, par_coupling, transfer, basis, nears):
    smem = pl.BlockSpec(memory_space=pltpu.SMEM)
    anywhere = pl.BlockSpec(memory_space=pl.ANY)
    leaves = 4 * STEP_PARENTS
    part = pl.BlockSpec((32, 128 * leaves), lambda i: (0, i))
    return pl.pallas_call(
        far_kernel,
        out_shape=jax.ShapeDtypeStruct((32, 4096), BF16),
        grid=(PARENTS // STEP_PARENTS,),
        in_specs=[smem] * 3
        + [anywhere] * 8
        + [
            pl.BlockSpec((leaves, 8, 64, 64), lambda i: (i, 0, 0, 0)),
            pl.BlockSpec((STEP_PARENTS, 8, 64, 64), lambda i: (i, 0, 0, 0)),
            pl.BlockSpec((leaves, 64, 64), lambda i: (i, 0, 0)),
            pl.BlockSpec((leaves, 64, 128), lambda i: (i, 0, 0)),
        ]
        + [part] * 4,
        out_specs=part,
        scratch_shapes=[
            pltpu.VMEM((32, ROWS, 128), BF16),
            pltpu.SemaphoreType.DMA((32,)),
        ],
        compiler_params=pltpu.CompilerParams(vmem_limit_bytes=40 << 20),
    )(meta, far_leaf, far_par, *gathered, coupling, par_coupling, transfer, basis, *nears)


def place(y, x, core):
    return (y % SIDE) * 8 + (x % SIDE) * 2 + core


def around(distance, first):
    pairs = []
    for y in range(SIDE):
        for x in range(SIDE):
            for core in range(2):
                alongx = (core == 0) == first
                to = place(y, x + distance, core) if alongx else place(y + distance, x, core)
                pairs.append((place(y, x, core), to))
    return pairs


SWAP = [(i, i ^ 1) for i in range(32)]


def gather(chunk):
    def send(value, pairs):
        return lax.ppermute(value, "clus", pairs)

    across = send(chunk, around(2, True))
    before = send(chunk, around(1, True))
    after = send(chunk, around(-1, True))
    own = jnp.concatenate([chunk, before, after, across], axis=0)
    half = own.shape[0] // 2
    side_b = send(own, around(1, False))
    side_a = send(own, around(-1, False))
    own2 = send(own, SWAP)
    far_b = send(side_b[:half], around(1, False))
    far_a = send(side_a[half:], around(-1, False))
    sides2 = send(jnp.concatenate([side_b, side_a], axis=0), SWAP)
    far2 = send(jnp.concatenate([far_b, far_a], axis=0), SWAP)
    return own, side_b, side_a, far_b, far_a, own2, sides2, far2


def per_device(
    sources,
    leaf_basis,
    transfer,
    far_leaf,
    leaf_coupling,
    far_par,
    par_coupling,
    near_list,
    near_count,
    near_block,
):
    clus, rhs = lax.axis_index("clus"), lax.axis_index("rhs")
    meta = jnp.stack([rhs, clus, clus // 8, (clus // 2) % 4, clus % 2]).astype(jnp.int32)
    basis = jnp.swapaxes(leaf_basis, 1, 2)
    before = lax.ppermute(sources, "clus", [(i, (i + 1) % 32) for i in range(32)])
    after = lax.ppermute(sources, "clus", [((i + 1) % 32, i) for i in range(32)])
    chunk = coefficients(meta, sources, basis, transfer)
    gathered = gather(chunk)
    partials = near_partials(
        meta, near_list.T, near_count, sources, before, after, near_block
    )
    nears = [partials[0]]
    for d in (1, 2, 3):
        nears.append(lax.ppermute(partials[d], "rhs", [(j, (j + d) % 4) for j in range(4)]))
    return far_and_sum(
        meta, far_leaf.T, far_par, gathered, leaf_coupling, par_coupling, transfer, basis, nears
    )


def solution(mesh):
    in_specs = (
        P(None, "clus"),
        P("clus", None, None),
        P("clus", None, None),
        P("clus", None),
        P("clus", None, None, None),
        P("clus", None),
        P("clus", None, None, None),
        P("clus", "rhs"),
        P("clus"),
        P("clus", "rhs", None, None),
    )
    return jax.shard_map(
        per_device, mesh=mesh, in_specs=in_specs, out_specs=P("rhs", "clus"), check_vma=False
    )
```

time: 139 us -> 89.2 us (0.64)
  the two profiles are of different devices: /device:TPU:6 before, /device:TPU:1 now
where the time goes in v1:
time: 89.2 us; the launch traced here: 89 us
  starting transfers between devices  40.6 us (46%)
  waiting for transfers between devices  23.1 us (26%)
  Pallas kernels  21.5 us (24%)
  local copies, waits for them, and re-layouts  3.49 us (4%)
    ppermute x10, starting transfers between devices, send(): return lax.ppermute(value, 'clus', pairs)  32 us
    pallas_call x1, Pallas kernels, far_and_sum(): pl.pallas_call(far_kernel, out_shape=jax.ShapeDtypeStruct((32, 4096), BF1...  17.5 us
    ppermute x10, waiting for transfers between devices, send(): return lax.ppermute(value, 'clus', pairs)  11.8 us
    ppermute x3, waiting for transfers between devices, per_device(): lax.ppermute(partials[d], 'rhs', [(j, (j + d) % 4) for j in range(4)])  11.3 us
    ppermute x3, starting transfers between devices, per_device(): lax.ppermute(partials[d], 'rhs', [(j, (j + d) % 4) for j in range(4)])  5.74 us
    unnamed x24, local copies, waits for them, and re-layouts  3.36 us
    pallas_call x1, Pallas kernels, near_partials(): pl.pallas_call(near_kernel, out_shape=[jax.ShapeDtypeStruct((32, 4096), B...  2.73 us
    ppermute x1, starting transfers between devices, per_device(): lax.ppermute(sources, 'clus', [(i, (i + 1) % 32) for i in range(32)])  2.12 us
  transfers between devices with their start and end apart: 15, of which 6 were waited for; matrix products, arithmetic and copies ran while one was open for 0% of the time, Pallas kernels for 3%

profile of v1, /device:TPU:1, one launch (start us, length us, event | category | flops | bytes accessed | tf_op | source)
XLA Modules:
  0.0 89.0 jit_solution(6782782814101001061)
XLA Ops:
  0.1 1.2 %copy-done = bf16[128,4096]{1,0:T(8,128)(2,1)S(1)} copy-done((bf16[128,4096]{1,0:T(8,128)(2,1)S(1)}, bf16[128,4096]{1,0:T(8,128)(2,1)}, u32[]{:S(2)}) %copy-start) | copy-done | bytes 1048600
  1.3 1.0 %copy-done.3 = bf16[32,128,64]{1,2,0:T(8,128)(2,1)S(1)} copy-done((bf16[32,128,64]{1,2,0:T(8,128)(2,1)S(1)}, bf16[32,128,64]{1,2,0:T(8,128)(2,1)}, u32[]{:S(2)}) %copy-start.3) | copy-done | bytes 524312
  2.4 1.0 %copy-done.5 = bf16[32,64,64]{2,1,0:T(8,128)(2,1)S(1)} copy-done((bf16[32,64,64]{2,1,0:T(8,128)(2,1)S(1)}, bf16[32,64,64]{2,1,0:T(8,128)(2,1)}, u32[]{:S(2)}) %copy-start.5) | copy-done | bytes 262168
  3.4 1.2 %shard_map.100 = bf16[640,128]{1,0:T(8,128)(2,1)S(1)} custom-call(s32[5]{0:T(128)S(1)} %stack.23.meta, bf16[128,4096]{1,0:T(8,128)(2,1)S(1)} %copy-done, bf16[32,64,128]{2,1,0:T(8,128)(2,1)S(1)} %bitcast.8, bf16[32,64,64]{2,1,0:T(8,128)(2,1)S(1)} %copy-done.5), custom_call_target="tpu_custom_call" | custom-call | tf_op jit(solution)/shard_map/pallas_call | solution.py:48
  4.6 3.8 %collective-permute-start.2 = (bf16[640,128]{1,0:T(8,128)(2,1)S(1)}, bf16[640,128]{1,0:T(8,128)(2,1)S(1)}, u32[]{:S(2)}, u32[]{:S(2)}) collective-permute-start(bf16[640,128]{1,0:T(8,128)(2,1)S(1)} %shard_map.100), channel_id=1, source_target_pairs={{0,16},{4,68},{8,24},{12,76},{16,0},{20,84},{24,8},{28,92},{32,48}... | collective-permute-start | bytes 491528 | tf_op jit(solution)/shard_map/ppermute | solution.py:263
  8.4 0.8 collective-permute-start.1
  9.1 0.7 collective-permute-start
  9.8 1.5 %collective-permute-done.2 = bf16[640,128]{1,0:T(8,128)(2,1)S(1)} collective-permute-done((bf16[640,128]{1,0:T(8,128)(2,1)S(1)}, bf16[640,128]{1,0:T(8,128)(2,1)S(1)}, u32[]{:S(2)}, u32[]{:S(2)}) %collective-permute-start.2) | collective-permute-done | bytes 163872 | tf_op jit(solution)/shard_map/ppermute | solution.py:263
  11.4 2.1 %collective-permute-done.1 = bf16[640,128]{1,0:T(8,128)(2,1)S(1)} collective-permute-done((bf16[640,128]{1,0:T(8,128)(2,1)S(1)}, bf16[640,128]{1,0:T(8,128)(2,1)S(1)}, u32[]{:S(2)}, u32[]{:S(2)}) %collective-permute-start.1) | collective-permute-done | bytes 163872 | tf_op jit(solution)/shard_map/ppermute | solution.py:263
  13.5 1.3 %collective-permute-done = bf16[640,128]{1,0:T(8,128)(2,1)S(1)} collective-permute-done((bf16[640,128]{1,0:T(8,128)(2,1)S(1)}, bf16[640,128]{1,0:T(8,128)(2,1)S(1)}, u32[]{:S(2)}, u32[]{:S(2)}) %collective-permute-start) | collective-permute-done | bytes 163872 | tf_op jit(solution)/shard_map/ppermute | solution.py:263
  14.9 2.3 %collective-permute-start.4 = (bf16[2560,128]{1,0:T(8,128)(2,1)S(1)}, bf16[2560,128]{1,0:T(8,128)(2,1)S(1)}, u32[]{:S(2)}, u32[]{:S(2)}) collective-permute-start(bf16[2560,128]{1,0:T(8,128)(2,1)S(1)} %pad_maximum_fusion.1.rest_0_), channel_id=1, source_target_pairs={{0,96},{4,28},{8,104},{12,4},{16,112},{20,12},{24,120},{28,20},{32... | collective-permute-start | bytes 1966088 | tf_op jit(solution)/shard_map/ppermute | solution.py:263
  17.1 2.1 %collective-permute-start.10 = (bf16[128,4096]{1,0:T(8,128)(2,1)S(1)}, bf16[128,4096]{1,0:T(8,128)(2,1)S(1)}, u32[]{:S(2)}, u32[]{:S(2)}) collective-permute-start(bf16[128,4096]{1,0:T(8,128)(2,1)S(1)} %copy-done), channel_id=1, source_target_pairs={{0,4},{4,8},{8,12},{12,16},{16,20},{20,24},{24,28},{28,32},{32,36}... | collective-permute-start | bytes 3145736 | tf_op jit(solution)/shard_map/ppermute | solution.py:295
  19.2 0.7 collective-permute-start.11
  20.0 6.8 %collective-permute-done.4.rest_2_ = bf16[2560,128]{1,0:T(8,128)(2,1)S(1)} collective-permute-done((bf16[2560,128]{1,0:T(8,128)(2,1)S(1)}, bf16[2560,128]{1,0:T(8,128)(2,1)S(1)}, u32[]{:S(2)}, u32[]{:S(2)}) %collective-permute-start.4) | collective-permute-done | bytes 655392 | tf_op jit(solution)/shard_map/ppermute | solution.py:263
  26.8 1.4 %collective-permute-start.6 = (bf16[1280,128]{1,0:T(8,128)(2,1)S(1)}, bf16[1280,128]{1,0:T(8,128)(2,1)S(1)}, u32[]{:S(2)}, u32[]{:S(2)}) collective-permute-start(bf16[1280,128]{1,0:T(8,128)(2,1)S(1)} %slice.9), channel_id=1, source_target_pairs={{0,96},{4,28},{8,104},{12,4},{16,112},{20,12},{24,120},{28,20},{32... | collective-permute-start | bytes 983048 | tf_op jit(solution)/shard_map/ppermute | solution.py:263
  28.5 14.8 %collective-permute-start.8 = (bf16[5120,128]{1,0:T(8,128)(2,1)S(1)}, bf16[5120,128]{1,0:T(8,128)(2,1)S(1)}, u32[]{:S(2)}, u32[]{:S(2)}) collective-permute-start(bf16[5120,128]{1,0:T(8,128)(2,1)S(1)} %pad_maximum_fusion), channel_id=1, source_target_pairs={{0,4},{4,0},{8,12},{12,8},{16,20},{20,16},{24,28},{28,24},{32,36},... | collective-permute-start | bytes 3932168 | tf_op jit(solution)/shard_map/ppermute | solution.py:263
  43.5 8.0 %collective-permute-start.9 = (bf16[2560,128]{1,0:T(8,128)(2,1)S(1)}, bf16[2560,128]{1,0:T(8,128)(2,1)S(1)}, u32[]{:S(2)}, u32[]{:S(2)}) collective-permute-start(bf16[2560,128]{1,0:T(8,128)(2,1)S(1)} %pad_maximum_fusion.2), channel_id=1, source_target_pairs={{0,4},{4,0},{8,12},{12,8},{16,20},{20,16},{24,28},{28,24},{32,36},... | collective-permute-start | bytes 1966088 | tf_op jit(solution)/shard_map/ppermute | solution.py:263
  51.6 2.7 %shard_map.101 = (bf16[32,4096]{1,0:T(8,128)(2,1)S(1)}, bf16[32,4096]{1,0:T(8,128)(2,1)S(1)}, bf16[32,4096]{1,0:T(8,128)(2,1)S(1)}, bf16[32,4096]{1,0:T(8,128)(2,1)S(1)}) custom-call(s32[5]{0:T(128)S(1)} %stack.23.meta, s32[2,32]{1,0:T(2,128)S(1)} %bitcast.11, s32[32]{0:T(128)S(1)} %copy-done.11, bf16[128,4096]{1,0:T(8,128)(2,1)S(1)} %copy-done, ...), custom_call_target="tpu_custom_call" | custom-call | tf_op jit(solution)/shard_map/pallas_call | solution.py:103
  54.3 1.7 %collective-permute-start.12 = (bf16[32,4096]{1,0:T(8,128)(2,1)S(1)}, bf16[32,4096]{1,0:T(8,128)(2,1)S(1)}, u32[]{:S(2)}, u32[]{:S(2)}) collective-permute-start(bf16[32,4096]{1,0:T(8,128)(2,1)S(1)} %get-tuple-element.10), channel_id=1, source_target_pairs={{0,1},{1,2},{2,3},{3,0},{4,5},{5,6},{6,7},{7,4},{8,9},{9,10},{10,1... | collective-permute-start | bytes 786440 | tf_op jit(solution)/shard_map/ppermute | solution.py:304
  56.0 3.3 %collective-permute-start.13 = (bf16[32,4096]{1,0:T(8,128)(2,1)S(1)}, bf16[32,4096]{1,0:T(8,128)(2,1)S(1)}, u32[]{:S(2)}, u32[]{:S(2)}) collective-permute-start(bf16[32,4096]{1,0:T(8,128)(2,1)S(1)} %get-tuple-element.11), channel_id=1, source_target_pairs={{0,2},{1,3},{2,0},{3,1},{4,6},{5,7},{6,4},{7,5},{8,10},{9,11},{10,... | collective-permute-start | bytes 786440 | tf_op jit(solution)/shard_map/ppermute | solution.py:304
  59.3 0.7 collective-permute-start.14
  60.1 4.7 %collective-permute-done.12.rest_13_ = bf16[32,4096]{1,0:T(8,128)(2,1)S(1)} collective-permute-done((bf16[32,4096]{1,0:T(8,128)(2,1)S(1)}, bf16[32,4096]{1,0:T(8,128)(2,1)S(1)}, u32[]{:S(2)}, u32[]{:S(2)}) %collective-permute-start.12) | collective-permute-done | bytes 262176 | tf_op jit(solution)/shard_map/ppermute | solution.py:304
  64.8 6.6 %collective-permute-done.13.rest_14_ = bf16[32,4096]{1,0:T(8,128)(2,1)S(1)} collective-permute-done((bf16[32,4096]{1,0:T(8,128)(2,1)S(1)}, bf16[32,4096]{1,0:T(8,128)(2,1)S(1)}, u32[]{:S(2)}, u32[]{:S(2)}) %collective-permute-start.13) | collective-permute-done | bytes 262176 | tf_op jit(solution)/shard_map/ppermute | solution.py:304
  71.5 17.5 %shard_map.102 = bf16[32,4096]{1,0:T(8,128)(2,1)} custom-call(s32[5]{0:T(128)S(1)} %stack.23.meta, s32[8,32]{1,0:T(8,128)S(1)} %bitcast.10, s32[8,8]{1,0:T(8,128)S(1)} %copy-done.9, bf16[2560,128]{1,0:T(8,128)(2,1)S(1)} %pad_maximum_fusion.1.rest_0_, bf16[2560,128]{1,0:T(8,128)(2,1)S(1)} %collective-permute-done.3.rest_1_, ...), custom_call_target="tpu_custom_call" | custom-call | tf_op jit(solution)/shard_map/pallas_call | solution.py:221
  (39 shorter events, 0.7 us)
Async XLA Ops:
  4.6 6.8 %collective-permute-start.2 = (bf16[640,128]{1,0:T(8,128)(2,1)S(1)}, bf16[640,128]{1,0:T(8,128)(2,1)S(1)}, u32[]{:S(2)}, u32[]{:S(2)}) collective-permute-start(bf16[640,128]{1,0:T(8,128)(2,1)S(1)} %shard_map.100), channel_id=1, source_target_pairs={{0,16},{4,68},{8,24},{12,76},{16,0},{20,84},{24,8},{28,92},{32,48}... | collective-permute-start | bytes 491528 | tf_op jit(solution)/shard_map/ppermute | solution.py:263
  8.4 5.2 %collective-permute-start.1 = (bf16[640,128]{1,0:T(8,128)(2,1)S(1)}, bf16[640,128]{1,0:T(8,128)(2,1)S(1)}, u32[]{:S(2)}, u32[]{:S(2)}) collective-permute-start(bf16[640,128]{1,0:T(8,128)(2,1)S(1)} %shard_map.100), channel_id=1, source_target_pairs={{0,24},{4,100},{8,0},{12,108},{16,8},{20,116},{24,16},{28,124},{32... | collective-permute-start | bytes 491528 | tf_op jit(solution)/shard_map/ppermute | solution.py:263
  9.1 5.7 %collective-permute-start = (bf16[640,128]{1,0:T(8,128)(2,1)S(1)}, bf16[640,128]{1,0:T(8,128)(2,1)S(1)}, u32[]{:S(2)}, u32[]{:S(2)}) collective-permute-start(bf16[640,128]{1,0:T(8,128)(2,1)S(1)} %shard_map.100), channel_id=1, source_target_pairs={{0,8},{4,36},{8,16},{12,44},{16,24},{20,52},{24,0},{28,60},{32,40}... | collective-permute-start | bytes 491528 | tf_op jit(solution)/shard_map/ppermute | solution.py:263
  14.9 11.9 %collective-permute-start.4 = (bf16[2560,128]{1,0:T(8,128)(2,1)S(1)}, bf16[2560,128]{1,0:T(8,128)(2,1)S(1)}, u32[]{:S(2)}, u32[]{:S(2)}) collective-permute-start(bf16[2560,128]{1,0:T(8,128)(2,1)S(1)} %pad_maximum_fusion.1.rest_0_), channel_id=1, source_target_pairs={{0,96},{4,28},{8,104},{12,4},{16,112},{20,12},{24,120},{28,20},{32... | collective-permute-start | bytes 1966088 | tf_op jit(solution)/shard_map/ppermute | solution.py:263
  17.1 11.0 %collective-permute-start.3 = (bf16[2560,128]{1,0:T(8,128)(2,1)S(1)}, bf16[2560,128]{1,0:T(8,128)(2,1)S(1)}, u32[]{:S(2)}, u32[]{:S(2)}) collective-permute-start(bf16[2560,128]{1,0:T(8,128)(2,1)S(1)} %pad_maximum_fusion.1.rest_0_), channel_id=1, source_target_pairs={{0,32},{4,12},{8,40},{12,20},{16,48},{20,28},{24,56},{28,4},{32,64... | collective-permute-start | bytes 1966088 | tf_op jit(solution)/shard_map/ppermute | solution.py:263
  17.1 34.4 %collective-permute-start.10 = (bf16[128,4096]{1,0:T(8,128)(2,1)S(1)}, bf16[128,4096]{1,0:T(8,128)(2,1)S(1)}, u32[]{:S(2)}, u32[]{:S(2)}) collective-permute-start(bf16[128,4096]{1,0:T(8,128)(2,1)S(1)} %copy-done), channel_id=1, source_target_pairs={{0,4},{4,8},{8,12},{12,16},{16,20},{20,24},{24,28},{28,32},{32,36}... | collective-permute-start | bytes 3145736 | tf_op jit(solution)/shard_map/ppermute | solution.py:295
  19.2 32.3 %collective-permute-start.11 = (bf16[128,4096]{1,0:T(8,128)(2,1)S(1)}, bf16[128,4096]{1,0:T(8,128)(2,1)S(1)}, u32[]{:S(2)}, u32[]{:S(2)}) collective-permute-start(bf16[128,4096]{1,0:T(8,128)(2,1)S(1)} %copy-done), channel_id=1, source_target_pairs={{4,0},{8,4},{12,8},{16,12},{20,16},{24,20},{28,24},{32,28},{36,32}... | collective-permute-start | bytes 3145736 | tf_op jit(solution)/shard_map/ppermute | solution.py:296
  26.8 16.5 %collective-permute-start.6 = (bf16[1280,128]{1,0:T(8,128)(2,1)S(1)}, bf16[1280,128]{1,0:T(8,128)(2,1)S(1)}, u32[]{:S(2)}, u32[]{:S(2)}) collective-permute-start(bf16[1280,128]{1,0:T(8,128)(2,1)S(1)} %slice.9), channel_id=1, source_target_pairs={{0,96},{4,28},{8,104},{12,4},{16,112},{20,12},{24,120},{28,20},{32... | collective-permute-start | bytes 983048 | tf_op jit(solution)/shard_map/ppermute | solution.py:263
  28.2 15.2 %collective-permute-start.5 = (bf16[1280,128]{1,0:T(8,128)(2,1)S(1)}, bf16[1280,128]{1,0:T(8,128)(2,1)S(1)}, u32[]{:S(2)}, u32[]{:S(2)}) collective-permute-start(bf16[1280,128]{1,0:T(8,128)(2,1)S(1)} %slice.8), channel_id=1, source_target_pairs={{0,32},{4,12},{8,40},{12,20},{16,48},{20,28},{24,56},{28,4},{32,64... | collective-permute-start | bytes 983048 | tf_op jit(solution)/shard_map/ppermute | solution.py:263
  28.4 23.1 %copy-start.2 = (bf16[32,2,128,128]{3,2,1,0:T(8,128)(2,1)S(1)}, bf16[32,2,128,128]{3,2,1,0:T(8,128)(2,1)}, u32[]{:S(2)}) copy-start(bf16[32,2,128,128]{3,2,1,0:T(8,128)(2,1)} %near_block.1) | copy-start | bytes 6291460
  28.5 23.0 %copy-start.10 = (s32[32,2]{0,1:T(2,128)S(1)}, s32[32,2]{0,1:T(2,128)}, u32[]{:S(2)}) copy-start(s32[32,2]{0,1:T(2,128)} %param.17) | copy-start | bytes 772
  28.5 23.0 %copy-start.11 = (s32[32]{0:T(128)S(1)}, s32[32]{0:T(128)}, u32[]{:S(2)}) copy-start(s32[32]{0:T(128)} %near_count.1) | copy-start | bytes 388
  28.5 42.9 %collective-permute-start.8 = (bf16[5120,128]{1,0:T(8,128)(2,1)S(1)}, bf16[5120,128]{1,0:T(8,128)(2,1)S(1)}, u32[]{:S(2)}, u32[]{:S(2)}) collective-permute-start(bf16[5120,128]{1,0:T(8,128)(2,1)S(1)} %pad_maximum_fusion), channel_id=1, source_target_pairs={{0,4},{4,0},{8,12},{12,8},{16,20},{20,16},{24,28},{28,24},{32,36},... | collective-permute-start | bytes 3932168 | tf_op jit(solution)/shard_map/ppermute | solution.py:263
  43.3 16.0 %collective-permute-start.7 = (bf16[2560,128]{1,0:T(8,128)(2,1)S(1)}, bf16[2560,128]{1,0:T(8,128)(2,1)S(1)}, u32[]{:S(2)}, u32[]{:S(2)}) collective-permute-start(bf16[2560,128]{1,0:T(8,128)(2,1)S(1)} %pad_maximum_fusion.1.rest_0_), channel_id=1, source_target_pairs={{0,4},{4,0},{8,12},{12,8},{16,20},{20,16},{24,28},{28,24},{32,36},... | collective-permute-start | bytes 1966088 | tf_op jit(solution)/shard_map/ppermute | solution.py:263
  43.4 28.0 %copy-start.7 = (bf16[8,8,64,64]{3,2,1,0:T(8,128)(2,1)S(1)}, bf16[8,8,64,64]{3,2,1,0:T(8,128)(2,1)}, u32[]{:S(2)}) copy-start(bf16[8,8,64,64]{3,2,1,0:T(8,128)(2,1)} %rest_9_.1) | copy-start | bytes 1572868
  43.5 27.9 %collective-permute-start.9 = (bf16[2560,128]{1,0:T(8,128)(2,1)S(1)}, bf16[2560,128]{1,0:T(8,128)(2,1)S(1)}, u32[]{:S(2)}, u32[]{:S(2)}) collective-permute-start(bf16[2560,128]{1,0:T(8,128)(2,1)S(1)} %pad_maximum_fusion.2), channel_id=1, source_target_pairs={{0,4},{4,0},{8,12},{12,8},{16,20},{20,16},{24,28},{28,24},{32,36},... | collective-permute-start | bytes 1966088 | tf_op jit(solution)/shard_map/ppermute | solution.py:263
  51.5 19.9 %copy-start.1 = (bf16[32,8,64,64]{3,2,1,0:T(8,128)(2,1)S(1)}, bf16[32,8,64,64]{3,2,1,0:T(8,128)(2,1)}, u32[]{:S(2)}) copy-start(bf16[32,8,64,64]{3,2,1,0:T(8,128)(2,1)} %rest_8_.1) | copy-start | bytes 6291460
  51.5 19.9 %copy-start.4 = (bf16[32,128,64]{1,2,0:T(8,128)(2,1)S(1)}, bf16[32,128,64]{1,2,0:T(8,128)(2,1)}, u32[]{:S(2)}) copy-start(bf16[32,128,64]{1,2,0:T(8,128)(2,1)} %param.11) | copy-start | bytes 1572868
  51.5 19.9 %copy-start.6 = (bf16[32,64,64]{2,1,0:T(8,128)(2,1)S(1)}, bf16[32,64,64]{2,1,0:T(8,128)(2,1)}, u32[]{:S(2)}) copy-start(bf16[32,64,64]{2,1,0:T(8,128)(2,1)} %rest_10_.1) | copy-start | bytes 786436
  51.6 19.9 %copy-start.8 = (s32[32,8]{0,1:T(8,128)S(1)}, s32[32,8]{0,1:T(8,128)}, u32[]{:S(2)}) copy-start(s32[32,8]{0,1:T(8,128)} %param.13) | copy-start | bytes 3076
  51.6 19.9 %copy-start.9 = (s32[8,8]{1,0:T(8,128)S(1)}, s32[8,8]{1,0:T(8,128)}, u32[]{:S(2)}) copy-start(s32[8,8]{1,0:T(8,128)} %far_par.1) | copy-start | bytes 772
  54.3 10.5 %collective-permute-start.12 = (bf16[32,4096]{1,0:T(8,128)(2,1)S(1)}, bf16[32,4096]{1,0:T(8,128)(2,1)S(1)}, u32[]{:S(2)}, u32[]{:S(2)}) collective-permute-start(bf16[32,4096]{1,0:T(8,128)(2,1)S(1)} %get-tuple-element.10), channel_id=1, source_target_pairs={{0,1},{1,2},{2,3},{3,0},{4,5},{5,6},{6,7},{7,4},{8,9},{9,10},{10,1... | collective-permute-start | bytes 786440 | tf_op jit(solution)/shard_map/ppermute | solution.py:304
  56.0 15.4 %collective-permute-start.13 = (bf16[32,4096]{1,0:T(8,128)(2,1)S(1)}, bf16[32,4096]{1,0:T(8,128)(2,1)S(1)}, u32[]{:S(2)}, u32[]{:S(2)}) collective-permute-start(bf16[32,4096]{1,0:T(8,128)(2,1)S(1)} %get-tuple-element.11), channel_id=1, source_target_pairs={{0,2},{1,3},{2,0},{3,1},{4,6},{5,7},{6,4},{7,5},{8,10},{9,11},{10,... | collective-permute-start | bytes 786440 | tf_op jit(solution)/shard_map/ppermute | solution.py:304
  59.3 12.1 %collective-permute-start.14 = (bf16[32,4096]{1,0:T(8,128)(2,1)S(1)}, bf16[32,4096]{1,0:T(8,128)(2,1)S(1)}, u32[]{:S(2)}, u32[]{:S(2)}) collective-permute-start(bf16[32,4096]{1,0:T(8,128)(2,1)S(1)} %get-tuple-element.12), channel_id=1, source_target_pairs={{0,3},{1,0},{2,1},{3,2},{4,7},{5,4},{6,5},{7,6},{8,11},{9,8},{10,9... | collective-permute-start | bytes 786440 | tf_op jit(solution)/shard_map/ppermute | solution.py:304
  (3 other events, 3.3 us)

commit v2 on v1

v2 whole, which is shorter than its diff:
```python
import jax
import jax.numpy as jnp
from jax import lax
from jax.experimental import pallas as pl
from jax.experimental.pallas import tpu as pltpu
from jax.sharding import PartitionSpec as P

BF16 = jnp.bfloat16
F32 = jnp.float32
LEAVES = 32
PARENTS = 8
ROWS = 640
SIDE = 4
NT = (((1,), (1,)), ((), ()))


def dot_nt(a, b):
    return lax.dot_general(a, b, NT, preferred_element_type=F32)


def side_by_side(a, b):
    return jnp.concatenate([a, b], axis=1)


def diagonal(a, b):
    zeros = jnp.zeros_like(a)
    return jnp.concatenate([side_by_side(a, zeros), side_by_side(zeros, b)], axis=0)


def coef_kernel(meta, sources, basis, transfer, out, rows, basis_here, transfer_here, sems):
    z = meta[0]
    copies = [
        pltpu.make_async_copy(sources.at[pl.ds(pl.multiple_of(z * 32, 32), 32), :], rows, sems.at[0]),
        pltpu.make_async_copy(basis, basis_here, sems.at[1]),
        pltpu.make_async_copy(transfer, transfer_here, sems.at[2]),
    ]
    for copy in copies:
        copy.start()
    copies[0].wait()
    copies[1].wait()
    pairs = []
    for m in range(LEAVES // 2):
        weights = diagonal(basis_here[2 * m], basis_here[2 * m + 1])
        pair = dot_nt(rows[:, 256 * m : 256 * (m + 1)], weights).astype(BF16)
        out[32 * m : 32 * (m + 1), :] = pair
        pairs.append(pair)
    copies[2].wait()
    for n in range(PARENTS // 2):
        halves = []
        for q in (2 * n, 2 * n + 1):
            children = side_by_side(pairs[2 * q], pairs[2 * q + 1])
            weights = transfer_here[4 * q : 4 * q + 4].reshape(256, 64)
            halves.append(jnp.dot(children, weights, preferred_element_type=F32))
        out[512 + 32 * n : 512 + 32 * (n + 1), :] = side_by_side(*halves).astype(BF16)


def coefficients(meta, sources, basis, transfer):
    hbm = pl.BlockSpec(memory_space=pltpu.HBM)
    return pl.pallas_call(
        coef_kernel,
        out_shape=jax.ShapeDtypeStruct((ROWS, 128), BF16),
        in_specs=[pl.BlockSpec(memory_space=pltpu.SMEM)] + [hbm] * 3,
        out_specs=pl.BlockSpec(memory_space=pltpu.VMEM),
        scratch_shapes=[
            pltpu.VMEM((32, 4096), BF16),
            pltpu.VMEM((LEAVES, 64, 128), BF16),
            pltpu.VMEM((LEAVES, 64, 64), BF16),
            pltpu.SemaphoreType.DMA((3,)),
        ],
        compiler_params=pltpu.CompilerParams(vmem_limit_bytes=8 << 20),
    )(meta, sources, basis, transfer)


def near_kernel(meta, near_list, near_count, own, before, after, near_block, *rest):
    keep, pass_on, give, window, sems = rest
    copies = [
        pltpu.make_async_copy(part, window.at[:, pl.ds(4096 * k, 4096)], sems.at[k])
        for k, part in enumerate((before, own, after))
    ]
    for copy in copies:
        copy.start()
    for copy in copies:
        copy.wait()
    z, core = meta[0], meta[1] & 1
    first = (meta[1] - 1) * LEAVES
    owners = (z, z ^ jnp.where(core == 0, 3, 1), z ^ jnp.where(core == 0, 1, 3), z ^ 2)

    def body(t, carry):
        parts = []
        for i in range(2):
            place = jnp.clip(near_list[i, t] - first, 0, 3 * LEAVES - 1)
            columns = pl.ds(pl.multiple_of(place * 128, 128), 128)
            active = z * 2 + i < near_count[t]
            rows = [
                window[pl.ds(pl.multiple_of(owner * 32, 32), 32), columns] for owner in owners
            ]
            block = jnp.concatenate(rows, axis=0)
            parts.append(lax.select(active, block, jnp.zeros_like(block)))
        weights = side_by_side(near_block[t, 0], near_block[t, 1])
        result = dot_nt(side_by_side(*parts), weights).astype(BF16)
        here = pl.ds(pl.multiple_of(t * 128, 128), 128)
        keep[:, here] = result[:32]
        pass_on[:, here] = result[32:64]
        give[:, here] = result[64:]
        return carry

    lax.fori_loop(0, LEAVES, body, 0, unroll=4)


def near_partials(meta, near_list, near_count, own, before, after, near_block):
    smem = pl.BlockSpec(memory_space=pltpu.SMEM)
    anywhere = pl.BlockSpec(memory_space=pl.ANY)
    return pl.pallas_call(
        near_kernel,
        out_shape=[jax.ShapeDtypeStruct((n, 4096), BF16) for n in (32, 32, 64)],
        in_specs=[smem] * 3 + [anywhere] * 3 + [pl.BlockSpec(memory_space=pltpu.VMEM)],
        out_specs=[pl.BlockSpec(memory_space=pltpu.VMEM)] * 3,
        scratch_shapes=[
            pltpu.VMEM((128, 3 * 4096), BF16),
            pltpu.SemaphoreType.DMA((3,)),
        ],
        compiler_params=pltpu.CompilerParams(vmem_limit_bytes=12 << 20),
    )(meta, near_list, near_count, own, before, after, near_block)


def far_kernel(leaf_codes, par_codes, held, coupling, par_coupling, transfer, basis, *rest):
    nears, out = rest[:3], rest[3]
    lane = lax.broadcasted_iota(jnp.int32, (1, 128), 1)
    low = (lane < 64).astype(F32).astype(BF16)
    high = (lane >= 64).astype(F32).astype(BF16)

    def turned(code, wanted):
        pair = held[pl.ds(pl.multiple_of(code & ~31, 32), 32), :]
        swapped = side_by_side(pair[:, 64:], pair[:, :64])
        return lax.select((code & 1) == wanted, pair, swapped)

    def couple(codes, blocks):
        terms, weights = [], []
        for i in range(0, 8, 2):
            terms.append(turned(codes[i], 0) * low + turned(codes[i + 1], 1) * high)
            weights.append(side_by_side(blocks(i), blocks(i + 1)))
        return dot_nt(jnp.concatenate(terms, axis=1), jnp.concatenate(weights, axis=1))

    def body(q, carry):
        field = couple([par_codes[q, i] for i in range(8)], lambda i: par_coupling[q, i])
        spread = dot_nt(field.astype(BF16), transfer[pl.ds(4 * q, 4)].reshape(256, 64))
        for m in range(2):
            downs = []
            for c in (2 * m, 2 * m + 1):
                leaf = 4 * q + c
                codes = [leaf_codes[i, leaf] for i in range(8)]
                local = couple(codes, lambda i: coupling[leaf, i])
                downs.append(local + spread[:, 64 * c : 64 * (c + 1)])
            down = side_by_side(*downs).astype(BF16)
            leaf = 4 * q + 2 * m
            weights = diagonal(basis[leaf], basis[leaf + 1])
            result = jnp.dot(down, weights, preferred_element_type=F32)
            here = pl.ds(pl.multiple_of(128 * leaf, 256), 256)
            for near in nears:
                result += near[:32, here].astype(F32)
            out[:, here] = result.astype(BF16)
        return carry

    lax.fori_loop(0, PARENTS, body, 0, unroll=True)


def far_and_sum(leaf_codes, par_codes, held, coupling, par_coupling, transfer, basis, nears):
    smem = pl.BlockSpec(memory_space=pltpu.SMEM)
    vmem = pl.BlockSpec(memory_space=pltpu.VMEM)
    return pl.pallas_call(
        far_kernel,
        out_shape=jax.ShapeDtypeStruct((32, 4096), BF16),
        in_specs=[smem] * 2 + [vmem] * 8,
        out_specs=vmem,
        compiler_params=pltpu.CompilerParams(vmem_limit_bytes=18 << 20),
    )(leaf_codes, par_codes, held, coupling, par_coupling, transfer, basis, *nears)


def place(y, x, core):
    return (y % SIDE) * 8 + (x % SIDE) * 2 + core


def around(distance, first):
    pairs = []
    for y in range(SIDE):
        for x in range(SIDE):
            for core in range(2):
                alongx = (core == 0) == first
                to = place(y, x + distance, core) if alongx else place(y + distance, x, core)
                pairs.append((place(y, x, core), to))
    return pairs


def partners(first):
    return [
        (c * 4 + z, c * 4 + (z ^ (1 if (c % 2 == 0) == first else 3)))
        for c in range(32)
        for z in range(4)
    ]


SWAP = [(i, i ^ 1) for i in range(32)]


def send(value, pairs):
    return lax.ppermute(value, "clus", pairs)


def joined(*parts):
    return jnp.concatenate(parts, axis=0)


def codes_of(index, shift, first_row, y, x, core):
    source = index >> shift
    sy, sx, score = source >> 3, (source >> 1) & 3, source & 1
    dy, dx = (sy - y) & 3, (sx - x) & 3
    inner = jnp.where(score == 0, dx, dy)
    outer = jnp.where(score == 0, dy, dx)

    def rank(distance):
        return (0x78 >> (2 * distance)) & 3

    chunk = jnp.where(score == core, 0, 16) + 4 * rank(outer) + rank(inner)
    pair = (index & ((1 << shift) - 1)) >> 1
    return (chunk * ROWS + first_row + pair * 32) | (index & 1)


def per_device(
    sources,
    leaf_basis,
    transfer,
    far_leaf,
    leaf_coupling,
    far_par,
    par_coupling,
    near_list,
    near_count,
    near_block,
):
    clus, rhs = lax.axis_index("clus"), lax.axis_index("rhs")
    y, x, core = clus >> 3, (clus >> 1) & 3, clus & 1
    meta = jnp.stack([rhs, clus]).astype(jnp.int32)
    leaf_codes = codes_of(far_leaf.T, 5, 0, y, x, core)
    par_codes = codes_of(far_par, 3, 512, y, x, core)
    basis = jnp.swapaxes(leaf_basis, 1, 2)
    halo_before = send(sources, [(i, (i + 1) % 32) for i in range(32)])
    halo_after = send(sources, [((i + 1) % 32, i) for i in range(32)])
    chunk = coefficients(meta, sources, basis, transfer)

    before = send(chunk, around(1, True))
    after = send(chunk, around(-1, True))
    across = send(chunk, around(2, True))
    before, after, across, halo_before, halo_after = lax.optimization_barrier(
        (before, after, across, halo_before, halo_after)
    )
    own = joined(chunk, before, after, across)
    side_b = send(own, around(1, False))
    side_a = send(own, around(-1, False))
    keep, pass_on, give = near_partials(
        meta, near_list.T, near_count, sources, halo_before, halo_after, near_block
    )
    taken = lax.ppermute(give, ("clus", "rhs"), partners(True))
    side_b, side_a, pass_on = lax.optimization_barrier((side_b, side_a, pass_on))
    half = own.shape[0] // 2
    far_b = send(side_b[:half], around(1, False))
    far_a = send(side_a[half:], around(-1, False))
    pass_on = (pass_on.astype(F32) + taken[32:].astype(F32)).astype(BF16)
    far_b, far_a, pass_on = lax.optimization_barrier((far_b, far_a, pass_on))
    nears = (keep, taken, lax.ppermute(pass_on, ("clus", "rhs"), partners(False)))
    sides, far = joined(side_b, side_a), joined(far_b, far_a)
    held = joined(own, sides, far, send(own, SWAP), send(sides, SWAP), send(far, SWAP))
    return far_and_sum(
        leaf_codes, par_codes, held, leaf_coupling, par_coupling, transfer, basis, nears
    )


def solution(mesh):
    in_specs = (
        P(None, "clus"),
        P("clus", None, None),
        P("clus", None, None),
        P("clus", None),
        P("clus", None, None, None),
        P("clus", None),
        P("clus", None, None, None),
        P("clus", "rhs"),
        P("clus"),
        P("clus", "rhs", None, None),
    )
    return jax.shard_map(
        per_device, mesh=mesh, in_specs=in_specs, out_specs=P("rhs", "clus"), check_vma=False
    )
```

time: 89.2 us -> 61.5 us (0.69)
  the two profiles are of different devices: /device:TPU:1 before, /device:TPU:6 now
where the time goes in v2:
time: 61.5 us; the launch traced here: 61 us
  waiting for transfers between devices  19.5 us (32%)
  starting transfers between devices  19.1 us (31%)
  Pallas kernels  11 us (18%)
  local copies, waits for them, and re-layouts  8.45 us (14%)
  other arithmetic  2.72 us (4%)
    ppermute x12, starting transfers between devices, send(): return lax.ppermute(value, 'clus', pairs)  15.6 us
    ppermute x12, waiting for transfers between devices, send(): return lax.ppermute(value, 'clus', pairs)  12.7 us
    unnamed x32, local copies, waits for them, and re-layouts  8.32 us
    pallas_call x1, Pallas kernels, far_and_sum(): pl.pallas_call(far_kernel, out_shape=jax.ShapeDtypeStruct((32, 4096), BF1...  5.77 us
    ppermute x1, waiting for transfers between devices, per_device(): lax.ppermute(pass_on, ('clus', 'rhs'), partners(False))  5.72 us
    pallas_call x1, Pallas kernels, near_partials(): pl.pallas_call(near_kernel, out_shape=[jax.ShapeDtypeStruct((n, 4096), BF...  3.88 us
    ppermute x1, starting transfers between devices, per_device(): taken = lax.ppermute(give, ('clus', 'rhs'), partners(True))  2.1 us
    or x2, other arithmetic, codes_of(): return chunk * ROWS + first_row + pair * 32 | index & 1  1.41 us
  transfers between devices with their start and end apart: 14, of which 5 were waited for; matrix products, arithmetic and copies ran while one was open for 7% of the time, Pallas kernels for 9%

profile of v2, /device:TPU:6, one launch (start us, length us, event | category | flops | bytes accessed | tf_op | source)
XLA Modules:
  0.0 61.0 jit_solution(16514624843854589041)
XLA Ops:
  0.0 1.7 %collective-permute-start.4 = (bf16[128,4096]{1,0:T(8,128)(2,1)}, bf16[128,4096]{1,0:T(8,128)(2,1)}, u32[]{:S(2)}, u32[]{:S(2)}) collective-permute-start(bf16[128,4096]{1,0:T(8,128)(2,1)} %own.1), channel_id=1, source_target_pairs={{4,0},{8,4},{12,8},{16,12},{20,16},{24,20},{28,24},{32,28},{36,32}... | collective-permute-start | bytes 3145736 | tf_op jit(solution)/shard_map/ppermute | solution.py:206
  1.8 1.2 %copy-done = bf16[128,4096]{1,0:T(8,128)(2,1)S(1)} copy-done((bf16[128,4096]{1,0:T(8,128)(2,1)S(1)}, bf16[128,4096]{1,0:T(8,128)(2,1)}, u32[]{:S(2)}) %copy-start) | copy-done | bytes 1048600
  3.0 1.0 %copy-done.4 = bf16[32,128,64]{1,2,0:T(8,128)(2,1)S(1)} copy-done((bf16[32,128,64]{1,2,0:T(8,128)(2,1)S(1)}, bf16[32,128,64]{1,2,0:T(8,128)(2,1)}, u32[]{:S(2)}) %copy-start.4) | copy-done | bytes 524312
  4.1 1.0 %copy-done.6 = bf16[32,64,64]{2,1,0:T(8,128)(2,1)S(1)} copy-done((bf16[32,64,64]{2,1,0:T(8,128)(2,1)S(1)}, bf16[32,64,64]{2,1,0:T(8,128)(2,1)}, u32[]{:S(2)}) %copy-start.6) | copy-done | bytes 262168
  5.1 1.4 %shard_map.100 = bf16[640,128]{1,0:T(8,128)(2,1)S(1)} custom-call(s32[2]{0:T(128)S(1)} %pad_add_fusion.meta, bf16[128,4096]{1,0:T(8,128)(2,1)S(1)} %copy-done, bf16[32,64,128]{2,1,0:T(8,128)(2,1)S(1)} %bitcast.6, bf16[32,64,64]{2,1,0:T(8,128)(2,1)S(1)} %copy-done.6), custom_call_target="tpu_custom_call" | custom-call | tf_op jit(solution)/shard_map/pallas_call | solution.py:59
  6.5 3.8 %collective-permute-start = (bf16[640,128]{1,0:T(8,128)(2,1)S(1)}, bf16[640,128]{1,0:T(8,128)(2,1)S(1)}, u32[]{:S(2)}, u32[]{:S(2)}) collective-permute-start(bf16[640,128]{1,0:T(8,128)(2,1)S(1)} %shard_map.100), channel_id=1, source_target_pairs={{0,8},{4,36},{8,16},{12,44},{16,24},{20,52},{24,0},{28,60},{32,40}... | collective-permute-start | bytes 491528 | tf_op jit(solution)/shard_map/ppermute | solution.py:206
  10.3 1.5 %collective-permute-start.2 = (bf16[640,128]{1,0:T(8,128)(2,1)S(1)}, bf16[640,128]{1,0:T(8,128)(2,1)}, u32[]{:S(2)}, u32[]{:S(2)}) collective-permute-start(bf16[640,128]{1,0:T(8,128)(2,1)S(1)} %shard_map.100), channel_id=1, source_target_pairs={{0,16},{4,68},{8,24},{12,76},{16,0},{20,84},{24,8},{28,92},{32,48}... | collective-permute-start | bytes 491528 | tf_op jit(solution)/shard_map/ppermute | solution.py:206
  12.6 2.4 %collective-permute-done = bf16[640,128]{1,0:T(8,128)(2,1)S(1)} collective-permute-done((bf16[640,128]{1,0:T(8,128)(2,1)S(1)}, bf16[640,128]{1,0:T(8,128)(2,1)S(1)}, u32[]{:S(2)}, u32[]{:S(2)}) %collective-permute-start) | collective-permute-done | bytes 163872 | tf_op jit(solution)/shard_map/ppermute | solution.py:206
  15.0 7.1 %collective-permute-done.1 = bf16[640,128]{1,0:T(8,128)(2,1)} collective-permute-done((bf16[640,128]{1,0:T(8,128)(2,1)S(1)}, bf16[640,128]{1,0:T(8,128)(2,1)}, u32[]{:S(2)}, u32[]{:S(2)}) %collective-permute-start.1) | collective-permute-done | bytes 163872 | tf_op jit(solution)/shard_map/ppermute | solution.py:206
  22.1 1.0 %pad_maximum_fusion.1 = bf16[2560,128]{1,0:T(8,128)(2,1)S(1)} fusion(bf16[640,128]{1,0:T(8,128)(2,1)} %collective-permute-done.2, bf16[640,128]{1,0:T(8,128)(2,1)} %collective-permute-done.1, bf16[640,128]{1,0:T(8,128)(2,1)S(1)} %collective-permute-done, bf16[640,128]{1,0:T(8,128)(2,1)S(1)} %shard_map.100), kind=kLoop, calls=%fused_computation.1 | loop fusion | flops 2621440 | bytes 1310720 | tf_op jit(solution)/shard_map/concatenate | solution.py:210
  23.7 2.8 %collective-permute-start.6 = (bf16[2560,128]{1,0:T(8,128)(2,1)S(1)}, bf16[2560,128]{1,0:T(8,128)(2,1)S(1)}, u32[]{:S(2)}, u32[]{:S(2)}) collective-permute-start(bf16[2560,128]{1,0:T(8,128)(2,1)S(1)} %pad_maximum_fusion.1), channel_id=1, source_target_pairs={{0,96},{4,28},{8,104},{12,4},{16,112},{20,12},{24,120},{28,20},{32... | collective-permute-start | bytes 1966088 | tf_op jit(solution)/shard_map/ppermute | solution.py:206
  26.5 0.7 %and_or_fusion.par_codes = s32[8,8]{1,0:T(8,128)S(1)} fusion(s32[8,8]{1,0:T(8,128)} %param.15, s32[]{:T(128)S(6)} %and.76, s32[]{:T(128)S(6)} %shift_right_arithmetic.52, s32[]{:T(128)S(6)} %and.72), kind=kLoop, calls=%fused_computation.16 | loop fusion | flops 1984 | bytes 524 | tf_op jit(solution)/shard_map/or | solution.py:225
  27.3 1.2 %copy-done.1 = bf16[128,4096]{1,0:T(8,128)(2,1)S(1)} copy-done((bf16[128,4096]{1,0:T(8,128)(2,1)S(1)}, bf16[128,4096]{1,0:T(8,128)(2,1)}, u32[]{:S(2)}) %copy-start.1) | copy-done | bytes 1048600
  29.9 3.9 %shard_map.101 = (bf16[32,4096]{1,0:T(8,128)(2,1)S(1)}, bf16[32,4096]{1,0:T(8,128)(2,1)S(1)}, bf16[64,4096]{1,0:T(8,128)(2,1)S(1)}) custom-call(s32[2]{0:T(128)S(1)} %pad_add_fusion.meta, s32[2,32]{1,0:T(2,128)S(1)} %bitcast.8, s32[32]{0:T(128)S(1)} %copy-done.10, bf16[128,4096]{1,0:T(8,128)(2,1)S(1)} %copy-done.1, ...), custom_call_target="tpu_custom_call" | custom-call | tf_op jit(solution)/shard_map/pallas_call | solution.py:113
  33.7 2.1 %collective-permute-start.9 = (bf16[64,4096]{1,0:T(8,128)(2,1)S(1)}, bf16[64,4096]{1,0:T(8,128)(2,1)S(1)}, u32[]{:S(2)}, u32[]{:S(2)}) collective-permute-start(bf16[64,4096]{1,0:T(8,128)(2,1)S(1)} %get-tuple-element.28), channel_id=1, source_target_pairs={{0,1},{1,0},{2,3},{3,2},{4,7},{5,6},{6,5},{7,4},{8,9},{9,8},{10,11... | collective-permute-start | bytes 1572872 | tf_op jit(solution)/shard_map/ppermute | solution.py:262
  35.9 0.9 %constant_dynamic-update-slice_fusion.8 = bf16[20480,128]{1,0:T(8,128)(2,1)S(1)} fusion(bf16[20480,128]{1,0:T(8,128)(2,1)S(1)} %constant_dynamic-update-slice_fusion.9, bf16[640,128]{1,0:T(8,128)(2,1)} %collective-permute-done.1), kind=kLoop, calls=%fused_computation.12 | loop fusion | bytes 327680
  36.8 0.9 %constant_dynamic-update-slice_fusion.7 = bf16[20480,128]{1,0:T(8,128)(2,1)S(1)} fusion(bf16[20480,128]{1,0:T(8,128)(2,1)S(1)} %constant_dynamic-update-slice_fusion.8, bf16[640,128]{1,0:T(8,128)(2,1)} %collective-permute-done.2), kind=kLoop, calls=%fused_computation.11 | loop fusion | bytes 327680
  38.1 3.2 %collective-permute-start.8 = (bf16[1280,128]{1,0:T(8,128)(2,1)S(1)}, bf16[1280,128]{1,0:T(8,128)(2,1)S(1)}, u32[]{:S(2)}, u32[]{:S(2)}) collective-permute-start(bf16[1280,128]{1,0:T(8,128)(2,1)S(1)} %slice.10), channel_id=1, source_target_pairs={{0,96},{4,28},{8,104},{12,4},{16,112},{20,12},{24,120},{28,20},{32... | collective-permute-start | bytes 983048 | tf_op jit(solution)/shard_map/ppermute | solution.py:206
  41.9 1.1 %collective-permute-done.9.rest_1_ = bf16[64,4096]{1,0:T(8,128)(2,1)S(1)} collective-permute-done((bf16[64,4096]{1,0:T(8,128)(2,1)S(1)}, bf16[64,4096]{1,0:T(8,128)(2,1)S(1)}, u32[]{:S(2)}, u32[]{:S(2)}) %collective-permute-start.9) | collective-permute-done | bytes 524320 | tf_op jit(solution)/shard_map/ppermute | solution.py:262
  43.2 3.1 %collective-permute-done.7 = bf16[1280,128]{1,0:T(8,128)(2,1)S(1)} collective-permute-done((bf16[1280,128]{1,0:T(8,128)(2,1)S(1)}, bf16[1280,128]{1,0:T(8,128)(2,1)S(1)}, u32[]{:S(2)}, u32[]{:S(2)}) %collective-permute-start.7) | collective-permute-done | bytes 327712 | tf_op jit(solution)/shard_map/ppermute | solution.py:206
  46.3 1.3 %collective-permute-start.12 = (bf16[2560,128]{1,0:T(8,128)(2,1)S(1)}, bf16[2560,128]{1,0:T(8,128)(2,1)S(1)}, u32[]{:S(2)}, u32[]{:S(2)}) collective-permute-start(bf16[2560,128]{1,0:T(8,128)(2,1)S(1)} %pad_maximum_fusion.2), channel_id=1, source_target_pairs={{0,4},{4,0},{8,12},{12,8},{16,20},{20,16},{24,28},{28,24},{32,36},... | collective-permute-start | bytes 1966088 | tf_op jit(solution)/shard_map/ppermute | solution.py:206
  47.6 1.4 %collective-permute-start.13 = (bf16[32,4096]{1,0:T(8,128)(2,1)S(1)}, bf16[32,4096]{1,0:T(8,128)(2,1)S(1)}, u32[]{:S(2)}, u32[]{:S(2)}) collective-permute-start(bf16[32,4096]{1,0:T(8,128)(2,1)S(1)} %add_convert_fusion), channel_id=1, source_target_pairs={{0,3},{1,2},{2,1},{3,0},{4,5},{5,4},{6,7},{7,6},{8,11},{9,10},{10,... | collective-permute-start | bytes 786440 | tf_op jit(solution)/shard_map/ppermute | solution.py:269
  49.5 5.7 %collective-permute-done.13.rest_2_ = bf16[32,4096]{1,0:T(8,128)(2,1)S(1)} collective-permute-done((bf16[32,4096]{1,0:T(8,128)(2,1)S(1)}, bf16[32,4096]{1,0:T(8,128)(2,1)S(1)}, u32[]{:S(2)}, u32[]{:S(2)}) %collective-permute-start.13) | collective-permute-done | bytes 262176 | tf_op jit(solution)/shard_map/ppermute | solution.py:269
  55.2 5.8 %shard_map.102 = bf16[32,4096]{1,0:T(8,128)(2,1)} custom-call(s32[8,32]{1,0:T(8,128)S(1)} %or_bitcast_fusion.leaf_codes, s32[8,8]{1,0:T(8,128)S(1)} %and_or_fusion.par_codes, bf16[20480,128]{1,0:T(8,128)(2,1)S(1)} %constant_dynamic-update-slice_fusion.held, bf16[32,8,64,64]{3,2,1,0:T(8,128)(2,1)S(1)} %copy-done.2, bf16[8,8,64,64]{3,2,1,0:T(8,128)(2,1)S(1)} %copy-done.8, ...), custom_call_target="tpu_custom_call" | custom-call | tf_op jit(solution)/shard_map/pallas_call | solution.py:170
  (49 shorter events, 4.3 us)
Async XLA Ops:
  0.0 22.1 %collective-permute-start.3 = (bf16[128,4096]{1,0:T(8,128)(2,1)}, bf16[128,4096]{1,0:T(8,128)(2,1)S(1)}, u32[]{:S(2)}, u32[]{:S(2)}) collective-permute-start(bf16[128,4096]{1,0:T(8,128)(2,1)} %own.1), channel_id=1, source_target_pairs={{0,4},{4,8},{8,12},{12,16},{16,20},{20,24},{24,28},{28,32},{32,36}... | collective-permute-start | bytes 3145736 | tf_op jit(solution)/shard_map/ppermute | solution.py:206
  0.0 22.1 %collective-permute-start.4 = (bf16[128,4096]{1,0:T(8,128)(2,1)}, bf16[128,4096]{1,0:T(8,128)(2,1)}, u32[]{:S(2)}, u32[]{:S(2)}) collective-permute-start(bf16[128,4096]{1,0:T(8,128)(2,1)} %own.1), channel_id=1, source_target_pairs={{4,0},{8,4},{12,8},{16,12},{20,16},{24,20},{28,24},{32,28},{36,32}... | collective-permute-start | bytes 3145736 | tf_op jit(solution)/shard_map/ppermute | solution.py:206
  1.8 1.2 %copy-start = (bf16[128,4096]{1,0:T(8,128)(2,1)S(1)}, bf16[128,4096]{1,0:T(8,128)(2,1)}, u32[]{:S(2)}) copy-start(bf16[128,4096]{1,0:T(8,128)(2,1)} %own.1) | copy-start | bytes 3145732
  3.0 1.0 %copy-start.4 = (bf16[32,128,64]{1,2,0:T(8,128)(2,1)S(1)}, bf16[32,128,64]{1,2,0:T(8,128)(2,1)}, u32[]{:S(2)}) copy-start(bf16[32,128,64]{1,2,0:T(8,128)(2,1)} %param.11) | copy-start | bytes 1572868
  4.1 1.0 %copy-start.6 = (bf16[32,64,64]{2,1,0:T(8,128)(2,1)S(1)}, bf16[32,64,64]{2,1,0:T(8,128)(2,1)}, u32[]{:S(2)}) copy-start(bf16[32,64,64]{2,1,0:T(8,128)(2,1)} %transfer.3) | copy-start | bytes 786436
  5.1 22.1 %copy-start.3 = (bf16[32,2,128,128]{3,2,1,0:T(8,128)(2,1)S(1)}, bf16[32,2,128,128]{3,2,1,0:T(8,128)(2,1)}, u32[]{:S(2)}) copy-start(bf16[32,2,128,128]{3,2,1,0:T(8,128)(2,1)} %near_block.1) | copy-start | bytes 6291460
  6.5 8.4 %collective-permute-start = (bf16[640,128]{1,0:T(8,128)(2,1)S(1)}, bf16[640,128]{1,0:T(8,128)(2,1)S(1)}, u32[]{:S(2)}, u32[]{:S(2)}) collective-permute-start(bf16[640,128]{1,0:T(8,128)(2,1)S(1)} %shard_map.100), channel_id=1, source_target_pairs={{0,8},{4,36},{8,16},{12,44},{16,24},{20,52},{24,0},{28,60},{32,40}... | collective-permute-start | bytes 491528 | tf_op jit(solution)/shard_map/ppermute | solution.py:206
  10.3 11.8 %collective-permute-start.1 = (bf16[640,128]{1,0:T(8,128)(2,1)S(1)}, bf16[640,128]{1,0:T(8,128)(2,1)}, u32[]{:S(2)}, u32[]{:S(2)}) collective-permute-start(bf16[640,128]{1,0:T(8,128)(2,1)S(1)} %shard_map.100), channel_id=1, source_target_pairs={{0,24},{4,100},{8,0},{12,108},{16,8},{20,116},{24,16},{28,124},{32... | collective-permute-start | bytes 491528 | tf_op jit(solution)/shard_map/ppermute | solution.py:206
  10.3 11.8 %collective-permute-start.2 = (bf16[640,128]{1,0:T(8,128)(2,1)S(1)}, bf16[640,128]{1,0:T(8,128)(2,1)}, u32[]{:S(2)}, u32[]{:S(2)}) collective-permute-start(bf16[640,128]{1,0:T(8,128)(2,1)S(1)} %shard_map.100), channel_id=1, source_target_pairs={{0,16},{4,68},{8,24},{12,76},{16,0},{20,84},{24,8},{28,92},{32,48}... | collective-permute-start | bytes 491528 | tf_op jit(solution)/shard_map/ppermute | solution.py:206
  23.2 14.6 %collective-permute-start.5 = (bf16[2560,128]{1,0:T(8,128)(2,1)S(1)}, bf16[2560,128]{1,0:T(8,128)(2,1)S(1)}, u32[]{:S(2)}, u32[]{:S(2)}) collective-permute-start(bf16[2560,128]{1,0:T(8,128)(2,1)S(1)} %pad_maximum_fusion.1), channel_id=1, source_target_pairs={{0,32},{4,12},{8,40},{12,20},{16,48},{20,28},{24,56},{28,4},{32,64... | collective-permute-start | bytes 1966088 | tf_op jit(solution)/shard_map/ppermute | solution.py:206
  23.7 14.1 %collective-permute-start.6 = (bf16[2560,128]{1,0:T(8,128)(2,1)S(1)}, bf16[2560,128]{1,0:T(8,128)(2,1)S(1)}, u32[]{:S(2)}, u32[]{:S(2)}) collective-permute-start(bf16[2560,128]{1,0:T(8,128)(2,1)S(1)} %pad_maximum_fusion.1), channel_id=1, source_target_pairs={{0,96},{4,28},{8,104},{12,4},{16,112},{20,12},{24,120},{28,20},{32... | collective-permute-start | bytes 1966088 | tf_op jit(solution)/shard_map/ppermute | solution.py:206
  27.2 21.9 %collective-permute-start.10 = (bf16[2560,128]{1,0:T(8,128)(2,1)S(1)}, bf16[2560,128]{1,0:T(8,128)(2,1)S(1)}, u32[]{:S(2)}, u32[]{:S(2)}) collective-permute-start(bf16[2560,128]{1,0:T(8,128)(2,1)S(1)} %pad_maximum_fusion.1), channel_id=1, source_target_pairs={{0,4},{4,0},{8,12},{12,8},{16,20},{20,16},{24,28},{28,24},{32,36},... | collective-permute-start | bytes 1966088 | tf_op jit(solution)/shard_map/ppermute | solution.py:206
  27.3 1.2 %copy-start.1 = (bf16[128,4096]{1,0:T(8,128)(2,1)S(1)}, bf16[128,4096]{1,0:T(8,128)(2,1)}, u32[]{:S(2)}) copy-start(bf16[128,4096]{1,0:T(8,128)(2,1)} %own.1) | copy-start | bytes 3145732
  28.5 0.7 %copy-start.9 = (s32[32,2]{0,1:T(2,128)S(1)}, s32[32,2]{0,1:T(2,128)}, u32[]{:S(2)}) copy-start(s32[32,2]{0,1:T(2,128)} %param.17) | copy-start | bytes 772
  33.7 9.3 %collective-permute-start.9 = (bf16[64,4096]{1,0:T(8,128)(2,1)S(1)}, bf16[64,4096]{1,0:T(8,128)(2,1)S(1)}, u32[]{:S(2)}, u32[]{:S(2)}) collective-permute-start(bf16[64,4096]{1,0:T(8,128)(2,1)S(1)} %get-tuple-element.28), channel_id=1, source_target_pairs={{0,1},{1,0},{2,3},{3,2},{4,7},{5,6},{6,5},{7,4},{8,9},{9,8},{10,11... | collective-permute-start | bytes 1572872 | tf_op jit(solution)/shard_map/ppermute | solution.py:262
  37.9 8.4 %collective-permute-start.7 = (bf16[1280,128]{1,0:T(8,128)(2,1)S(1)}, bf16[1280,128]{1,0:T(8,128)(2,1)S(1)}, u32[]{:S(2)}, u32[]{:S(2)}) collective-permute-start(bf16[1280,128]{1,0:T(8,128)(2,1)S(1)} %slice.9), channel_id=1, source_target_pairs={{0,32},{4,12},{8,40},{12,20},{16,48},{20,28},{24,56},{28,4},{32,64... | collective-permute-start | bytes 983048 | tf_op jit(solution)/shard_map/ppermute | solution.py:206
  38.1 8.2 %collective-permute-start.8 = (bf16[1280,128]{1,0:T(8,128)(2,1)S(1)}, bf16[1280,128]{1,0:T(8,128)(2,1)S(1)}, u32[]{:S(2)}, u32[]{:S(2)}) collective-permute-start(bf16[1280,128]{1,0:T(8,128)(2,1)S(1)} %slice.10), channel_id=1, source_target_pairs={{0,96},{4,28},{8,104},{12,4},{16,112},{20,12},{24,120},{28,20},{32... | collective-permute-start | bytes 983048 | tf_op jit(solution)/shard_map/ppermute | solution.py:206
  41.2 8.0 %collective-permute-start.11 = (bf16[5120,128]{1,0:T(8,128)(2,1)S(1)}, bf16[5120,128]{1,0:T(8,128)(2,1)S(1)}, u32[]{:S(2)}, u32[]{:S(2)}) collective-permute-start(bf16[5120,128]{1,0:T(8,128)(2,1)S(1)} %pad_maximum_fusion), channel_id=1, source_target_pairs={{0,4},{4,0},{8,12},{12,8},{16,20},{20,16},{24,28},{28,24},{32,36},... | collective-permute-start | bytes 3932168 | tf_op jit(solution)/shard_map/ppermute | solution.py:206
  41.9 13.4 %copy-start.2 = (bf16[32,8,64,64]{3,2,1,0:T(8,128)(2,1)S(1)}, bf16[32,8,64,64]{3,2,1,0:T(8,128)(2,1)}, u32[]{:S(2)}) copy-start(bf16[32,8,64,64]{3,2,1,0:T(8,128)(2,1)} %coupling.1) | copy-start | bytes 6291460
  41.9 13.4 %copy-start.5 = (bf16[32,128,64]{1,2,0:T(8,128)(2,1)S(1)}, bf16[32,128,64]{1,2,0:T(8,128)(2,1)}, u32[]{:S(2)}) copy-start(bf16[32,128,64]{1,2,0:T(8,128)(2,1)} %param.11) | copy-start | bytes 1572868
  41.9 13.4 %copy-start.7 = (bf16[32,64,64]{2,1,0:T(8,128)(2,1)S(1)}, bf16[32,64,64]{2,1,0:T(8,128)(2,1)}, u32[]{:S(2)}) copy-start(bf16[32,64,64]{2,1,0:T(8,128)(2,1)} %transfer.3) | copy-start | bytes 786436
  41.9 13.3 %copy-start.8 = (bf16[8,8,64,64]{3,2,1,0:T(8,128)(2,1)S(1)}, bf16[8,8,64,64]{3,2,1,0:T(8,128)(2,1)}, u32[]{:S(2)}) copy-start(bf16[8,8,64,64]{3,2,1,0:T(8,128)(2,1)} %par_coupling.1) | copy-start | bytes 1572868
  46.3 3.1 %collective-permute-start.12 = (bf16[2560,128]{1,0:T(8,128)(2,1)S(1)}, bf16[2560,128]{1,0:T(8,128)(2,1)S(1)}, u32[]{:S(2)}, u32[]{:S(2)}) collective-permute-start(bf16[2560,128]{1,0:T(8,128)(2,1)S(1)} %pad_maximum_fusion.2), channel_id=1, source_target_pairs={{0,4},{4,0},{8,12},{12,8},{16,20},{20,16},{24,28},{28,24},{32,36},... | collective-permute-start | bytes 1966088 | tf_op jit(solution)/shard_map/ppermute | solution.py:206
  47.6 7.6 %collective-permute-start.13 = (bf16[32,4096]{1,0:T(8,128)(2,1)S(1)}, bf16[32,4096]{1,0:T(8,128)(2,1)S(1)}, u32[]{:S(2)}, u32[]{:S(2)}) collective-permute-start(bf16[32,4096]{1,0:T(8,128)(2,1)S(1)} %add_convert_fusion), channel_id=1, source_target_pairs={{0,3},{1,2},{2,1},{3,0},{4,5},{5,4},{6,7},{7,6},{8,11},{9,10},{10,... | collective-permute-start | bytes 786440 | tf_op jit(solution)/shard_map/ppermute | solution.py:269
  (1 other events, 0.7 us)

commit v3 on v2

--- a/solution.py
+++ b/solution.py
@@ -27,24 +27,54 @@
     return jnp.concatenate([side_by_side(a, zeros), side_by_side(zeros, b)], axis=0)
 
 
-def coef_kernel(meta, sources, basis, transfer, out, rows, basis_here, transfer_here, sems):
-    z = meta[0]
-    copies = [
-        pltpu.make_async_copy(sources.at[pl.ds(pl.multiple_of(z * 32, 32), 32), :], rows, sems.at[0]),
-        pltpu.make_async_copy(basis, basis_here, sems.at[1]),
-        pltpu.make_async_copy(transfer, transfer_here, sems.at[2]),
-    ]
+def codes_of(index, shift, first_row, y, x, core):
+    source = index >> shift
+    dy, dx = ((source >> 3) - y) & 3, ((source >> 1) - x) & 3
+    along_x = (source & 1) == 0
+    inner, outer = jnp.where(along_x, dx, dy), jnp.where(along_x, dy, dx)
+
+    def rank(distance):
+        return jnp.where(distance == 0, 0, jnp.where(distance == 3, 1, distance + 1))
+
+    chunk = ((source ^ core) & 1) * 16 + 4 * rank(outer) + rank(inner)
+    pair = (index & ((1 << shift) - 1)) >> 1
+    return (chunk * ROWS + first_row + pair * 32) | (index & 1)
+
+
+def coef_kernel(meta, *refs):
+    sources, basis, transfer, far_leaf, far_par, near_list, near_count, near_block = refs[:8]
+    out, leaf_codes, par_codes, near_codes, own, near_here = refs[8:14]
+    rows, basis_here, transfer_here, leaf_here, par_here, list_here, count_here, sems = refs[14:]
+    z, clus = meta[0], meta[1]
+    mine = sources.at[pl.ds(pl.multiple_of(z * 32, 32), 32), :]
+    moves = (
+        (mine, rows),
+        (basis, basis_here),
+        (transfer, transfer_here),
+        (far_leaf, leaf_here),
+        (far_par, par_here),
+        (near_list, list_here),
+        (near_count, count_here),
+        (sources, own),
+        (near_block, near_here),
+    )
+    copies = [pltpu.make_async_copy(a, b, sems.at[n]) for n, (a, b) in enumerate(moves)]
     for copy in copies:
         copy.start()
-    copies[0].wait()
-    copies[1].wait()
+    for copy in copies[:7]:
+        copy.wait()
+    y, x, core = clus >> 3, (clus >> 1) & 3, clus & 1
+    leaf_codes[...] = codes_of(leaf_here[...], 5, 0, y, x, core)
+    par_codes[...] = codes_of(par_here[...], 3, 512, y, x, core)
+    slot = z * 2 + lax.broadcasted_iota(jnp.int32, (2, LEAVES), 0)
+    place = jnp.clip(list_here[...] - (clus - 1) * LEAVES, 0, 3 * LEAVES - 1)
+    near_codes[...] = jnp.where(slot < count_here[...], place, -1)
     pairs = []
     for m in range(LEAVES // 2):
         weights = diagonal(basis_here[2 * m], basis_here[2 * m + 1])
         pair = dot_nt(rows[:, 256 * m : 256 * (m + 1)], weights).astype(BF16)
         out[32 * m : 32 * (m + 1), :] = pair
         pairs.append(pair)
-    copies[2].wait()
     for n in range(PARENTS // 2):
         halves = []
         for q in (2 * n, 2 * n + 1):
@@ -52,50 +82,70 @@
             weights = transfer_here[4 * q : 4 * q + 4].reshape(256, 64)
             halves.append(jnp.dot(children, weights, preferred_element_type=F32))
         out[512 + 32 * n : 512 + 32 * (n + 1), :] = side_by_side(*halves).astype(BF16)
-
-
-def coefficients(meta, sources, basis, transfer):
+    for copy in copies[7:]:
+        copy.wait()
+
+
+def coefficients(meta, *arrays):
     hbm = pl.BlockSpec(memory_space=pltpu.HBM)
+    vmem = pl.BlockSpec(memory_space=pltpu.VMEM)
+    tables = [(8, LEAVES), (PARENTS, 8), (2, LEAVES)]
     return pl.pallas_call(
         coef_kernel,
-        out_shape=jax.ShapeDtypeStruct((ROWS, 128), BF16),
-        in_specs=[pl.BlockSpec(memory_space=pltpu.SMEM)] + [hbm] * 3,
-        out_specs=pl.BlockSpec(memory_space=pltpu.VMEM),
+        out_shape=[pltpu.VMEM((ROWS, 128), BF16)]
+        + [jax.ShapeDtypeStruct(table, jnp.int32) for table in tables]
+        + [pltpu.VMEM((128, 4096), BF16), pltpu.VMEM((LEAVES, 2, 128, 128), BF16)],
+        in_specs=[pl.BlockSpec(memory_space=pltpu.SMEM)] + [hbm] * 8,
+        out_specs=[vmem] * 6,
         scratch_shapes=[
             pltpu.VMEM((32, 4096), BF16),
             pltpu.VMEM((LEAVES, 64, 128), BF16),
             pltpu.VMEM((LEAVES, 64, 64), BF16),
-            pltpu.SemaphoreType.DMA((3,)),
+            pltpu.VMEM(tables[0], jnp.int32),
+            pltpu.VMEM(tables[1], jnp.int32),
+            pltpu.VMEM(tables[2], jnp.int32),
+            pltpu.VMEM((1, LEAVES), jnp.int32),
+            pltpu.SemaphoreType.DMA((9,)),
         ],
         compiler_params=pltpu.CompilerParams(vmem_limit_bytes=8 << 20),
-    )(meta, sources, basis, transfer)
-
-
-def near_kernel(meta, near_list, near_count, own, before, after, near_block, *rest):
-    keep, pass_on, give, window, sems = rest
-    copies = [
-        pltpu.make_async_copy(part, window.at[:, pl.ds(4096 * k, 4096)], sems.at[k])
-        for k, part in enumerate((before, own, after))
-    ]
-    for copy in copies:
-        copy.start()
-    for copy in copies:
-        copy.wait()
+    )(meta, *(pltpu.with_memory_space_constraint(array, pltpu.HBM) for array in arrays))
+
+
+def stack_kernel(*refs):
+    out = refs[-1]
+    for k, part in enumerate(refs[:-1]):
+        out[ROWS * k : ROWS * (k + 1), :] = part[...]
+
+
+def stacked(*parts):
+    vmem = pl.BlockSpec(memory_space=pltpu.VMEM)
+    return pl.pallas_call(
+        stack_kernel,
+        out_shape=pltpu.VMEM((ROWS * len(parts), 128), BF16),
+        in_specs=[vmem] * len(parts),
+        out_specs=vmem,
+        compiler_params=pltpu.CompilerParams(vmem_limit_bytes=4 << 20),
+    )(*(pltpu.with_memory_space_constraint(part, pltpu.VMEM) for part in parts))
+
+
+def near_kernel(meta, near_codes, own, before, after, near_block, keep, pass_on, give):
     z, core = meta[0], meta[1] & 1
-    first = (meta[1] - 1) * LEAVES
     owners = (z, z ^ jnp.where(core == 0, 3, 1), z ^ jnp.where(core == 0, 1, 3), z ^ 2)
 
     def body(t, carry):
         parts = []
         for i in range(2):
-            place = jnp.clip(near_list[i, t] - first, 0, 3 * LEAVES - 1)
-            columns = pl.ds(pl.multiple_of(place * 128, 128), 128)
-            active = z * 2 + i < near_count[t]
-            rows = [
-                window[pl.ds(pl.multiple_of(owner * 32, 32), 32), columns] for owner in owners
-            ]
+            code = near_codes[i, t]
+            index = jnp.maximum(code, 0)
+            columns = pl.ds(pl.multiple_of((index & 31) * 128, 128), 128)
+            rows = []
+            for owner in owners:
+                here = pl.ds(pl.multiple_of(owner * 32, 32), 32)
+                outer = lax.select(index < 32, before[here, columns], after[here, columns])
+                inside = (index >> 5) == 1
+                rows.append(lax.select(inside, own[here, columns], outer))
             block = jnp.concatenate(rows, axis=0)
-            parts.append(lax.select(active, block, jnp.zeros_like(block)))
+            parts.append(lax.select(code >= 0, block, jnp.zeros_like(block)))
         weights = side_by_side(near_block[t, 0], near_block[t, 1])
         result = dot_nt(side_by_side(*parts), weights).astype(BF16)
         here = pl.ds(pl.multiple_of(t * 128, 128), 128)
@@ -104,23 +154,19 @@
         give[:, here] = result[64:]
         return carry
 
-    lax.fori_loop(0, LEAVES, body, 0, unroll=4)
-
-
-def near_partials(meta, near_list, near_count, own, before, after, near_block):
+    lax.fori_loop(0, LEAVES, body, 0, unroll=8)
+
+
+def near_partials(meta, near_codes, own, before, after, near_block):
     smem = pl.BlockSpec(memory_space=pltpu.SMEM)
-    anywhere = pl.BlockSpec(memory_space=pl.ANY)
+    vmem = pl.BlockSpec(memory_space=pltpu.VMEM)
     return pl.pallas_call(
         near_kernel,
         out_shape=[jax.ShapeDtypeStruct((n, 4096), BF16) for n in (32, 32, 64)],
-        in_specs=[smem] * 3 + [anywhere] * 3 + [pl.BlockSpec(memory_space=pltpu.VMEM)],
-        out_specs=[pl.BlockSpec(memory_space=pltpu.VMEM)] * 3,
-        scratch_shapes=[
-            pltpu.VMEM((128, 3 * 4096), BF16),
-            pltpu.SemaphoreType.DMA((3,)),
-        ],
+        in_specs=[smem] * 2 + [vmem] * 4,
+        out_specs=[vmem] * 3,
         compiler_params=pltpu.CompilerParams(vmem_limit_bytes=12 << 20),
-    )(meta, near_list, near_count, own, before, after, near_block)
+    )(meta, near_codes, own, before, after, near_block)
 
 
 def far_kernel(leaf_codes, par_codes, held, coupling, par_coupling, transfer, basis, *rest):
@@ -210,21 +256,6 @@
     return jnp.concatenate(parts, axis=0)
 
 
-def codes_of(index, shift, first_row, y, x, core):
-    source = index >> shift
-    sy, sx, score = source >> 3, (source >> 1) & 3, source & 1
-    dy, dx = (sy - y) & 3, (sx - x) & 3
-    inner = jnp.where(score == 0, dx, dy)
-    outer = jnp.where(score == 0, dy, dx)
-
-    def rank(distance):
-        return (0x78 >> (2 * distance)) & 3
-
-    chunk = jnp.where(score == core, 0, 16) + 4 * rank(outer) + rank(inner)
-    pair = (index & ((1 << shift) - 1)) >> 1
-    return (chunk * ROWS + first_row + pair * 32) | (index & 1)
-
-
 def per_device(
     sources,
     leaf_basis,
@@ -238,26 +269,33 @@
     near_block,
 ):
     clus, rhs = lax.axis_index("clus"), lax.axis_index("rhs")
-    y, x, core = clus >> 3, (clus >> 1) & 3, clus & 1
     meta = jnp.stack([rhs, clus]).astype(jnp.int32)
-    leaf_codes = codes_of(far_leaf.T, 5, 0, y, x, core)
-    par_codes = codes_of(far_par, 3, 512, y, x, core)
     basis = jnp.swapaxes(leaf_basis, 1, 2)
     halo_before = send(sources, [(i, (i + 1) % 32) for i in range(32)])
     halo_after = send(sources, [((i + 1) % 32, i) for i in range(32)])
-    chunk = coefficients(meta, sources, basis, transfer)
-
+    chunk, leaf_codes, par_codes, near_codes, sources_here, near_here = coefficients(
+        meta,
+        sources,
+        basis,
+        transfer,
+        far_leaf.T,
+        far_par,
+        near_list.T,
+        near_count.reshape(1, -1),
+        near_block,
+    )
+
+    across = send(chunk, around(2, True))
     before = send(chunk, around(1, True))
     after = send(chunk, around(-1, True))
-    across = send(chunk, around(2, True))
     before, after, across, halo_before, halo_after = lax.optimization_barrier(
         (before, after, across, halo_before, halo_after)
     )
-    own = joined(chunk, before, after, across)
+    own = stacked(chunk, before, after, across)
     side_b = send(own, around(1, False))
     side_a = send(own, around(-1, False))
     keep, pass_on, give = near_partials(
-        meta, near_list.T, near_count, sources, halo_before, halo_after, near_block
+        meta, near_codes, sources_here, halo_before, halo_after, near_here
     )
     taken = lax.ppermute(give, ("clus", "rhs"), partners(True))
     side_b, side_a, pass_on = lax.optimization_barrier((side_b, side_a, pass_on))
@@ -265,8 +303,9 @@
     far_b = send(side_b[:half], around(1, False))
     far_a = send(side_a[half:], around(-1, False))
     pass_on = (pass_on.astype(F32) + taken[32:].astype(F32)).astype(BF16)
-    far_b, far_a, pass_on = lax.optimization_barrier((far_b, far_a, pass_on))
-    nears = (keep, taken, lax.ppermute(pass_on, ("clus", "rhs"), partners(False)))
+    passed = lax.ppermute(pass_on, ("clus", "rhs"), partners(False))
+    far_b, far_a, passed = lax.optimization_barrier((far_b, far_a, passed))
+    nears = (keep, taken, passed)
     sides, far = joined(side_b, side_a), joined(far_b, far_a)
     held = joined(own, sides, far, send(own, SWAP), send(sides, SWAP), send(far, SWAP))
     return far_and_sum(

time: 61.5 us -> 54.8 us (0.89)
  local copies, waits for them, and re-layouts: 8.45 us -> 0.72 us
  other arithmetic: 2.72 us -> 0.27 us
  waiting for transfers between devices: 19.5 us -> 21.4 us
  starting transfers between devices: 19.1 us -> 20.1 us
  Pallas kernels: 11 us -> 11.7 us
    unnamed x32 -> x15, local copies, waits for them, and re-layouts: 8.32 us -> 0.59 us
    ppermute x12, waiting for transfers between devices: 12.7 us -> 17.1 us  [send(): return lax.ppermute(value, 'clus', pairs)]
    ppermute x1, starting transfers between devices: 1.37 us -> 4.2 us  [per_device(): passed = lax.ppermute(pass_on, ('clus', 'rhs'), partners(False))]
    ppermute x12, starting transfers between devices: 15.6 us -> 13.9 us  [send(): return lax.ppermute(value, 'clus', pairs)]
    pallas_call x1 -> x2, Pallas kernels: 1.38 us -> 3.05 us  [the longest x1 3.01 us: coefficients(): pl.pallas_call(coef_kernel, out_shape=[pltpu.VMEM((ROWS, 128), BF16)] + [...]
    ppermute x1, waiting for transfers between devices: 5.72 us -> 4.26 us  [per_device(): passed = lax.ppermute(pass_on, ('clus', 'rhs'), partners(False))]
    or x2 -> x0, other arithmetic: 1.41 us -> none  [codes_of(): return chunk * ROWS + first_row + pair * 32 | index & 1]
    ppermute x1, waiting for transfers between devices: 1.1 us -> 0.01 us  [per_device(): taken = lax.ppermute(give, ('clus', 'rhs'), partners(True))]
  transfers between devices with their start and end apart: 14 -> 14, of which waited for: 5 -> 5; matrix products, arithmetic and copies ran while one was open for 7% -> 2% of each run, Pallas kernels for 9% -> 11%
where the time goes in v3:
time: 54.8 us; the launch traced here: 54.4 us
  waiting for transfers between devices  21.4 us (39%)
  starting transfers between devices  20.1 us (37%)
  Pallas kernels  11.7 us (21%)
  local copies, waits for them, and re-layouts  0.72 us (1%)
    ppermute x12, waiting for transfers between devices, send(): return lax.ppermute(value, 'clus', pairs)  17.1 us
    ppermute x12, starting transfers between devices, send(): return lax.ppermute(value, 'clus', pairs)  13.9 us
    pallas_call x1, Pallas kernels, far_and_sum(): pl.pallas_call(far_kernel, out_shape=jax.ShapeDtypeStruct((32, 4096), BF1...  5.76 us
    ppermute x1, waiting for transfers between devices, per_device(): passed = lax.ppermute(pass_on, ('clus', 'rhs'), partners(False))  4.26 us
    ppermute x1, starting transfers between devices, per_device(): passed = lax.ppermute(pass_on, ('clus', 'rhs'), partners(False))  4.2 us
    pallas_call x1, Pallas kernels, coefficients(): pl.pallas_call(coef_kernel, out_shape=[pltpu.VMEM((ROWS, 128), BF16)] + [...  3.01 us
    pallas_call x1, Pallas kernels, near_partials(): pl.pallas_call(near_kernel, out_shape=[jax.ShapeDtypeStruct((n, 4096), BF...  2.85 us
    ppermute x1, starting transfers between devices, per_device(): taken = lax.ppermute(give, ('clus', 'rhs'), partners(True))  2.08 us
  transfers between devices with their start and end apart: 14, of which 5 were waited for; matrix products, arithmetic and copies ran while one was open for 2% of the time, Pallas kernels for 11%

profile of v3, /device:TPU:6, one launch (start us, length us, event | category | flops | bytes accessed | tf_op | source)
XLA Modules:
  0.0 54.4 jit_solution(10929786585596909198)
XLA Ops:
  0.0 1.7 %collective-permute-start.4 = (bf16[128,4096]{1,0:T(8,128)(2,1)}, bf16[128,4096]{1,0:T(8,128)(2,1)S(1)}, u32[]{:S(2)}, u32[]{:S(2)}) collective-permute-start(bf16[128,4096]{1,0:T(8,128)(2,1)} %refs_0_.1), channel_id=1, source_target_pairs={{4,0},{8,4},{12,8},{16,12},{20,16},{24,20},{28,24},{32,28},{36,32}... | collective-permute-start | bytes 3145736 | tf_op jit(solution)/shard_map/ppermute | solution.py:252
  1.8 3.0 %shard_map.100 = (bf16[640,128]{1,0:T(8,128)(2,1)S(1)}, s32[8,32]{1,0:T(8,128)S(1)}, s32[8,8]{1,0:T(8,128)S(1)}, s32[2,32]{1,0:T(2,128)S(1)}, bf16[128,4096]{1,0...) custom-call(s32[2]{0:T(128)S(1)} %pad_add_fusion.meta, bf16[128,4096]{1,0:T(8,128)(2,1)} %refs_0_.1, ...), custom_call_target="tpu_custom_call" | custom-call | tf_op jit(solution)/shard_map/pallas_call | solution.py:93
  4.8 3.8 %collective-permute-start = (bf16[640,128]{1,0:T(8,128)(2,1)S(1)}, bf16[640,128]{1,0:T(8,128)(2,1)S(1)}, u32[]{:S(2)}, u32[]{:S(2)}) collective-permute-start(bf16[640,128]{1,0:T(8,128)(2,1)S(1)} %get-tuple-element.27.refs_0_), channel_id=1, source_target_pairs={{0,8},{4,36},{8,16},{12,44},{16,24},{20,52},{24,0},{28,60},{32,40}... | collective-permute-start | bytes 491528 | tf_op jit(solution)/shard_map/ppermute | solution.py:252
  8.6 1.5 %collective-permute-start.2 = (bf16[640,128]{1,0:T(8,128)(2,1)S(1)}, bf16[640,128]{1,0:T(8,128)(2,1)S(1)}, u32[]{:S(2)}, u32[]{:S(2)}) collective-permute-start(bf16[640,128]{1,0:T(8,128)(2,1)S(1)} %get-tuple-element.27.refs_0_), channel_id=1, source_target_pairs={{0,16},{4,68},{8,24},{12,76},{16,0},{20,84},{24,8},{28,92},{32,48}... | collective-permute-start | bytes 491528 | tf_op jit(solution)/shard_map/ppermute | solution.py:252
  10.2 3.1 %collective-permute-done.refs_1_ = bf16[640,128]{1,0:T(8,128)(2,1)S(1)} collective-permute-done((bf16[640,128]{1,0:T(8,128)(2,1)S(1)}, bf16[640,128]{1,0:T(8,128)(2,1)S(1)}, u32[]{:S(2)}, u32[]{:S(2)}) %collective-permute-start) | collective-permute-done | bytes 163872 | tf_op jit(solution)/shard_map/ppermute | solution.py:252
  13.3 8.7 %collective-permute-done.1.refs_2_ = bf16[640,128]{1,0:T(8,128)(2,1)S(1)} collective-permute-done((bf16[640,128]{1,0:T(8,128)(2,1)S(1)}, bf16[640,128]{1,0:T(8,128)(2,1)S(1)}, u32[]{:S(2)}, u32[]{:S(2)}) %collective-permute-start.1) | collective-permute-done | bytes 163872 | tf_op jit(solution)/shard_map/ppermute | solution.py:252
  22.1 0.5 collective-permute-start.5
  22.6 2.8 %collective-permute-start.6 = (bf16[2560,128]{1,0:T(8,128)(2,1)S(1)}, bf16[2560,128]{1,0:T(8,128)(2,1)S(1)}, u32[]{:S(2)}, u32[]{:S(2)}) collective-permute-start(bf16[2560,128]{1,0:T(8,128)(2,1)S(1)} %shard_map.101), channel_id=1, source_target_pairs={{0,96},{4,28},{8,104},{12,4},{16,112},{20,12},{24,120},{28,20},{32... | collective-permute-start | bytes 1966088 | tf_op jit(solution)/shard_map/ppermute | solution.py:252
  25.4 2.8 %shard_map.102 = (bf16[32,4096]{1,0:T(8,128)(2,1)S(1)}, bf16[32,4096]{1,0:T(8,128)(2,1)S(1)}, bf16[64,4096]{1,0:T(8,128)(2,1)S(1)}) custom-call(s32[2]{0:T(128)S(1)} %pad_add_fusion.meta, s32[2,32]{1,0:T(2,128)S(1)} %get-tuple-element.31.near_codes, bf16[128,4096]{1,0:T(8,128)(2,1)S(1)} %get-tuple-element.32.own, ...), custom_call_target="tpu_custom_call" | custom-call | tf_op jit(solution)/shard_map/pallas_call | solution.py:163
  28.2 2.1 %collective-permute-start.9 = (bf16[64,4096]{1,0:T(8,128)(2,1)S(1)}, bf16[64,4096]{1,0:T(8,128)(2,1)S(1)}, u32[]{:S(2)}, u32[]{:S(2)}) collective-permute-start(bf16[64,4096]{1,0:T(8,128)(2,1)S(1)} %get-tuple-element.40), channel_id=1, source_target_pairs={{0,1},{1,0},{2,3},{3,2},{4,7},{5,6},{6,5},{7,4},{8,9},{9,8},{10,11... | collective-permute-start | bytes 1572872 | tf_op jit(solution)/shard_map/ppermute | solution.py:300
  30.4 3.6 %collective-permute-done.5 = bf16[2560,128]{1,0:T(8,128)(2,1)S(1)} collective-permute-done((bf16[2560,128]{1,0:T(8,128)(2,1)S(1)}, bf16[2560,128]{1,0:T(8,128)(2,1)S(1)}, u32[]{:S(2)}, u32[]{:S(2)}) %collective-permute-start.5) | collective-permute-done | bytes 655392 | tf_op jit(solution)/shard_map/ppermute | solution.py:252
  34.0 0.1 constant_dynamic-update-slice_fusion.6
  34.1 0.9 %collective-permute-start.7 = (bf16[1280,128]{1,0:T(8,128)(2,1)S(1)}, bf16[1280,128]{1,0:T(8,128)(2,1)S(1)}, u32[]{:S(2)}, u32[]{:S(2)}) collective-permute-start(bf16[1280,128]{1,0:T(8,128)(2,1)S(1)} %slice.9), channel_id=1, source_target_pairs={{0,32},{4,12},{8,40},{12,20},{16,48},{20,28},{24,56},{28,4},{32,64... | collective-permute-start | bytes 983048 | tf_op jit(solution)/shard_map/ppermute | solution.py:252
  35.0 2.5 %collective-permute-start.8 = (bf16[1280,128]{1,0:T(8,128)(2,1)S(1)}, bf16[1280,128]{1,0:T(8,128)(2,1)S(1)}, u32[]{:S(2)}, u32[]{:S(2)}) collective-permute-start(bf16[1280,128]{1,0:T(8,128)(2,1)S(1)} %slice.10), channel_id=1, source_target_pairs={{0,96},{4,28},{8,104},{12,4},{16,112},{20,12},{24,120},{28,20},{32... | collective-permute-start | bytes 983048 | tf_op jit(solution)/shard_map/ppermute | solution.py:252
  37.5 0.1 pad_maximum_fusion
  37.7 4.2 %collective-permute-start.10 = (bf16[32,4096]{1,0:T(8,128)(2,1)S(1)}, bf16[32,4096]{1,0:T(8,128)(2,1)S(1)}, u32[]{:S(2)}, u32[]{:S(2)}) collective-permute-start(bf16[32,4096]{1,0:T(8,128)(2,1)S(1)} %add_convert_fusion), channel_id=1, source_target_pairs={{0,3},{1,2},{2,1},{3,0},{4,5},{5,4},{6,7},{7,6},{8,11},{9,10},{10,... | collective-permute-start | bytes 786440 | tf_op jit(solution)/shard_map/ppermute | solution.py:306
  41.9 0.1 constant_dynamic-update-slice_fusion.5
  42.0 4.3 %collective-permute-done.10.rest_2_ = bf16[32,4096]{1,0:T(8,128)(2,1)S(1)} collective-permute-done((bf16[32,4096]{1,0:T(8,128)(2,1)S(1)}, bf16[32,4096]{1,0:T(8,128)(2,1)S(1)}, u32[]{:S(2)}, u32[]{:S(2)}) %collective-permute-start.10) | collective-permute-done | bytes 262176 | tf_op jit(solution)/shard_map/ppermute | solution.py:306
  46.3 0.1 collective-permute-start.13
  46.5 0.1 constant_dynamic-update-slice_fusion.2
  46.6 0.2 constant_dynamic-update-slice_fusion.1
  46.8 1.7 %collective-permute-done.13 = bf16[2560,128]{1,0:T(8,128)(2,1)S(1)} collective-permute-done((bf16[2560,128]{1,0:T(8,128)(2,1)S(1)}, bf16[2560,128]{1,0:T(8,128)(2,1)S(1)}, u32[]{:S(2)}, u32[]{:S(2)}) %collective-permute-start.13) | collective-permute-done | bytes 655392 | tf_op jit(solution)/shard_map/ppermute | solution.py:252
  48.5 0.1 constant_dynamic-update-slice_fusion.held
  48.6 5.8 %shard_map.103 = bf16[32,4096]{1,0:T(8,128)(2,1)} custom-call(s32[8,32]{1,0:T(8,128)S(1)} %get-tuple-element.25.leaf_codes, s32[8,8]{1,0:T(8,128)S(1)} %get-tuple-element.26.par_codes, bf16[20480,128]{1,0:T(8,128)(2,1)S(1)} %constant_dynamic-update-slice_fusion.held, bf16[32,8,64,64]{3,2,1,0:T(8,128)(2,1)S(1)} %copy-done, ...), custom_call_target="tpu_custom_call" | custom-call | tf_op jit(solution)/shard_map/pallas_call | solution.py:216
  (30 shorter events, 0.5 us)
Async XLA Ops:
  0.0 22.0 %collective-permute-start.3 = (bf16[128,4096]{1,0:T(8,128)(2,1)}, bf16[128,4096]{1,0:T(8,128)(2,1)S(1)}, u32[]{:S(2)}, u32[]{:S(2)}) collective-permute-start(bf16[128,4096]{1,0:T(8,128)(2,1)} %refs_0_.1), channel_id=1, source_target_pairs={{0,4},{4,8},{8,12},{12,16},{16,20},{20,24},{24,28},{28,32},{32,36}... | collective-permute-start | bytes 3145736 | tf_op jit(solution)/shard_map/ppermute | solution.py:252
  0.0 22.0 %collective-permute-start.4 = (bf16[128,4096]{1,0:T(8,128)(2,1)}, bf16[128,4096]{1,0:T(8,128)(2,1)S(1)}, u32[]{:S(2)}, u32[]{:S(2)}) collective-permute-start(bf16[128,4096]{1,0:T(8,128)(2,1)} %refs_0_.1), channel_id=1, source_target_pairs={{4,0},{8,4},{12,8},{16,12},{20,16},{24,20},{28,24},{32,28},{36,32}... | collective-permute-start | bytes 3145736 | tf_op jit(solution)/shard_map/ppermute | solution.py:252
  4.8 8.4 %collective-permute-start = (bf16[640,128]{1,0:T(8,128)(2,1)S(1)}, bf16[640,128]{1,0:T(8,128)(2,1)S(1)}, u32[]{:S(2)}, u32[]{:S(2)}) collective-permute-start(bf16[640,128]{1,0:T(8,128)(2,1)S(1)} %get-tuple-element.27.refs_0_), channel_id=1, source_target_pairs={{0,8},{4,36},{8,16},{12,44},{16,24},{20,52},{24,0},{28,60},{32,40}... | collective-permute-start | bytes 491528 | tf_op jit(solution)/shard_map/ppermute | solution.py:252
  8.6 13.4 %collective-permute-start.1 = (bf16[640,128]{1,0:T(8,128)(2,1)S(1)}, bf16[640,128]{1,0:T(8,128)(2,1)S(1)}, u32[]{:S(2)}, u32[]{:S(2)}) collective-permute-start(bf16[640,128]{1,0:T(8,128)(2,1)S(1)} %get-tuple-element.27.refs_0_), channel_id=1, source_target_pairs={{0,24},{4,100},{8,0},{12,108},{16,8},{20,116},{24,16},{28,124},{32... | collective-permute-start | bytes 491528 | tf_op jit(solution)/shard_map/ppermute | solution.py:252
  8.6 13.4 %collective-permute-start.2 = (bf16[640,128]{1,0:T(8,128)(2,1)S(1)}, bf16[640,128]{1,0:T(8,128)(2,1)S(1)}, u32[]{:S(2)}, u32[]{:S(2)}) collective-permute-start(bf16[640,128]{1,0:T(8,128)(2,1)S(1)} %get-tuple-element.27.refs_0_), channel_id=1, source_target_pairs={{0,16},{4,68},{8,24},{12,76},{16,0},{20,84},{24,8},{28,92},{32,48}... | collective-permute-start | bytes 491528 | tf_op jit(solution)/shard_map/ppermute | solution.py:252
  22.1 11.9 %collective-permute-start.5 = (bf16[2560,128]{1,0:T(8,128)(2,1)S(1)}, bf16[2560,128]{1,0:T(8,128)(2,1)S(1)}, u32[]{:S(2)}, u32[]{:S(2)}) collective-permute-start(bf16[2560,128]{1,0:T(8,128)(2,1)S(1)} %shard_map.101), channel_id=1, source_target_pairs={{0,32},{4,12},{8,40},{12,20},{16,48},{20,28},{24,56},{28,4},{32,64... | collective-permute-start | bytes 1966088 | tf_op jit(solution)/shard_map/ppermute | solution.py:252
  22.6 11.3 %collective-permute-start.6 = (bf16[2560,128]{1,0:T(8,128)(2,1)S(1)}, bf16[2560,128]{1,0:T(8,128)(2,1)S(1)}, u32[]{:S(2)}, u32[]{:S(2)}) collective-permute-start(bf16[2560,128]{1,0:T(8,128)(2,1)S(1)} %shard_map.101), channel_id=1, source_target_pairs={{0,96},{4,28},{8,104},{12,4},{16,112},{20,12},{24,120},{28,20},{32... | collective-permute-start | bytes 1966088 | tf_op jit(solution)/shard_map/ppermute | solution.py:252
  25.4 21.1 %collective-permute-start.11 = (bf16[2560,128]{1,0:T(8,128)(2,1)S(1)}, bf16[2560,128]{1,0:T(8,128)(2,1)S(1)}, u32[]{:S(2)}, u32[]{:S(2)}) collective-permute-start(bf16[2560,128]{1,0:T(8,128)(2,1)S(1)} %shard_map.101), channel_id=1, source_target_pairs={{0,4},{4,0},{8,12},{12,8},{16,20},{20,16},{24,28},{28,24},{32,36},... | collective-permute-start | bytes 1966088 | tf_op jit(solution)/shard_map/ppermute | solution.py:252
  28.2 9.4 %collective-permute-start.9 = (bf16[64,4096]{1,0:T(8,128)(2,1)S(1)}, bf16[64,4096]{1,0:T(8,128)(2,1)S(1)}, u32[]{:S(2)}, u32[]{:S(2)}) collective-permute-start(bf16[64,4096]{1,0:T(8,128)(2,1)S(1)} %get-tuple-element.40), channel_id=1, source_target_pairs={{0,1},{1,0},{2,3},{3,2},{4,7},{5,6},{6,5},{7,4},{8,9},{9,8},{10,11... | collective-permute-start | bytes 1572872 | tf_op jit(solution)/shard_map/ppermute | solution.py:300
  34.1 12.2 %collective-permute-start.7 = (bf16[1280,128]{1,0:T(8,128)(2,1)S(1)}, bf16[1280,128]{1,0:T(8,128)(2,1)S(1)}, u32[]{:S(2)}, u32[]{:S(2)}) collective-permute-start(bf16[1280,128]{1,0:T(8,128)(2,1)S(1)} %slice.9), channel_id=1, source_target_pairs={{0,32},{4,12},{8,40},{12,20},{16,48},{20,28},{24,56},{28,4},{32,64... | collective-permute-start | bytes 983048 | tf_op jit(solution)/shard_map/ppermute | solution.py:252
  35.0 11.3 %collective-permute-start.8 = (bf16[1280,128]{1,0:T(8,128)(2,1)S(1)}, bf16[1280,128]{1,0:T(8,128)(2,1)S(1)}, u32[]{:S(2)}, u32[]{:S(2)}) collective-permute-start(bf16[1280,128]{1,0:T(8,128)(2,1)S(1)} %slice.10), channel_id=1, source_target_pairs={{0,96},{4,28},{8,104},{12,4},{16,112},{20,12},{24,120},{28,20},{32... | collective-permute-start | bytes 983048 | tf_op jit(solution)/shard_map/ppermute | solution.py:252
  37.6 11.0 %copy-start = (bf16[32,8,64,64]{3,2,1,0:T(8,128)(2,1)S(1)}, bf16[32,8,64,64]{3,2,1,0:T(8,128)(2,1)}, u32[]{:S(2)}) copy-start(bf16[32,8,64,64]{3,2,1,0:T(8,128)(2,1)} %coupling.1) | copy-start | bytes 6291460
  37.6 11.0 %copy-start.1 = (bf16[32,128,64]{1,2,0:T(8,128)(2,1)S(1)}, bf16[32,128,64]{1,2,0:T(8,128)(2,1)}, u32[]{:S(2)}) copy-start(bf16[32,128,64]{1,2,0:T(8,128)(2,1)} %param.11) | copy-start | bytes 1572868
  37.6 11.0 %copy-start.2 = (bf16[32,64,64]{2,1,0:T(8,128)(2,1)S(1)}, bf16[32,64,64]{2,1,0:T(8,128)(2,1)}, u32[]{:S(2)}) copy-start(bf16[32,64,64]{2,1,0:T(8,128)(2,1)} %transfer.1) | copy-start | bytes 786436
  37.6 11.0 %copy-start.3 = (bf16[8,8,64,64]{3,2,1,0:T(8,128)(2,1)S(1)}, bf16[8,8,64,64]{3,2,1,0:T(8,128)(2,1)}, u32[]{:S(2)}) copy-start(bf16[8,8,64,64]{3,2,1,0:T(8,128)(2,1)} %par_coupling.1) | copy-start | bytes 1572868
  37.7 8.6 %collective-permute-start.10 = (bf16[32,4096]{1,0:T(8,128)(2,1)S(1)}, bf16[32,4096]{1,0:T(8,128)(2,1)S(1)}, u32[]{:S(2)}, u32[]{:S(2)}) collective-permute-start(bf16[32,4096]{1,0:T(8,128)(2,1)S(1)} %add_convert_fusion), channel_id=1, source_target_pairs={{0,3},{1,2},{2,1},{3,0},{4,5},{5,4},{6,7},{7,6},{8,11},{9,10},{10,... | collective-permute-start | bytes 786440 | tf_op jit(solution)/shard_map/ppermute | solution.py:306
  41.9 4.7 %collective-permute-start.12 = (bf16[5120,128]{1,0:T(8,128)(2,1)S(1)}, bf16[5120,128]{1,0:T(8,128)(2,1)S(1)}, u32[]{:S(2)}, u32[]{:S(2)}) collective-permute-start(bf16[5120,128]{1,0:T(8,128)(2,1)S(1)} %pad_maximum_fusion), channel_id=1, source_target_pairs={{0,4},{4,0},{8,12},{12,8},{16,20},{20,16},{24,28},{28,24},{32,36},... | collective-permute-start | bytes 3932168 | tf_op jit(solution)/shard_map/ppermute | solution.py:252
  46.3 2.2 %collective-permute-start.13 = (bf16[2560,128]{1,0:T(8,128)(2,1)S(1)}, bf16[2560,128]{1,0:T(8,128)(2,1)S(1)}, u32[]{:S(2)}, u32[]{:S(2)}) collective-permute-start(bf16[2560,128]{1,0:T(8,128)(2,1)S(1)} %pad_maximum_fusion.1), channel_id=1, source_target_pairs={{0,4},{4,0},{8,12},{12,8},{16,20},{20,16},{24,28},{28,24},{32,36},... | collective-permute-start | bytes 1966088 | tf_op jit(solution)/shard_map/ppermute | solution.py:252

commit v4 on v3

--- a/solution.py
+++ b/solution.py
@@ -11,7 +11,12 @@
 PARENTS = 8
 ROWS = 640
 SIDE = 4
+COEF_US, STACK_US, NEAR_US, FAR_US, ADD_US = 3, 0, 3, 3, 10
 NT = (((1,), (1,)), ((), ()))
+
+
+def cost(us):
+    return pl.CostEstimate(flops=us * 10**9, bytes_accessed=us * 35 * 10**5, transcendentals=0)
 
 
 def dot_nt(a, b):
@@ -107,6 +112,7 @@
             pltpu.VMEM((1, LEAVES), jnp.int32),
             pltpu.SemaphoreType.DMA((9,)),
         ],
+        cost_estimate=cost(COEF_US),
         compiler_params=pltpu.CompilerParams(vmem_limit_bytes=8 << 20),
     )(meta, *(pltpu.with_memory_space_constraint(array, pltpu.HBM) for array in arrays))
 
@@ -124,53 +130,80 @@
         out_shape=pltpu.VMEM((ROWS * len(parts), 128), BF16),
         in_specs=[vmem] * len(parts),
         out_specs=vmem,
+        cost_estimate=cost(STACK_US),
         compiler_params=pltpu.CompilerParams(vmem_limit_bytes=4 << 20),
     )(*(pltpu.with_memory_space_constraint(part, pltpu.VMEM) for part in parts))
 
 
-def near_kernel(meta, near_codes, own, before, after, near_block, keep, pass_on, give):
+def near_kernel(meta, near_codes, own, sibling, far_mine, far_other, near_block, *rest):
+    keep, pass_on, give, result = rest
     z, core = meta[0], meta[1] & 1
-    owners = (z, z ^ jnp.where(core == 0, 3, 1), z ^ jnp.where(core == 0, 1, 3), z ^ 2)
+    half = z & 1
+    mine = pl.ds(pl.multiple_of(half * 64, 64), 64)
+    other = pl.ds(pl.multiple_of(64 - half * 64, 64), 64)
+    outside = lax.select(core == 0, 0, 2)
 
     def body(t, carry):
         parts = []
         for i in range(2):
             code = near_codes[i, t]
             index = jnp.maximum(code, 0)
+            part = index >> 5
             columns = pl.ds(pl.multiple_of((index & 31) * 128, 128), 128)
             rows = []
-            for owner in owners:
-                here = pl.ds(pl.multiple_of(owner * 32, 32), 32)
-                outer = lax.select(index < 32, before[here, columns], after[here, columns])
-                inside = (index >> 5) == 1
-                rows.append(lax.select(inside, own[here, columns], outer))
+            for here, far in ((mine, far_mine), (other, far_other)):
+                near = lax.select(part == 1, own[here, columns], sibling[here, columns])
+                rows.append(lax.select(part == outside, far[:, columns], near))
             block = jnp.concatenate(rows, axis=0)
             parts.append(lax.select(code >= 0, block, jnp.zeros_like(block)))
         weights = side_by_side(near_block[t, 0], near_block[t, 1])
-        result = dot_nt(side_by_side(*parts), weights).astype(BF16)
         here = pl.ds(pl.multiple_of(t * 128, 128), 128)
-        keep[:, here] = result[:32]
-        pass_on[:, here] = result[32:64]
-        give[:, here] = result[64:]
+        result[:, here] = dot_nt(side_by_side(*parts), weights).astype(BF16)
         return carry
 
     lax.fori_loop(0, LEAVES, body, 0, unroll=8)
 
-
-def near_partials(meta, near_codes, own, before, after, near_block):
+    def of(owner):
+        start = (((owner >> 1) ^ half) & 1) * 64 + (owner & 1) * 32
+        return result[pl.ds(pl.multiple_of(start, 32), 32), :]
+
+    keep[...] = of(z)
+    pass_on[...] = of(z ^ lax.select(core == 0, 3, 1))
+    give[:32, :] = of(z ^ lax.select(core == 0, 1, 3))
+    give[32:, :] = of(z ^ 2)
+
+
+def near_partials(meta, near_codes, own, sibling, far_mine, far_other, near_block):
     smem = pl.BlockSpec(memory_space=pltpu.SMEM)
     vmem = pl.BlockSpec(memory_space=pltpu.VMEM)
     return pl.pallas_call(
         near_kernel,
         out_shape=[jax.ShapeDtypeStruct((n, 4096), BF16) for n in (32, 32, 64)],
-        in_specs=[smem] * 2 + [vmem] * 4,
+        in_specs=[smem] * 2 + [vmem] * 5,
         out_specs=[vmem] * 3,
+        scratch_shapes=[pltpu.VMEM((128, 4096), BF16)],
+        cost_estimate=cost(NEAR_US),
         compiler_params=pltpu.CompilerParams(vmem_limit_bytes=12 << 20),
-    )(meta, near_codes, own, before, after, near_block)
-
-
-def far_kernel(leaf_codes, par_codes, held, coupling, par_coupling, transfer, basis, *rest):
-    nears, out = rest[:3], rest[3]
+    )(meta, near_codes, own, sibling, far_mine, far_other, near_block)
+
+
+def add_kernel(mine, taken, out):
+    out[...] = (mine[...].astype(F32) + taken[32:, :].astype(F32)).astype(BF16)
+
+
+def added(mine, taken):
+    vmem = pl.BlockSpec(memory_space=pltpu.VMEM)
+    return pl.pallas_call(
+        add_kernel,
+        out_shape=jax.ShapeDtypeStruct((32, 4096), BF16),
+        in_specs=[vmem] * 2,
+        out_specs=vmem,
+        cost_estimate=cost(ADD_US),
+        compiler_params=pltpu.CompilerParams(vmem_limit_bytes=4 << 20),
+    )(mine, taken)
+
+
+def far_kernel(leaf_codes, par_codes, held, coupling, par_coupling, transfer, out):
     lane = lax.broadcasted_iota(jnp.int32, (1, 128), 1)
     low = (lane < 64).astype(F32).astype(BF16)
     high = (lane >= 64).astype(F32).astype(BF16)
@@ -197,29 +230,45 @@
                 codes = [leaf_codes[i, leaf] for i in range(8)]
                 local = couple(codes, lambda i: coupling[leaf, i])
                 downs.append(local + spread[:, 64 * c : 64 * (c + 1)])
-            down = side_by_side(*downs).astype(BF16)
-            leaf = 4 * q + 2 * m
-            weights = diagonal(basis[leaf], basis[leaf + 1])
-            result = jnp.dot(down, weights, preferred_element_type=F32)
-            here = pl.ds(pl.multiple_of(128 * leaf, 256), 256)
-            for near in nears:
-                result += near[:32, here].astype(F32)
-            out[:, here] = result.astype(BF16)
+            here = pl.ds(pl.multiple_of((2 * q + m) * 128, 128), 128)
+            out[:, here] = side_by_side(*downs).astype(BF16)
         return carry
 
     lax.fori_loop(0, PARENTS, body, 0, unroll=True)
 
 
-def far_and_sum(leaf_codes, par_codes, held, coupling, par_coupling, transfer, basis, nears):
+def far_down(leaf_codes, par_codes, held, coupling, par_coupling, transfer):
     smem = pl.BlockSpec(memory_space=pltpu.SMEM)
     vmem = pl.BlockSpec(memory_space=pltpu.VMEM)
     return pl.pallas_call(
         far_kernel,
+        out_shape=jax.ShapeDtypeStruct((32, 2048), BF16),
+        in_specs=[smem] * 2 + [vmem] * 4,
+        out_specs=vmem,
+        cost_estimate=cost(FAR_US),
+        compiler_params=pltpu.CompilerParams(vmem_limit_bytes=18 << 20),
+    )(leaf_codes, par_codes, held, coupling, par_coupling, transfer)
+
+
+def sum_kernel(down, basis, keep, taken, passed, out):
+    for m in range(LEAVES // 2):
+        weights = diagonal(basis[2 * m], basis[2 * m + 1])
+        pair = down[:, 128 * m : 128 * (m + 1)]
+        result = jnp.dot(pair, weights, preferred_element_type=F32)
+        here = slice(256 * m, 256 * (m + 1))
+        near = keep[:, here].astype(F32) + taken[:32, here].astype(F32)
+        out[:, here] = (result + (near + passed[:, here].astype(F32))).astype(BF16)
+
+
+def far_and_sum(down, basis, *nears):
+    vmem = pl.BlockSpec(memory_space=pltpu.VMEM)
+    return pl.pallas_call(
+        sum_kernel,
         out_shape=jax.ShapeDtypeStruct((32, 4096), BF16),
-        in_specs=[smem] * 2 + [vmem] * 8,
+        in_specs=[vmem] * 5,
         out_specs=vmem,
-        compiler_params=pltpu.CompilerParams(vmem_limit_bytes=18 << 20),
-    )(leaf_codes, par_codes, held, coupling, par_coupling, transfer, basis, *nears)
+        compiler_params=pltpu.CompilerParams(vmem_limit_bytes=8 << 20),
+    )(down, basis, *nears)
 
 
 def place(y, x, core):
@@ -245,11 +294,18 @@
     ]
 
 
+OUTWARD = [(i, (i + (1 if i % 2 else -1)) % 32) for i in range(32)]
 SWAP = [(i, i ^ 1) for i in range(32)]
 
 
-def send(value, pairs):
-    return lax.ppermute(value, "clus", pairs)
+def send(value, pairs, name):
+    with jax.named_scope(name):
+        return lax.ppermute(value, "clus", pairs)
+
+
+def trade(value, first, name):
+    with jax.named_scope(name):
+        return lax.ppermute(value, ("clus", "rhs"), partners(first))
 
 
 def joined(*parts):
@@ -271,8 +327,9 @@
     clus, rhs = lax.axis_index("clus"), lax.axis_index("rhs")
     meta = jnp.stack([rhs, clus]).astype(jnp.int32)
     basis = jnp.swapaxes(leaf_basis, 1, 2)
-    halo_before = send(sources, [(i, (i + 1) % 32) for i in range(32)])
-    halo_after = send(sources, [((i + 1) % 32, i) for i in range(32)])
+    half = lax.dynamic_slice_in_dim(sources, (rhs & 1) * 64, 64, 0)
+    far_mine = send(half, OUTWARD, "halo")
+    sibling = send(sources, SWAP, "sibling")
     chunk, leaf_codes, par_codes, near_codes, sources_here, near_here = coefficients(
         meta,
         sources,
@@ -285,32 +342,28 @@
         near_block,
     )
 
-    across = send(chunk, around(2, True))
-    before = send(chunk, around(1, True))
-    after = send(chunk, around(-1, True))
-    before, after, across, halo_before, halo_after = lax.optimization_barrier(
-        (before, after, across, halo_before, halo_after)
-    )
+    across = send(chunk, around(2, True), "across")
+    before = send(chunk, around(1, True), "before")
+    after = send(chunk, around(-1, True), "after")
+    far_other = trade(far_mine, True, "halo_half")
     own = stacked(chunk, before, after, across)
-    side_b = send(own, around(1, False))
-    side_a = send(own, around(-1, False))
+    side_b = send(own, around(1, False), "side_b")
+    side_a = send(own, around(-1, False), "side_a")
     keep, pass_on, give = near_partials(
-        meta, near_codes, sources_here, halo_before, halo_after, near_here
-    )
-    taken = lax.ppermute(give, ("clus", "rhs"), partners(True))
+        meta, near_codes, sources_here, sibling, far_mine, far_other, near_here
+    )
+    taken = trade(give, True, "near_pairs")
     side_b, side_a, pass_on = lax.optimization_barrier((side_b, side_a, pass_on))
     half = own.shape[0] // 2
-    far_b = send(side_b[:half], around(1, False))
-    far_a = send(side_a[half:], around(-1, False))
-    pass_on = (pass_on.astype(F32) + taken[32:].astype(F32)).astype(BF16)
-    passed = lax.ppermute(pass_on, ("clus", "rhs"), partners(False))
-    far_b, far_a, passed = lax.optimization_barrier((far_b, far_a, passed))
-    nears = (keep, taken, passed)
-    sides, far = joined(side_b, side_a), joined(far_b, far_a)
-    held = joined(own, sides, far, send(own, SWAP), send(sides, SWAP), send(far, SWAP))
-    return far_and_sum(
-        leaf_codes, par_codes, held, leaf_coupling, par_coupling, transfer, basis, nears
-    )
+    far_b = send(side_b[:half], around(1, False), "far_b")
+    far_a = send(side_a[half:], around(-1, False), "far_a")
+    pass_on = added(pass_on, taken)
+    far_b, far_a, pass_on = lax.optimization_barrier((far_b, far_a, pass_on))
+    passed = trade(pass_on, False, "near_last")
+    inner, far = joined(own, side_b, side_a), joined(far_b, far_a)
+    held = joined(inner, far, send(inner, SWAP, "swap_inner"), send(far, SWAP, "swap_far"))
+    down = far_down(leaf_codes, par_codes, held, leaf_coupling, par_coupling, transfer)
+    return far_and_sum(down, basis, keep, taken, passed)
 
 
 def solution(mesh):

time: 54.8 us -> 51.4 us (0.938)
  the two profiles are of different devices: /device:TPU:6 before, /device:TPU:24 now
where the time goes in v4:
time: 51.4 us; the launch traced here: 51.3 us
  waiting for transfers between devices  21 us (41%)
  starting transfers between devices  17.8 us (35%)
  Pallas kernels  10.3 us (20%)
  local copies, waits for them, and re-layouts  1.79 us (3%)
    ppermute x11, waiting for transfers between devices, send(): return lax.ppermute(value, 'clus', pairs)  14 us
    ppermute x11, starting transfers between devices, send(): return lax.ppermute(value, 'clus', pairs)  11.2 us
    ppermute x3, waiting for transfers between devices, trade(): return lax.ppermute(value, ('clus', 'rhs'), partners(first))  6.91 us
    ppermute x3, starting transfers between devices, trade(): return lax.ppermute(value, ('clus', 'rhs'), partners(first))  6.62 us
    pallas_call x1, Pallas kernels, far_down(): pl.pallas_call(far_kernel, out_shape=jax.ShapeDtypeStruct((32, 2048), BF1...  3.3 us
    pallas_call x1, Pallas kernels, coefficients(): pl.pallas_call(coef_kernel, out_shape=[pltpu.VMEM((ROWS, 128), BF16)] + [...  3.01 us
    pallas_call x1, Pallas kernels, near_partials(): pl.pallas_call(near_kernel, out_shape=[jax.ShapeDtypeStruct((n, 4096), BF...  2.89 us
    dynamic_slice x1, local copies, waits for them, and re-layouts, per_device(): half = lax.dynamic_slice_in_dim(sources, (rhs & 1) * 64, 64, 0)  1.08 us
  transfers between devices with their start and end apart: 14, of which 10 were waited for; matrix products, arithmetic and copies ran while one was open for 4% of the time, Pallas kernels for 18%

profile of v4, /device:TPU:24, one launch (start us, length us, event | category | flops | bytes accessed | tf_op | source)
XLA Modules:
  0.0 51.3 jit_solution(16780098928110752229)
XLA Ops:
  0.0 1.1 %constant_dynamic-slice_fusion = bf16[64,4096]{1,0:T(8,128)(2,1)S(1)} fusion(bf16[128,4096]{1,0:T(8,128)(2,1)} %refs_0_.1, s32[]{:T(128)S(6)} %select_n.3), kind=kLoop, calls=%fused_computation.10 | loop fusion | bytes 1048580 | tf_op jit(solution)/shard_map/dynamic_slice | solution.py:330
  1.1 3.1 %collective-permute-start.6 = (bf16[64,4096]{1,0:T(8,128)(2,1)S(1)}, bf16[64,4096]{1,0:T(8,128)(2,1)S(1)}, u32[]{:S(2)}, u32[]{:S(2)}) collective-permute-start(bf16[64,4096]{1,0:T(8,128)(2,1)S(1)} %constant_dynamic-slice_fusion), channel_id=1, source_target_pairs={{0,124},{4,8},{8,4},{12,16},{16,12},{20,24},{24,20},{28,32},{32,28... | collective-permute-start | bytes 1572872 | tf_op jit(solution)/shard_map/halo/ppermute | solution.py:303
  4.3 3.0 %shard_map.100 = (bf16[640,128]{1,0:T(8,128)(2,1)S(1)}, s32[8,32]{1,0:T(8,128)S(1)}, s32[8,8]{1,0:T(8,128)S(1)}, s32[2,32]{1,0:T(2,128)S(1)}, bf16[128,4096]{1,0...) custom-call(s32[2]{0:T(128)S(1)} %pad_add_fusion.meta, bf16[128,4096]{1,0:T(8,128)(2,1)} %refs_0_.1, ...), custom_call_target="tpu_custom_call" | custom-call | flops 3000000000 | bytes 10500000 | tf_op jit(solution)/shard_map/pallas_call | solution.py:98
  7.4 3.2 %collective-permute-start.1 = (bf16[640,128]{1,0:T(8,128)(2,1)S(1)}, bf16[640,128]{1,0:T(8,128)(2,1)S(1)}, u32[]{:S(2)}, u32[]{:S(2)}) collective-permute-start(bf16[640,128]{1,0:T(8,128)(2,1)S(1)} %get-tuple-element.22.refs_0_), channel_id=1, source_target_pairs={{0,24},{4,100},{8,0},{12,108},{16,8},{20,116},{24,16},{28,124},{32... | collective-permute-start | bytes 491528 | tf_op jit(solution)/shard_map/after/ppermute | solution.py:303
  10.6 1.4 %collective-permute-done.6.far_mine = bf16[64,4096]{1,0:T(8,128)(2,1)S(1)} collective-permute-done((bf16[64,4096]{1,0:T(8,128)(2,1)S(1)}, bf16[64,4096]{1,0:T(8,128)(2,1)S(1)}, u32[]{:S(2)}, u32[]{:S(2)}) %collective-permute-start.6) | collective-permute-done | bytes 524320 | tf_op jit(solution)/shard_map/halo/ppermute | solution.py:303
  12.0 1.9 %collective-permute-start.7 = (bf16[64,4096]{1,0:T(8,128)(2,1)S(1)}, bf16[64,4096]{1,0:T(8,128)(2,1)S(1)}, u32[]{:S(2)}, u32[]{:S(2)}) collective-permute-start(bf16[64,4096]{1,0:T(8,128)(2,1)S(1)} %collective-permute-done.6.far_mine), channel_id=1, source_target_pairs={{0,1},{1,0},{2,3},{3,2},{4,7},{5,6},{6,5},{7,4},{8,9},{9,8},{10,11... | collective-permute-start | bytes 1572872 | tf_op jit(solution)/shard_map/halo_half/ppermute | solution.py:308
  13.9 1.3 %collective-permute-done.1.refs_2_ = bf16[640,128]{1,0:T(8,128)(2,1)S(1)} collective-permute-done((bf16[640,128]{1,0:T(8,128)(2,1)S(1)}, bf16[640,128]{1,0:T(8,128)(2,1)S(1)}, u32[]{:S(2)}, u32[]{:S(2)}) %collective-permute-start.1) | collective-permute-done | bytes 163872 | tf_op jit(solution)/shard_map/after/ppermute | solution.py:303
  15.2 2.2 %collective-permute-done.2.refs_3_ = bf16[640,128]{1,0:T(8,128)(2,1)S(1)} collective-permute-done((bf16[640,128]{1,0:T(8,128)(2,1)S(1)}, bf16[640,128]{1,0:T(8,128)(2,1)S(1)}, u32[]{:S(2)}, u32[]{:S(2)}) %collective-permute-start.2) | collective-permute-done | bytes 163872 | tf_op jit(solution)/shard_map/across/ppermute | solution.py:303
  17.5 2.6 %collective-permute-start.3 = (bf16[2560,128]{1,0:T(8,128)(2,1)S(1)}, bf16[2560,128]{1,0:T(8,128)(2,1)S(1)}, u32[]{:S(2)}, u32[]{:S(2)}) collective-permute-start(bf16[2560,128]{1,0:T(8,128)(2,1)S(1)} %shard_map.101), channel_id=1, source_target_pairs={{0,32},{4,12},{8,40},{12,20},{16,48},{20,28},{24,56},{28,4},{32,64... | collective-permute-start | bytes 1966088 | tf_op jit(solution)/shard_map/side_b/ppermute | solution.py:303
  20.1 1.1 %collective-permute-done.7.far_other = bf16[64,4096]{1,0:T(8,128)(2,1)S(1)} collective-permute-done((bf16[64,4096]{1,0:T(8,128)(2,1)S(1)}, bf16[64,4096]{1,0:T(8,128)(2,1)S(1)}, u32[]{:S(2)}, u32[]{:S(2)}) %collective-permute-start.7) | collective-permute-done | bytes 524320 | tf_op jit(solution)/shard_map/halo_half/ppermute | solution.py:308
  21.2 2.9 %shard_map.102 = (bf16[32,4096]{1,0:T(8,128)(2,1)S(1)}, bf16[32,4096]{1,0:T(8,128)(2,1)S(1)}, bf16[64,4096]{1,0:T(8,128)(2,1)S(1)}) custom-call(s32[2]{0:T(128)S(1)} %pad_add_fusion.meta, s32[2,32]{1,0:T(2,128)S(1)} %get-tuple-element.23.near_codes, bf16[128,4096]{1,0:T(8,128)(2,1)S(1)} %get-tuple-element.24.own, ...), custom_call_target="tpu_custom_call" | custom-call | flops 3000000000 | bytes 10500000 | tf_op jit(solution)/shard_map/pallas_call | solution.py:179
  24.1 4.1 %collective-permute-done.3 = bf16[2560,128]{1,0:T(8,128)(2,1)S(1)} collective-permute-done((bf16[2560,128]{1,0:T(8,128)(2,1)S(1)}, bf16[2560,128]{1,0:T(8,128)(2,1)S(1)}, u32[]{:S(2)}, u32[]{:S(2)}) %collective-permute-start.3) | collective-permute-done | bytes 655392 | tf_op jit(solution)/shard_map/side_b/ppermute | solution.py:303
  28.1 3.7 %collective-permute-done.4 = bf16[2560,128]{1,0:T(8,128)(2,1)S(1)} collective-permute-done((bf16[2560,128]{1,0:T(8,128)(2,1)S(1)}, bf16[2560,128]{1,0:T(8,128)(2,1)S(1)}, u32[]{:S(2)}, u32[]{:S(2)}) %collective-permute-start.4) | collective-permute-done | bytes 655392 | tf_op jit(solution)/shard_map/side_a/ppermute | solution.py:303
  31.8 1.9 %collective-permute-start.10 = (bf16[64,4096]{1,0:T(8,128)(2,1)S(1)}, bf16[64,4096]{1,0:T(8,128)(2,1)S(1)}, u32[]{:S(2)}, u32[]{:S(2)}) collective-permute-start(bf16[64,4096]{1,0:T(8,128)(2,1)S(1)} %get-tuple-element.30), channel_id=1, source_target_pairs={{0,1},{1,0},{2,3},{3,2},{4,7},{5,6},{6,5},{7,4},{8,9},{9,8},{10,11... | collective-permute-start | bytes 1572872 | tf_op jit(solution)/shard_map/near_pairs/ppermute | solution.py:308
  33.8 0.1 pad_maximum_fusion
  33.9 0.1 constant_dynamic-update-slice_fusion.5
  34.1 2.0 %collective-permute-start.9 = (bf16[1280,128]{1,0:T(8,128)(2,1)S(1)}, bf16[1280,128]{1,0:T(8,128)(2,1)S(1)}, u32[]{:S(2)}, u32[]{:S(2)}) collective-permute-start(bf16[1280,128]{1,0:T(8,128)(2,1)S(1)} %slice.7), channel_id=1, source_target_pairs={{0,96},{4,28},{8,104},{12,4},{16,112},{20,12},{24,120},{28,20},{32... | collective-permute-start | bytes 983048 | tf_op jit(solution)/shard_map/far_a/ppermute | solution.py:303
  36.2 4.8 %collective-permute-done.10.taken = bf16[64,4096]{1,0:T(8,128)(2,1)S(1)} collective-permute-done((bf16[64,4096]{1,0:T(8,128)(2,1)S(1)}, bf16[64,4096]{1,0:T(8,128)(2,1)S(1)}, u32[]{:S(2)}, u32[]{:S(2)}) %collective-permute-start.10) | collective-permute-done | bytes 524320 | tf_op jit(solution)/shard_map/near_pairs/ppermute | solution.py:308
  41.2 1.3 %collective-permute-done.9 = bf16[1280,128]{1,0:T(8,128)(2,1)S(1)} collective-permute-done((bf16[1280,128]{1,0:T(8,128)(2,1)S(1)}, bf16[1280,128]{1,0:T(8,128)(2,1)S(1)}, u32[]{:S(2)}, u32[]{:S(2)}) %collective-permute-start.9) | collective-permute-done | bytes 327712 | tf_op jit(solution)/shard_map/far_a/ppermute | solution.py:303
  42.6 2.8 %collective-permute-start.13 = (bf16[32,4096]{1,0:T(8,128)(2,1)S(1)}, bf16[32,4096]{1,0:T(8,128)(2,1)S(1)}, u32[]{:S(2)}, u32[]{:S(2)}) collective-permute-start(bf16[32,4096]{1,0:T(8,128)(2,1)S(1)} %shard_map.103), channel_id=1, source_target_pairs={{0,3},{1,2},{2,1},{3,0},{4,5},{5,4},{6,7},{7,6},{8,11},{9,10},{10,... | collective-permute-start | bytes 786440 | tf_op jit(solution)/shard_map/near_last/ppermute | solution.py:308
  45.5 0.3 constant_dynamic-update-slice_fusion.1
  45.9 3.3 %shard_map.104.down = bf16[32,2048]{1,0:T(8,128)(2,1)S(1)} custom-call(s32[8,32]{1,0:T(8,128)S(1)} %get-tuple-element.20.leaf_codes, s32[8,8]{1,0:T(8,128)S(1)} %get-tuple-element.21.par_codes, bf16[20480,128]{1,0:T(8,128)(2,1)S(1)} %constant_dynamic-update-slice_fusion.held, bf16[32,8,64,64]{3,2,1,0:T(8,128)(2,1)S(1)} %copy-done, ...), custom_call_target="tpu_custom_call" | custom-call | flops 3000000000 | bytes 10500000 | tf_op jit(solution)/shard_map/pallas_call | solution.py:243
  49.2 1.1 %collective-permute-done.13.passed = bf16[32,4096]{1,0:T(8,128)(2,1)S(1)} collective-permute-done((bf16[32,4096]{1,0:T(8,128)(2,1)S(1)}, bf16[32,4096]{1,0:T(8,128)(2,1)S(1)}, u32[]{:S(2)}, u32[]{:S(2)}) %collective-permute-start.13) | collective-permute-done | bytes 262176 | tf_op jit(solution)/shard_map/near_last/ppermute | solution.py:308
  50.3 1.0 %shard_map.105 = bf16[32,4096]{1,0:T(8,128)(2,1)} custom-call(bf16[32,2048]{1,0:T(8,128)(2,1)S(1)} %shard_map.104.down, bf16[32,64,128]{2,1,0:T(8,128)(2,1)S(1)} %bitcast.7, bf16[32,4096]{1,0:T(8,128)(2,1)S(1)} %get-tuple-element.33.keep, bf16[64,4096]{1,0:T(8,128)(2,1)S(1)} %collective-permute-done.10.taken, bf16[32,4096]{1,0:T(8,128)(2,1)S(1)} %collective-permute-done.13.passed), custom_call_target="tpu_custom_call" | custom-call | tf_op jit(solution)/shard_map/pallas_call | solution.py:265
  (31 shorter events, 0.9 us)
Async XLA Ops:
  0.0 20.1 %collective-permute-start.5 = (bf16[128,4096]{1,0:T(8,128)(2,1)}, bf16[128,4096]{1,0:T(8,128)(2,1)S(1)}, u32[]{:S(2)}, u32[]{:S(2)}) collective-permute-start(bf16[128,4096]{1,0:T(8,128)(2,1)} %refs_0_.1), channel_id=1, source_target_pairs={{0,4},{4,0},{8,12},{12,8},{16,20},{20,16},{24,28},{28,24},{32,36},... | collective-permute-start | bytes 3145736 | tf_op jit(solution)/shard_map/sibling/ppermute | solution.py:303
  1.1 10.9 %collective-permute-start.6 = (bf16[64,4096]{1,0:T(8,128)(2,1)S(1)}, bf16[64,4096]{1,0:T(8,128)(2,1)S(1)}, u32[]{:S(2)}, u32[]{:S(2)}) collective-permute-start(bf16[64,4096]{1,0:T(8,128)(2,1)S(1)} %constant_dynamic-slice_fusion), channel_id=1, source_target_pairs={{0,124},{4,8},{8,4},{12,16},{16,12},{20,24},{24,20},{28,32},{32,28... | collective-permute-start | bytes 1572872 | tf_op jit(solution)/shard_map/halo/ppermute | solution.py:303
  7.3 6.6 %collective-permute-start = (bf16[640,128]{1,0:T(8,128)(2,1)S(1)}, bf16[640,128]{1,0:T(8,128)(2,1)S(1)}, u32[]{:S(2)}, u32[]{:S(2)}) collective-permute-start(bf16[640,128]{1,0:T(8,128)(2,1)S(1)} %get-tuple-element.22.refs_0_), channel_id=1, source_target_pairs={{0,8},{4,36},{8,16},{12,44},{16,24},{20,52},{24,0},{28,60},{32,40}... | collective-permute-start | bytes 491528 | tf_op jit(solution)/shard_map/before/ppermute | solution.py:303
  7.4 7.8 %collective-permute-start.1 = (bf16[640,128]{1,0:T(8,128)(2,1)S(1)}, bf16[640,128]{1,0:T(8,128)(2,1)S(1)}, u32[]{:S(2)}, u32[]{:S(2)}) collective-permute-start(bf16[640,128]{1,0:T(8,128)(2,1)S(1)} %get-tuple-element.22.refs_0_), channel_id=1, source_target_pairs={{0,24},{4,100},{8,0},{12,108},{16,8},{20,116},{24,16},{28,124},{32... | collective-permute-start | bytes 491528 | tf_op jit(solution)/shard_map/after/ppermute | solution.py:303
  10.6 6.8 %collective-permute-start.2 = (bf16[640,128]{1,0:T(8,128)(2,1)S(1)}, bf16[640,128]{1,0:T(8,128)(2,1)S(1)}, u32[]{:S(2)}, u32[]{:S(2)}) collective-permute-start(bf16[640,128]{1,0:T(8,128)(2,1)S(1)} %get-tuple-element.22.refs_0_), channel_id=1, source_target_pairs={{0,16},{4,68},{8,24},{12,76},{16,0},{20,84},{24,8},{28,92},{32,48}... | collective-permute-start | bytes 491528 | tf_op jit(solution)/shard_map/across/ppermute | solution.py:303
  12.0 9.2 %collective-permute-start.7 = (bf16[64,4096]{1,0:T(8,128)(2,1)S(1)}, bf16[64,4096]{1,0:T(8,128)(2,1)S(1)}, u32[]{:S(2)}, u32[]{:S(2)}) collective-permute-start(bf16[64,4096]{1,0:T(8,128)(2,1)S(1)} %collective-permute-done.6.far_mine), channel_id=1, source_target_pairs={{0,1},{1,0},{2,3},{3,2},{4,7},{5,6},{6,5},{7,4},{8,9},{9,8},{10,11... | collective-permute-start | bytes 1572872 | tf_op jit(solution)/shard_map/halo_half/ppermute | solution.py:308
  17.5 10.7 %collective-permute-start.3 = (bf16[2560,128]{1,0:T(8,128)(2,1)S(1)}, bf16[2560,128]{1,0:T(8,128)(2,1)S(1)}, u32[]{:S(2)}, u32[]{:S(2)}) collective-permute-start(bf16[2560,128]{1,0:T(8,128)(2,1)S(1)} %shard_map.101), channel_id=1, source_target_pairs={{0,32},{4,12},{8,40},{12,20},{16,48},{20,28},{24,56},{28,4},{32,64... | collective-permute-start | bytes 1966088 | tf_op jit(solution)/shard_map/side_b/ppermute | solution.py:303
  20.0 11.8 %collective-permute-start.4 = (bf16[2560,128]{1,0:T(8,128)(2,1)S(1)}, bf16[2560,128]{1,0:T(8,128)(2,1)S(1)}, u32[]{:S(2)}, u32[]{:S(2)}) collective-permute-start(bf16[2560,128]{1,0:T(8,128)(2,1)S(1)} %shard_map.101), channel_id=1, source_target_pairs={{0,96},{4,28},{8,104},{12,4},{16,112},{20,12},{24,120},{28,20},{32... | collective-permute-start | bytes 1966088 | tf_op jit(solution)/shard_map/side_a/ppermute | solution.py:303
  31.8 9.2 %collective-permute-start.10 = (bf16[64,4096]{1,0:T(8,128)(2,1)S(1)}, bf16[64,4096]{1,0:T(8,128)(2,1)S(1)}, u32[]{:S(2)}, u32[]{:S(2)}) collective-permute-start(bf16[64,4096]{1,0:T(8,128)(2,1)S(1)} %get-tuple-element.30), channel_id=1, source_target_pairs={{0,1},{1,0},{2,3},{3,2},{4,7},{5,6},{6,5},{7,4},{8,9},{9,8},{10,11... | collective-permute-start | bytes 1572872 | tf_op jit(solution)/shard_map/near_pairs/ppermute | solution.py:308
  34.0 7.1 %collective-permute-start.8 = (bf16[1280,128]{1,0:T(8,128)(2,1)S(1)}, bf16[1280,128]{1,0:T(8,128)(2,1)S(1)}, u32[]{:S(2)}, u32[]{:S(2)}) collective-permute-start(bf16[1280,128]{1,0:T(8,128)(2,1)S(1)} %slice.6), channel_id=1, source_target_pairs={{0,32},{4,12},{8,40},{12,20},{16,48},{20,28},{24,56},{28,4},{32,64... | collective-permute-start | bytes 983048 | tf_op jit(solution)/shard_map/far_b/ppermute | solution.py:303
  34.1 8.4 %collective-permute-start.9 = (bf16[1280,128]{1,0:T(8,128)(2,1)S(1)}, bf16[1280,128]{1,0:T(8,128)(2,1)S(1)}, u32[]{:S(2)}, u32[]{:S(2)}) collective-permute-start(bf16[1280,128]{1,0:T(8,128)(2,1)S(1)} %slice.7), channel_id=1, source_target_pairs={{0,96},{4,28},{8,104},{12,4},{16,112},{20,12},{24,120},{28,20},{32... | collective-permute-start | bytes 983048 | tf_op jit(solution)/shard_map/far_a/ppermute | solution.py:303
  36.1 9.4 %collective-permute-start.11 = (bf16[7680,128]{1,0:T(8,128)(2,1)S(1)}, bf16[7680,128]{1,0:T(8,128)(2,1)S(1)}, u32[]{:S(2)}, u32[]{:S(2)}) collective-permute-start(bf16[7680,128]{1,0:T(8,128)(2,1)S(1)} %pad_maximum_fusion), channel_id=1, source_target_pairs={{0,4},{4,0},{8,12},{12,8},{16,20},{20,16},{24,28},{28,24},{32,36},... | collective-permute-start | bytes 5898248 | tf_op jit(solution)/shard_map/swap_inner/ppermute | solution.py:303
  41.1 4.8 %copy-start = (bf16[32,8,64,64]{3,2,1,0:T(8,128)(2,1)S(1)}, bf16[32,8,64,64]{3,2,1,0:T(8,128)(2,1)}, u32[]{:S(2)}) copy-start(bf16[32,8,64,64]{3,2,1,0:T(8,128)(2,1)} %coupling.1) | copy-start | bytes 6291460
  41.1 4.8 %copy-start.1 = (bf16[8,8,64,64]{3,2,1,0:T(8,128)(2,1)S(1)}, bf16[8,8,64,64]{3,2,1,0:T(8,128)(2,1)}, u32[]{:S(2)}) copy-start(bf16[8,8,64,64]{3,2,1,0:T(8,128)(2,1)} %par_coupling.1) | copy-start | bytes 1572868
  41.1 4.8 %copy-start.2 = (bf16[32,64,64]{2,1,0:T(8,128)(2,1)S(1)}, bf16[32,64,64]{2,1,0:T(8,128)(2,1)}, u32[]{:S(2)}) copy-start(bf16[32,64,64]{2,1,0:T(8,128)(2,1)} %transfer.1) | copy-start | bytes 786436
  42.5 3.3 %collective-permute-start.12 = (bf16[2560,128]{1,0:T(8,128)(2,1)S(1)}, bf16[2560,128]{1,0:T(8,128)(2,1)S(1)}, u32[]{:S(2)}, u32[]{:S(2)}) collective-permute-start(bf16[2560,128]{1,0:T(8,128)(2,1)S(1)} %pad_maximum_fusion.1), channel_id=1, source_target_pairs={{0,4},{4,0},{8,12},{12,8},{16,20},{20,16},{24,28},{28,24},{32,36},... | collective-permute-start | bytes 1966088 | tf_op jit(solution)/shard_map/swap_far/ppermute | solution.py:303
  42.6 7.7 %collective-permute-start.13 = (bf16[32,4096]{1,0:T(8,128)(2,1)S(1)}, bf16[32,4096]{1,0:T(8,128)(2,1)S(1)}, u32[]{:S(2)}, u32[]{:S(2)}) collective-permute-start(bf16[32,4096]{1,0:T(8,128)(2,1)S(1)} %shard_map.103), channel_id=1, source_target_pairs={{0,3},{1,2},{2,1},{3,0},{4,5},{5,4},{6,7},{7,6},{8,11},{9,10},{10,... | collective-permute-start | bytes 786440 | tf_op jit(solution)/shard_map/near_last/ppermute | solution.py:308
  45.9 4.4 %copy-start.3 = (bf16[32,128,64]{1,2,0:T(8,128)(2,1)S(1)}, bf16[32,128,64]{1,2,0:T(8,128)(2,1)}, u32[]{:S(2)}) copy-start(bf16[32,128,64]{1,2,0:T(8,128)(2,1)} %param.11) | copy-start | bytes 1572868

commit v5 on v4

--- a/solution.py
+++ b/solution.py
@@ -11,12 +11,14 @@
 PARENTS = 8
 ROWS = 640
 SIDE = 4
-COEF_US, STACK_US, NEAR_US, FAR_US, ADD_US = 3, 0, 3, 3, 10
+COEF_US, STACK_US, NEAR_US, FAR_US, ADD_US = 3, 4, 3, 0, 3
+SIDE_STEP, FAR_STEP = 4 * ROWS, ROWS
 NT = (((1,), (1,)), ((), ()))
 
 
 def cost(us):
-    return pl.CostEstimate(flops=us * 10**9, bytes_accessed=us * 35 * 10**5, transcendentals=0)
+    work = int(us * 10**6)
+    return pl.CostEstimate(flops=1000 * work, bytes_accessed=3 * work, transcendentals=0)
 
 
 def dot_nt(a, b):
@@ -117,21 +119,26 @@
     )(meta, *(pltpu.with_memory_space_constraint(array, pltpu.HBM) for array in arrays))
 
 
+def fill(out, parts):
+    start = 0
+    for part in parts:
+        out[start : start + part.shape[0], :] = part[...]
+        start += part.shape[0]
+
+
 def stack_kernel(*refs):
-    out = refs[-1]
-    for k, part in enumerate(refs[:-1]):
-        out[ROWS * k : ROWS * (k + 1), :] = part[...]
-
-
-def stacked(*parts):
+    fill(refs[-1], refs[:-1])
+
+
+def stacked(*parts, us=0):
     vmem = pl.BlockSpec(memory_space=pltpu.VMEM)
     return pl.pallas_call(
         stack_kernel,
-        out_shape=pltpu.VMEM((ROWS * len(parts), 128), BF16),
+        out_shape=pltpu.VMEM((sum(part.shape[0] for part in parts), 128), BF16),
         in_specs=[vmem] * len(parts),
         out_specs=vmem,
-        cost_estimate=cost(STACK_US),
-        compiler_params=pltpu.CompilerParams(vmem_limit_bytes=4 << 20),
+        cost_estimate=cost(us),
+        compiler_params=pltpu.CompilerParams(vmem_limit_bytes=6 << 20),
     )(*(pltpu.with_memory_space_constraint(part, pltpu.VMEM) for part in parts))
 
 
@@ -203,7 +210,9 @@
     )(mine, taken)
 
 
-def far_kernel(leaf_codes, par_codes, held, coupling, par_coupling, transfer, out):
+def far_kernel(leaf_codes, par_codes, *refs):
+    coupling, par_coupling, transfer, out, held = refs[-5:]
+    fill(held, refs[:-5])
     lane = lax.broadcasted_iota(jnp.int32, (1, 128), 1)
     low = (lane < 64).astype(F32).astype(BF16)
     high = (lane >= 64).astype(F32).astype(BF16)
@@ -237,17 +246,19 @@
     lax.fori_loop(0, PARENTS, body, 0, unroll=True)
 
 
-def far_down(leaf_codes, par_codes, held, coupling, par_coupling, transfer):
+def far_down(leaf_codes, par_codes, gathered, coupling, par_coupling, transfer):
     smem = pl.BlockSpec(memory_space=pltpu.SMEM)
     vmem = pl.BlockSpec(memory_space=pltpu.VMEM)
+    gathered = [pltpu.with_memory_space_constraint(part, pltpu.VMEM) for part in gathered]
     return pl.pallas_call(
         far_kernel,
         out_shape=jax.ShapeDtypeStruct((32, 2048), BF16),
-        in_specs=[smem] * 2 + [vmem] * 4,
+        in_specs=[smem] * 2 + [vmem] * (len(gathered) + 3),
         out_specs=vmem,
+        scratch_shapes=[pltpu.VMEM((32 * ROWS, 128), BF16)],
         cost_estimate=cost(FAR_US),
-        compiler_params=pltpu.CompilerParams(vmem_limit_bytes=18 << 20),
-    )(leaf_codes, par_codes, held, coupling, par_coupling, transfer)
+        compiler_params=pltpu.CompilerParams(vmem_limit_bytes=22 << 20),
+    )(leaf_codes, par_codes, *gathered, coupling, par_coupling, transfer)
 
 
 def sum_kernel(down, basis, keep, taken, passed, out):
@@ -306,10 +317,6 @@
 def trade(value, first, name):
     with jax.named_scope(name):
         return lax.ppermute(value, ("clus", "rhs"), partners(first))
-
-
-def joined(*parts):
-    return jnp.concatenate(parts, axis=0)
 
 
 def per_device(
@@ -346,23 +353,32 @@
     before = send(chunk, around(1, True), "before")
     after = send(chunk, around(-1, True), "after")
     far_other = trade(far_mine, True, "halo_half")
-    own = stacked(chunk, before, after, across)
+    own = stacked(chunk, before, after, across, us=STACK_US)
     side_b = send(own, around(1, False), "side_b")
     side_a = send(own, around(-1, False), "side_a")
     keep, pass_on, give = near_partials(
         meta, near_codes, sources_here, sibling, far_mine, far_other, near_here
     )
     taken = trade(give, True, "near_pairs")
-    side_b, side_a, pass_on = lax.optimization_barrier((side_b, side_a, pass_on))
+    own_other = send(own, SWAP, "swap_own")
+    side_b, side_a, pass_on, own_other = lax.optimization_barrier(
+        (side_b, side_a, pass_on, own_other)
+    )
     half = own.shape[0] // 2
     far_b = send(side_b[:half], around(1, False), "far_b")
     far_a = send(side_a[half:], around(-1, False), "far_a")
     pass_on = added(pass_on, taken)
+    passed = trade(pass_on, False, "near_last")
     far_b, far_a, pass_on = lax.optimization_barrier((far_b, far_a, pass_on))
-    passed = trade(pass_on, False, "near_last")
-    inner, far = joined(own, side_b, side_a), joined(far_b, far_a)
-    held = joined(inner, far, send(inner, SWAP, "swap_inner"), send(far, SWAP, "swap_far"))
-    down = far_down(leaf_codes, par_codes, held, leaf_coupling, par_coupling, transfer)
+    def swapped(name, *parts, step):
+        pieces = [part[k : k + step] for part in parts for k in range(0, part.shape[0], step)]
+        return tuple(send(piece, SWAP, name) for piece in pieces)
+
+    mine = (own, side_b, side_a, far_b, far_a)
+    inner = (own_other,) + swapped("swap_side", side_b, side_a, step=SIDE_STEP)
+    outer = swapped("swap_far", far_b, far_a, step=FAR_STEP)
+    gathered = mine + inner + outer
+    down = far_down(leaf_codes, par_codes, gathered, leaf_coupling, par_coupling, transfer)
     return far_and_sum(down, basis, keep, taken, passed)
 
 

time: 51.4 us -> 50.4 us (0.981)
  the two profiles are of different devices: /device:TPU:24 before, /device:TPU:6 now
where the time goes in v5:
time: 50.4 us; the launch traced here: 49.8 us
  waiting for transfers between devices  19 us (38%)
  starting transfers between devices  18.7 us (37%)
  Pallas kernels  10.6 us (21%)
  local copies, waits for them, and re-layouts  1.19 us (2%)
    ppermute x16, waiting for transfers between devices, send(): return lax.ppermute(value, 'clus', pairs)  19 us
    ppermute x16, starting transfers between devices, send(): return lax.ppermute(value, 'clus', pairs)  15.4 us
    pallas_call x1, Pallas kernels, far_down(): pl.pallas_call(far_kernel, out_shape=jax.ShapeDtypeStruct((32, 2048), BF1...  3.65 us
    ppermute x3, starting transfers between devices, trade(): return lax.ppermute(value, ('clus', 'rhs'), partners(first))  3.26 us
    pallas_call x1, Pallas kernels, coefficients(): pl.pallas_call(coef_kernel, out_shape=[pltpu.VMEM((ROWS, 128), BF16)] + [...  3.01 us
    pallas_call x1, Pallas kernels, near_partials(): pl.pallas_call(near_kernel, out_shape=[jax.ShapeDtypeStruct((n, 4096), BF...  2.89 us
    dynamic_slice x1, local copies, waits for them, and re-layouts, per_device(): half = lax.dynamic_slice_in_dim(sources, (rhs & 1) * 64, 64, 0)  1.08 us
  transfers between devices with their start and end apart: 19, of which 10 were waited for; matrix products, arithmetic and copies ran while one was open for 0% of the time, Pallas kernels for 19%

profile of v5, /device:TPU:6, one launch (start us, length us, event | category | flops | bytes accessed | tf_op | source)
XLA Modules:
  0.0 49.8 jit_solution(11794882713380805689)
XLA Ops:
  0.0 1.1 %constant_dynamic-slice_fusion = bf16[64,4096]{1,0:T(8,128)(2,1)S(1)} fusion(bf16[128,4096]{1,0:T(8,128)(2,1)} %refs_0_.1, s32[]{:T(128)S(6)} %select_n.3), kind=kLoop, calls=%fused_computation.1 | loop fusion | bytes 1048580 | tf_op jit(solution)/shard_map/dynamic_slice | solution.py:337
  1.1 0.3 collective-permute-start.6
  1.4 1.3 %collective-permute-start.5 = (bf16[128,4096]{1,0:T(8,128)(2,1)}, bf16[128,4096]{1,0:T(8,128)(2,1)S(1)}, u32[]{:S(2)}, u32[]{:S(2)}) collective-permute-start(bf16[128,4096]{1,0:T(8,128)(2,1)} %refs_0_.1), channel_id=1, source_target_pairs={{0,4},{4,0},{8,12},{12,8},{16,20},{20,16},{24,28},{28,24},{32,36},... | collective-permute-start | bytes 3145736 | tf_op jit(solution)/shard_map/sibling/ppermute | solution.py:314
  2.8 3.0 %shard_map.100 = (bf16[640,128]{1,0:T(8,128)(2,1)S(1)}, s32[8,32]{1,0:T(8,128)S(1)}, s32[8,8]{1,0:T(8,128)S(1)}, s32[2,32]{1,0:T(2,128)S(1)}, bf16[128,4096]{1,0...) custom-call(s32[2]{0:T(128)S(1)} %pad_add_fusion.meta, bf16[128,4096]{1,0:T(8,128)(2,1)} %refs_0_.1, ...), custom_call_target="tpu_custom_call" | custom-call | flops 3000000000 | bytes 9000000 | tf_op jit(solution)/shard_map/pallas_call | solution.py:100
  5.9 1.5 %collective-permute-start.2 = (bf16[640,128]{1,0:T(8,128)(2,1)S(1)}, bf16[640,128]{1,0:T(8,128)(2,1)S(1)}, u32[]{:S(2)}, u32[]{:S(2)}) collective-permute-start(bf16[640,128]{1,0:T(8,128)(2,1)S(1)} %get-tuple-element.22.refs_0_), channel_id=1, source_target_pairs={{0,16},{4,68},{8,24},{12,76},{16,0},{20,84},{24,8},{28,92},{32,48}... | collective-permute-start | bytes 491528 | tf_op jit(solution)/shard_map/across/ppermute | solution.py:314
  7.3 3.0 %collective-permute-start.1 = (bf16[640,128]{1,0:T(8,128)(2,1)S(1)}, bf16[640,128]{1,0:T(8,128)(2,1)S(1)}, u32[]{:S(2)}, u32[]{:S(2)}) collective-permute-start(bf16[640,128]{1,0:T(8,128)(2,1)S(1)} %get-tuple-element.22.refs_0_), channel_id=1, source_target_pairs={{0,24},{4,100},{8,0},{12,108},{16,8},{20,116},{24,16},{28,124},{32... | collective-permute-start | bytes 491528 | tf_op jit(solution)/shard_map/after/ppermute | solution.py:314
  10.3 0.3 collective-permute-start
  10.6 1.9 %collective-permute-start.7 = (bf16[64,4096]{1,0:T(8,128)(2,1)S(1)}, bf16[64,4096]{1,0:T(8,128)(2,1)S(1)}, u32[]{:S(2)}, u32[]{:S(2)}) collective-permute-start(bf16[64,4096]{1,0:T(8,128)(2,1)S(1)} %collective-permute-done.6.far_mine), channel_id=1, source_target_pairs={{0,1},{1,0},{2,3},{3,2},{4,7},{5,6},{6,5},{7,4},{8,9},{9,8},{10,11... | collective-permute-start | bytes 1572872 | tf_op jit(solution)/shard_map/halo_half/ppermute | solution.py:319
  12.5 0.4 collective-permute-done.2.refs_3_
  12.9 4.3 %collective-permute-done.1.refs_2_ = bf16[640,128]{1,0:T(8,128)(2,1)S(1)} collective-permute-done((bf16[640,128]{1,0:T(8,128)(2,1)S(1)}, bf16[640,128]{1,0:T(8,128)(2,1)S(1)}, u32[]{:S(2)}, u32[]{:S(2)}) %collective-permute-start.1) | collective-permute-done | bytes 163872 | tf_op jit(solution)/shard_map/after/ppermute | solution.py:314
  17.3 5.2 %collective-permute-start.4 = (bf16[2560,128]{1,0:T(8,128)(2,1)S(1)}, bf16[2560,128]{1,0:T(8,128)(2,1)S(1)}, u32[]{:S(2)}, u32[]{:S(2)}) collective-permute-start(bf16[2560,128]{1,0:T(8,128)(2,1)S(1)} %shard_map.101.refs_0_), channel_id=1, source_target_pairs={{0,96},{4,28},{8,104},{12,4},{16,112},{20,12},{24,120},{28,20},{32... | collective-permute-start | bytes 1966088 | tf_op jit(solution)/shard_map/side_a/ppermute | solution.py:314
  22.5 2.9 %shard_map.102 = (bf16[32,4096]{1,0:T(8,128)(2,1)S(1)}, bf16[32,4096]{1,0:T(8,128)(2,1)S(1)}, bf16[64,4096]{1,0:T(8,128)(2,1)S(1)}) custom-call(s32[2]{0:T(128)S(1)} %pad_add_fusion.meta, s32[2,32]{1,0:T(2,128)S(1)} %get-tuple-element.23.near_codes, bf16[128,4096]{1,0:T(8,128)(2,1)S(1)} %get-tuple-element.24.own, ...), custom_call_target="tpu_custom_call" | custom-call | flops 3000000000 | bytes 9000000 | tf_op jit(solution)/shard_map/pallas_call | solution.py:186
  25.4 5.1 %collective-permute-done.4.refs_2_ = bf16[2560,128]{1,0:T(8,128)(2,1)S(1)} collective-permute-done((bf16[2560,128]{1,0:T(8,128)(2,1)S(1)}, bf16[2560,128]{1,0:T(8,128)(2,1)S(1)}, u32[]{:S(2)}, u32[]{:S(2)}) %collective-permute-start.4) | collective-permute-done | bytes 655392 | tf_op jit(solution)/shard_map/side_a/ppermute | solution.py:314
  30.5 3.7 %collective-permute-done.3.refs_1_ = bf16[2560,128]{1,0:T(8,128)(2,1)S(1)} collective-permute-done((bf16[2560,128]{1,0:T(8,128)(2,1)S(1)}, bf16[2560,128]{1,0:T(8,128)(2,1)S(1)}, u32[]{:S(2)}, u32[]{:S(2)}) %collective-permute-start.3) | collective-permute-done | bytes 655392 | tf_op jit(solution)/shard_map/side_b/ppermute | solution.py:314
  34.4 2.0 %collective-permute-start.9 = (bf16[1280,128]{1,0:T(8,128)(2,1)S(1)}, bf16[1280,128]{1,0:T(8,128)(2,1)S(1)}, u32[]{:S(2)}, u32[]{:S(2)}) collective-permute-start(bf16[1280,128]{1,0:T(8,128)(2,1)S(1)} %slice.18), channel_id=1, source_target_pairs={{0,32},{4,12},{8,40},{12,20},{16,48},{20,28},{24,56},{28,4},{32,64... | collective-permute-start | bytes 983048 | tf_op jit(solution)/shard_map/far_b/ppermute | solution.py:314
  36.4 0.5 %collective-permute-start.13 = (bf16[2560,128]{1,0:T(8,128)(2,1)S(1)}, bf16[2560,128]{1,0:T(8,128)(2,1)S(1)}, u32[]{:S(2)}, u32[]{:S(2)}) collective-permute-start(bf16[2560,128]{1,0:T(8,128)(2,1)S(1)} %collective-permute-done.4.refs_2_), channel_id=1, source_target_pairs={{0,4},{4,0},{8,12},{12,8},{16,20},{20,16},{24,28},{28,24},{32,36},... | collective-permute-start | bytes 1966088 | tf_op jit(solution)/shard_map/swap_side/ppermute | solution.py:314
  37.0 1.3 %collective-permute-start.18 = (bf16[32,4096]{1,0:T(8,128)(2,1)S(1)}, bf16[32,4096]{1,0:T(8,128)(2,1)S(1)}, u32[]{:S(2)}, u32[]{:S(2)}) collective-permute-start(bf16[32,4096]{1,0:T(8,128)(2,1)S(1)} %shard_map.103), channel_id=1, source_target_pairs={{0,3},{1,2},{2,1},{3,0},{4,5},{5,4},{6,7},{7,6},{8,11},{9,10},{10,... | collective-permute-start | bytes 786440 | tf_op jit(solution)/shard_map/near_last/ppermute | solution.py:319
  38.3 3.2 %collective-permute-done.10.refs_4_ = bf16[1280,128]{1,0:T(8,128)(2,1)S(1)} collective-permute-done((bf16[1280,128]{1,0:T(8,128)(2,1)S(1)}, bf16[1280,128]{1,0:T(8,128)(2,1)S(1)}, u32[]{:S(2)}, u32[]{:S(2)}) %collective-permute-start.10) | collective-permute-done | bytes 327712 | tf_op jit(solution)/shard_map/far_a/ppermute | solution.py:314
  41.5 1.3 %collective-permute-done.9.refs_3_ = bf16[1280,128]{1,0:T(8,128)(2,1)S(1)} collective-permute-done((bf16[1280,128]{1,0:T(8,128)(2,1)S(1)}, bf16[1280,128]{1,0:T(8,128)(2,1)S(1)}, u32[]{:S(2)}, u32[]{:S(2)}) %collective-permute-start.9) | collective-permute-done | bytes 327712 | tf_op jit(solution)/shard_map/far_b/ppermute | solution.py:314
  42.9 0.5 collective-permute-start.14
  43.6 0.4 collective-permute-start.16
  44.5 0.4 collective-permute-done.17.refs_11_
  45.1 3.6 %shard_map.104.down = bf16[32,2048]{1,0:T(8,128)(2,1)S(1)} custom-call(s32[8,32]{1,0:T(8,128)S(1)} %get-tuple-element.20.leaf_codes, s32[8,8]{1,0:T(8,128)S(1)} %get-tuple-element.21.par_codes, bf16[2560,128]{1,0:T(8,128)(2,1)S(1)} %shard_map.101.refs_0_, bf16[2560,128]{1,0:T(8,128)(2,1)S(1)} %collective-permute-done.3.refs_1_, ...), custom_call_target="tpu_custom_call" | custom-call | tf_op jit(solution)/shard_map/pallas_call | solution.py:253
  48.8 1.0 %shard_map.105 = bf16[32,4096]{1,0:T(8,128)(2,1)} custom-call(bf16[32,2048]{1,0:T(8,128)(2,1)S(1)} %shard_map.104.down, bf16[32,64,128]{2,1,0:T(8,128)(2,1)S(1)} %bitcast.7, bf16[32,4096]{1,0:T(8,128)(2,1)S(1)} %get-tuple-element.34.keep, bf16[64,4096]{1,0:T(8,128)(2,1)S(1)} %collective-permute-done.11.taken, bf16[32,4096]{1,0:T(8,128)(2,1)S(1)} %collective-permute-done.18.passed), custom_call_target="tpu_custom_call" | custom-call | tf_op jit(solution)/shard_map/pallas_call | solution.py:276
  (34 shorter events, 1.5 us)
Async XLA Ops:
  1.1 9.5 %collective-permute-start.6 = (bf16[64,4096]{1,0:T(8,128)(2,1)S(1)}, bf16[64,4096]{1,0:T(8,128)(2,1)S(1)}, u32[]{:S(2)}, u32[]{:S(2)}) collective-permute-start(bf16[64,4096]{1,0:T(8,128)(2,1)S(1)} %constant_dynamic-slice_fusion), channel_id=1, source_target_pairs={{0,124},{4,8},{8,4},{12,16},{16,12},{20,24},{24,20},{28,32},{32,28... | collective-permute-start | bytes 1572872 | tf_op jit(solution)/shard_map/halo/ppermute | solution.py:314
  1.4 21.0 %collective-permute-start.5 = (bf16[128,4096]{1,0:T(8,128)(2,1)}, bf16[128,4096]{1,0:T(8,128)(2,1)S(1)}, u32[]{:S(2)}, u32[]{:S(2)}) collective-permute-start(bf16[128,4096]{1,0:T(8,128)(2,1)} %refs_0_.1), channel_id=1, source_target_pairs={{0,4},{4,0},{8,12},{12,8},{16,20},{20,16},{24,28},{28,24},{32,36},... | collective-permute-start | bytes 3145736 | tf_op jit(solution)/shard_map/sibling/ppermute | solution.py:314
  5.9 7.0 %collective-permute-start.2 = (bf16[640,128]{1,0:T(8,128)(2,1)S(1)}, bf16[640,128]{1,0:T(8,128)(2,1)S(1)}, u32[]{:S(2)}, u32[]{:S(2)}) collective-permute-start(bf16[640,128]{1,0:T(8,128)(2,1)S(1)} %get-tuple-element.22.refs_0_), channel_id=1, source_target_pairs={{0,16},{4,68},{8,24},{12,76},{16,0},{20,84},{24,8},{28,92},{32,48}... | collective-permute-start | bytes 491528 | tf_op jit(solution)/shard_map/across/ppermute | solution.py:314
  7.3 9.8 %collective-permute-start.1 = (bf16[640,128]{1,0:T(8,128)(2,1)S(1)}, bf16[640,128]{1,0:T(8,128)(2,1)S(1)}, u32[]{:S(2)}, u32[]{:S(2)}) collective-permute-start(bf16[640,128]{1,0:T(8,128)(2,1)S(1)} %get-tuple-element.22.refs_0_), channel_id=1, source_target_pairs={{0,24},{4,100},{8,0},{12,108},{16,8},{20,116},{24,16},{28,124},{32... | collective-permute-start | bytes 491528 | tf_op jit(solution)/shard_map/after/ppermute | solution.py:314
  10.3 6.8 %collective-permute-start = (bf16[640,128]{1,0:T(8,128)(2,1)S(1)}, bf16[640,128]{1,0:T(8,128)(2,1)S(1)}, u32[]{:S(2)}, u32[]{:S(2)}) collective-permute-start(bf16[640,128]{1,0:T(8,128)(2,1)S(1)} %get-tuple-element.22.refs_0_), channel_id=1, source_target_pairs={{0,8},{4,36},{8,16},{12,44},{16,24},{20,52},{24,0},{28,60},{32,40}... | collective-permute-start | bytes 491528 | tf_op jit(solution)/shard_map/before/ppermute | solution.py:314
  10.6 11.9 %collective-permute-start.7 = (bf16[64,4096]{1,0:T(8,128)(2,1)S(1)}, bf16[64,4096]{1,0:T(8,128)(2,1)S(1)}, u32[]{:S(2)}, u32[]{:S(2)}) collective-permute-start(bf16[64,4096]{1,0:T(8,128)(2,1)S(1)} %collective-permute-done.6.far_mine), channel_id=1, source_target_pairs={{0,1},{1,0},{2,3},{3,2},{4,7},{5,6},{6,5},{7,4},{8,9},{9,8},{10,11... | collective-permute-start | bytes 1572872 | tf_op jit(solution)/shard_map/halo_half/ppermute | solution.py:319
  17.2 8.3 %collective-permute-start.8 = (bf16[2560,128]{1,0:T(8,128)(2,1)S(1)}, bf16[2560,128]{1,0:T(8,128)(2,1)S(1)}, u32[]{:S(2)}, u32[]{:S(2)}) collective-permute-start(bf16[2560,128]{1,0:T(8,128)(2,1)S(1)} %shard_map.101.refs_0_), channel_id=1, source_target_pairs={{0,4},{4,0},{8,12},{12,8},{16,20},{20,16},{24,28},{28,24},{32,36},... | collective-permute-start | bytes 1966088 | tf_op jit(solution)/shard_map/swap_own/ppermute | solution.py:314
  17.3 13.3 %collective-permute-start.4 = (bf16[2560,128]{1,0:T(8,128)(2,1)S(1)}, bf16[2560,128]{1,0:T(8,128)(2,1)S(1)}, u32[]{:S(2)}, u32[]{:S(2)}) collective-permute-start(bf16[2560,128]{1,0:T(8,128)(2,1)S(1)} %shard_map.101.refs_0_), channel_id=1, source_target_pairs={{0,96},{4,28},{8,104},{12,4},{16,112},{20,12},{24,120},{28,20},{32... | collective-permute-start | bytes 1966088 | tf_op jit(solution)/shard_map/side_a/ppermute | solution.py:314
  22.4 11.8 %collective-permute-start.3 = (bf16[2560,128]{1,0:T(8,128)(2,1)S(1)}, bf16[2560,128]{1,0:T(8,128)(2,1)S(1)}, u32[]{:S(2)}, u32[]{:S(2)}) collective-permute-start(bf16[2560,128]{1,0:T(8,128)(2,1)S(1)} %shard_map.101.refs_0_), channel_id=1, source_target_pairs={{0,32},{4,12},{8,40},{12,20},{16,48},{20,28},{24,56},{28,4},{32,64... | collective-permute-start | bytes 1966088 | tf_op jit(solution)/shard_map/side_b/ppermute | solution.py:314
  25.3 11.6 %collective-permute-start.11 = (bf16[64,4096]{1,0:T(8,128)(2,1)S(1)}, bf16[64,4096]{1,0:T(8,128)(2,1)S(1)}, u32[]{:S(2)}, u32[]{:S(2)}) collective-permute-start(bf16[64,4096]{1,0:T(8,128)(2,1)S(1)} %get-tuple-element.30), channel_id=1, source_target_pairs={{0,1},{1,0},{2,3},{3,2},{4,7},{5,6},{6,5},{7,4},{8,9},{9,8},{10,11... | collective-permute-start | bytes 1572872 | tf_op jit(solution)/shard_map/near_pairs/ppermute | solution.py:319
  34.3 10.8 %copy-start.1 = (bf16[8,8,64,64]{3,2,1,0:T(8,128)(2,1)S(1)}, bf16[8,8,64,64]{3,2,1,0:T(8,128)(2,1)}, u32[]{:S(2)}) copy-start(bf16[8,8,64,64]{3,2,1,0:T(8,128)(2,1)} %refs_13_.1) | copy-start | bytes 1572868
  34.3 10.8 %copy-start.2 = (bf16[32,64,64]{2,1,0:T(8,128)(2,1)S(1)}, bf16[32,64,64]{2,1,0:T(8,128)(2,1)}, u32[]{:S(2)}) copy-start(bf16[32,64,64]{2,1,0:T(8,128)(2,1)} %refs_14_.1) | copy-start | bytes 786436
  34.3 7.1 %collective-permute-start.10 = (bf16[1280,128]{1,0:T(8,128)(2,1)S(1)}, bf16[1280,128]{1,0:T(8,128)(2,1)S(1)}, u32[]{:S(2)}, u32[]{:S(2)}) collective-permute-start(bf16[1280,128]{1,0:T(8,128)(2,1)S(1)} %slice.19), channel_id=1, source_target_pairs={{0,96},{4,28},{8,104},{12,4},{16,112},{20,12},{24,120},{28,20},{32... | collective-permute-start | bytes 983048 | tf_op jit(solution)/shard_map/far_a/ppermute | solution.py:314
  34.4 8.4 %collective-permute-start.9 = (bf16[1280,128]{1,0:T(8,128)(2,1)S(1)}, bf16[1280,128]{1,0:T(8,128)(2,1)S(1)}, u32[]{:S(2)}, u32[]{:S(2)}) collective-permute-start(bf16[1280,128]{1,0:T(8,128)(2,1)S(1)} %slice.18), channel_id=1, source_target_pairs={{0,32},{4,12},{8,40},{12,20},{16,48},{20,28},{24,56},{28,4},{32,64... | collective-permute-start | bytes 983048 | tf_op jit(solution)/shard_map/far_b/ppermute | solution.py:314
  36.4 7.0 %collective-permute-start.12 = (bf16[2560,128]{1,0:T(8,128)(2,1)S(1)}, bf16[2560,128]{1,0:T(8,128)(2,1)S(1)}, u32[]{:S(2)}, u32[]{:S(2)}) collective-permute-start(bf16[2560,128]{1,0:T(8,128)(2,1)S(1)} %collective-permute-done.3.refs_1_), channel_id=1, source_target_pairs={{0,4},{4,0},{8,12},{12,8},{16,20},{20,16},{24,28},{28,24},{32,36},... | collective-permute-start | bytes 1966088 | tf_op jit(solution)/shard_map/swap_side/ppermute | solution.py:314
  36.4 7.2 %collective-permute-start.13 = (bf16[2560,128]{1,0:T(8,128)(2,1)S(1)}, bf16[2560,128]{1,0:T(8,128)(2,1)S(1)}, u32[]{:S(2)}, u32[]{:S(2)}) collective-permute-start(bf16[2560,128]{1,0:T(8,128)(2,1)S(1)} %collective-permute-done.4.refs_2_), channel_id=1, source_target_pairs={{0,4},{4,0},{8,12},{12,8},{16,20},{20,16},{24,28},{28,24},{32,36},... | collective-permute-start | bytes 1966088 | tf_op jit(solution)/shard_map/swap_side/ppermute | solution.py:314
  36.9 8.2 %copy-start = (bf16[32,8,64,64]{3,2,1,0:T(8,128)(2,1)S(1)}, bf16[32,8,64,64]{3,2,1,0:T(8,128)(2,1)}, u32[]{:S(2)}) copy-start(bf16[32,8,64,64]{3,2,1,0:T(8,128)(2,1)} %refs_12_.1) | copy-start | bytes 6291460
  37.0 11.8 %collective-permute-start.18 = (bf16[32,4096]{1,0:T(8,128)(2,1)S(1)}, bf16[32,4096]{1,0:T(8,128)(2,1)S(1)}, u32[]{:S(2)}, u32[]{:S(2)}) collective-permute-start(bf16[32,4096]{1,0:T(8,128)(2,1)S(1)} %shard_map.103), channel_id=1, source_target_pairs={{0,3},{1,2},{2,1},{3,0},{4,5},{5,4},{6,7},{7,6},{8,11},{9,10},{10,... | collective-permute-start | bytes 786440 | tf_op jit(solution)/shard_map/near_last/ppermute | solution.py:319
  42.8 1.5 %collective-permute-start.15 = (bf16[640,128]{1,0:T(8,128)(2,1)S(1)}, bf16[640,128]{1,0:T(8,128)(2,1)S(1)}, u32[]{:S(2)}, u32[]{:S(2)}) collective-permute-start(bf16[640,128]{1,0:T(8,128)(2,1)S(1)} %get-tuple-element.37), channel_id=1, source_target_pairs={{0,4},{4,0},{8,12},{12,8},{16,20},{20,16},{24,28},{28,24},{32,36},... | collective-permute-start | bytes 491528 | tf_op jit(solution)/shard_map/swap_far/ppermute | solution.py:314
  42.9 1.6 %collective-permute-start.14 = (bf16[640,128]{1,0:T(8,128)(2,1)S(1)}, bf16[640,128]{1,0:T(8,128)(2,1)S(1)}, u32[]{:S(2)}, u32[]{:S(2)}) collective-permute-start(bf16[640,128]{1,0:T(8,128)(2,1)S(1)} %get-tuple-element.38), channel_id=1, source_target_pairs={{0,4},{4,0},{8,12},{12,8},{16,20},{20,16},{24,28},{28,24},{32,36},... | collective-permute-start | bytes 491528 | tf_op jit(solution)/shard_map/swap_far/ppermute | solution.py:314
  43.4 1.5 %collective-permute-start.17 = (bf16[640,128]{1,0:T(8,128)(2,1)S(1)}, bf16[640,128]{1,0:T(8,128)(2,1)S(1)}, u32[]{:S(2)}, u32[]{:S(2)}) collective-permute-start(bf16[640,128]{1,0:T(8,128)(2,1)S(1)} %get-tuple-element.35), channel_id=1, source_target_pairs={{0,4},{4,0},{8,12},{12,8},{16,20},{20,16},{24,28},{28,24},{32,36},... | collective-permute-start | bytes 491528 | tf_op jit(solution)/shard_map/swap_far/ppermute | solution.py:314
  43.6 1.5 %collective-permute-start.16 = (bf16[640,128]{1,0:T(8,128)(2,1)S(1)}, bf16[640,128]{1,0:T(8,128)(2,1)S(1)}, u32[]{:S(2)}, u32[]{:S(2)}) collective-permute-start(bf16[640,128]{1,0:T(8,128)(2,1)S(1)} %get-tuple-element.36), channel_id=1, source_target_pairs={{0,4},{4,0},{8,12},{12,8},{16,20},{20,16},{24,28},{28,24},{32,36},... | collective-permute-start | bytes 491528 | tf_op jit(solution)/shard_map/swap_far/ppermute | solution.py:314
  45.1 3.7 %copy-start.3 = (bf16[32,128,64]{1,2,0:T(8,128)(2,1)S(1)}, bf16[32,128,64]{1,2,0:T(8,128)(2,1)}, u32[]{:S(2)}) copy-start(bf16[32,128,64]{1,2,0:T(8,128)(2,1)} %param.11) | copy-start | bytes 1572868

commit v6 on v5

--- a/solution.py
+++ b/solution.py
@@ -66,9 +66,13 @@
         (near_block, near_here),
     )
     copies = [pltpu.make_async_copy(a, b, sems.at[n]) for n, (a, b) in enumerate(moves)]
-    for copy in copies:
+    for copy in copies[:7]:
         copy.start()
-    for copy in copies[:7]:
+    for copy in copies[:2]:
+        copy.wait()
+    for copy in copies[7:]:
+        copy.start()
+    for copy in copies[3:7]:
         copy.wait()
     y, x, core = clus >> 3, (clus >> 1) & 3, clus & 1
     leaf_codes[...] = codes_of(leaf_here[...], 5, 0, y, x, core)
@@ -82,6 +86,7 @@
         pair = dot_nt(rows[:, 256 * m : 256 * (m + 1)], weights).astype(BF16)
         out[32 * m : 32 * (m + 1), :] = pair
         pairs.append(pair)
+    copies[2].wait()
     for n in range(PARENTS // 2):
         halves = []
         for q in (2 * n, 2 * n + 1):

time: 50.4 us -> 49.7 us (0.986)
  waiting for transfers between devices: 19 us -> 16.9 us
  starting transfers between devices: 18.7 us -> 19.5 us
  Pallas kernels: 10.6 us -> 11.3 us
    ppermute x16, waiting for transfers between devices: 19 us -> 16.9 us  [send(): return lax.ppermute(value, 'clus', pairs)]
    ppermute x3, starting transfers between devices: 3.26 us -> 4.55 us  [trade(): return lax.ppermute(value, ('clus', 'rhs'), partners(first))]
    pallas_call x1, Pallas kernels: 3.01 us -> 3.69 us  [coefficients(): pl.pallas_call(coef_kernel, out_shape=[pltpu.VMEM((ROWS, 128), BF16)] + [...]
    ppermute x16, starting transfers between devices: 15.4 us -> 14.9 us  [send(): return lax.ppermute(value, 'clus', pairs)]
  transfers between devices with their start and end apart: 19 -> 19, of which waited for: 10 -> 10; matrix products, arithmetic and copies ran while one was open for 0% -> 0% of each run, Pallas kernels for 19% -> 21%
where the time goes in v6:
time: 49.7 us; the launch traced here: 49.1 us
  starting transfers between devices  19.5 us (39%)
  waiting for transfers between devices  16.9 us (34%)
  Pallas kernels  11.3 us (23%)
  local copies, waits for them, and re-layouts  1.19 us (2%)
    ppermute x16, waiting for transfers between devices, send(): return lax.ppermute(value, 'clus', pairs)  16.9 us
    ppermute x16, starting transfers between devices, send(): return lax.ppermute(value, 'clus', pairs)  14.9 us
    ppermute x3, starting transfers between devices, trade(): return lax.ppermute(value, ('clus', 'rhs'), partners(first))  4.55 us
    pallas_call x1, Pallas kernels, coefficients(): pl.pallas_call(coef_kernel, out_shape=[pltpu.VMEM((ROWS, 128), BF16)] + [...  3.69 us
    pallas_call x1, Pallas kernels, far_down(): pl.pallas_call(far_kernel, out_shape=jax.ShapeDtypeStruct((32, 2048), BF1...  3.65 us
    pallas_call x1, Pallas kernels, near_partials(): pl.pallas_call(near_kernel, out_shape=[jax.ShapeDtypeStruct((n, 4096), BF...  2.88 us
    dynamic_slice x1, local copies, waits for them, and re-layouts, per_device(): half = lax.dynamic_slice_in_dim(sources, (rhs & 1) * 64, 64, 0)  1.08 us
  transfers between devices with their start and end apart: 19, of which 10 were waited for; matrix products, arithmetic and copies ran while one was open for 0% of the time, Pallas kernels for 21%

profile of v6, /device:TPU:6, one launch (start us, length us, event | category | flops | bytes accessed | tf_op | source)
XLA Modules:
  0.0 49.1 jit_solution(9280227462892337796)
XLA Ops:
  0.0 1.1 %constant_dynamic-slice_fusion = bf16[64,4096]{1,0:T(8,128)(2,1)S(1)} fusion(bf16[128,4096]{1,0:T(8,128)(2,1)} %refs_0_.1, s32[]{:T(128)S(6)} %select_n.3), kind=kLoop, calls=%fused_computation.1 | loop fusion | bytes 1048580 | tf_op jit(solution)/shard_map/dynamic_slice | solution.py:342
  1.1 0.3 collective-permute-start.6
  1.4 1.3 %collective-permute-start.5 = (bf16[128,4096]{1,0:T(8,128)(2,1)}, bf16[128,4096]{1,0:T(8,128)(2,1)S(1)}, u32[]{:S(2)}, u32[]{:S(2)}) collective-permute-start(bf16[128,4096]{1,0:T(8,128)(2,1)} %refs_0_.1), channel_id=1, source_target_pairs={{0,4},{4,0},{8,12},{12,8},{16,20},{20,16},{24,28},{28,24},{32,36},... | collective-permute-start | bytes 3145736 | tf_op jit(solution)/shard_map/sibling/ppermute | solution.py:319
  2.8 3.7 %shard_map.100 = (bf16[640,128]{1,0:T(8,128)(2,1)S(1)}, s32[8,32]{1,0:T(8,128)S(1)}, s32[8,8]{1,0:T(8,128)S(1)}, s32[2,32]{1,0:T(2,128)S(1)}, bf16[128,4096]{1,0...) custom-call(s32[2]{0:T(128)S(1)} %pad_add_fusion.meta, bf16[128,4096]{1,0:T(8,128)(2,1)} %refs_0_.1, ...), custom_call_target="tpu_custom_call" | custom-call | flops 3000000000 | bytes 9000000 | tf_op jit(solution)/shard_map/pallas_call | solution.py:105
  6.5 1.5 %collective-permute-start.2 = (bf16[640,128]{1,0:T(8,128)(2,1)S(1)}, bf16[640,128]{1,0:T(8,128)(2,1)S(1)}, u32[]{:S(2)}, u32[]{:S(2)}) collective-permute-start(bf16[640,128]{1,0:T(8,128)(2,1)S(1)} %get-tuple-element.22.refs_0_), channel_id=1, source_target_pairs={{0,16},{4,68},{8,24},{12,76},{16,0},{20,84},{24,8},{28,92},{32,48}... | collective-permute-start | bytes 491528 | tf_op jit(solution)/shard_map/across/ppermute | solution.py:319
  8.0 3.0 %collective-permute-start.1 = (bf16[640,128]{1,0:T(8,128)(2,1)S(1)}, bf16[640,128]{1,0:T(8,128)(2,1)S(1)}, u32[]{:S(2)}, u32[]{:S(2)}) collective-permute-start(bf16[640,128]{1,0:T(8,128)(2,1)S(1)} %get-tuple-element.22.refs_0_), channel_id=1, source_target_pairs={{0,24},{4,100},{8,0},{12,108},{16,8},{20,116},{24,16},{28,124},{32... | collective-permute-start | bytes 491528 | tf_op jit(solution)/shard_map/after/ppermute | solution.py:319
  11.3 1.9 %collective-permute-start.7 = (bf16[64,4096]{1,0:T(8,128)(2,1)S(1)}, bf16[64,4096]{1,0:T(8,128)(2,1)S(1)}, u32[]{:S(2)}, u32[]{:S(2)}) collective-permute-start(bf16[64,4096]{1,0:T(8,128)(2,1)S(1)} %collective-permute-done.6.far_mine), channel_id=1, source_target_pairs={{0,1},{1,0},{2,3},{3,2},{4,7},{5,6},{6,5},{7,4},{8,9},{9,8},{10,11... | collective-permute-start | bytes 1572872 | tf_op jit(solution)/shard_map/halo_half/ppermute | solution.py:324
  13.2 0.4 collective-permute-done.2.refs_3_
  13.5 3.4 %collective-permute-done.1.refs_2_ = bf16[640,128]{1,0:T(8,128)(2,1)S(1)} collective-permute-done((bf16[640,128]{1,0:T(8,128)(2,1)S(1)}, bf16[640,128]{1,0:T(8,128)(2,1)S(1)}, u32[]{:S(2)}, u32[]{:S(2)}) %collective-permute-start.1) | collective-permute-done | bytes 163872 | tf_op jit(solution)/shard_map/after/ppermute | solution.py:319
  17.1 4.7 %collective-permute-start.4 = (bf16[2560,128]{1,0:T(8,128)(2,1)S(1)}, bf16[2560,128]{1,0:T(8,128)(2,1)S(1)}, u32[]{:S(2)}, u32[]{:S(2)}) collective-permute-start(bf16[2560,128]{1,0:T(8,128)(2,1)S(1)} %shard_map.101.refs_0_), channel_id=1, source_target_pairs={{0,96},{4,28},{8,104},{12,4},{16,112},{20,12},{24,120},{28,20},{32... | collective-permute-start | bytes 1966088 | tf_op jit(solution)/shard_map/side_a/ppermute | solution.py:319
  21.8 2.9 %shard_map.102 = (bf16[32,4096]{1,0:T(8,128)(2,1)S(1)}, bf16[32,4096]{1,0:T(8,128)(2,1)S(1)}, bf16[64,4096]{1,0:T(8,128)(2,1)S(1)}) custom-call(s32[2]{0:T(128)S(1)} %pad_add_fusion.meta, s32[2,32]{1,0:T(2,128)S(1)} %get-tuple-element.23.near_codes, bf16[128,4096]{1,0:T(8,128)(2,1)S(1)} %get-tuple-element.24.own, ...), custom_call_target="tpu_custom_call" | custom-call | flops 3000000000 | bytes 9000000 | tf_op jit(solution)/shard_map/pallas_call | solution.py:191
  24.7 0.7 %collective-permute-start.11 = (bf16[64,4096]{1,0:T(8,128)(2,1)S(1)}, bf16[64,4096]{1,0:T(8,128)(2,1)S(1)}, u32[]{:S(2)}, u32[]{:S(2)}) collective-permute-start(bf16[64,4096]{1,0:T(8,128)(2,1)S(1)} %get-tuple-element.30), channel_id=1, source_target_pairs={{0,1},{1,0},{2,3},{3,2},{4,7},{5,6},{6,5},{7,4},{8,9},{9,8},{10,11... | collective-permute-start | bytes 1572872 | tf_op jit(solution)/shard_map/near_pairs/ppermute | solution.py:324
  25.3 4.5 %collective-permute-done.4.refs_2_ = bf16[2560,128]{1,0:T(8,128)(2,1)S(1)} collective-permute-done((bf16[2560,128]{1,0:T(8,128)(2,1)S(1)}, bf16[2560,128]{1,0:T(8,128)(2,1)S(1)}, u32[]{:S(2)}, u32[]{:S(2)}) %collective-permute-start.4) | collective-permute-done | bytes 655392 | tf_op jit(solution)/shard_map/side_a/ppermute | solution.py:319
  29.9 3.7 %collective-permute-done.3.refs_1_ = bf16[2560,128]{1,0:T(8,128)(2,1)S(1)} collective-permute-done((bf16[2560,128]{1,0:T(8,128)(2,1)S(1)}, bf16[2560,128]{1,0:T(8,128)(2,1)S(1)}, u32[]{:S(2)}, u32[]{:S(2)}) %collective-permute-start.3) | collective-permute-done | bytes 655392 | tf_op jit(solution)/shard_map/side_b/ppermute | solution.py:319
  33.7 2.0 %collective-permute-start.9 = (bf16[1280,128]{1,0:T(8,128)(2,1)S(1)}, bf16[1280,128]{1,0:T(8,128)(2,1)S(1)}, u32[]{:S(2)}, u32[]{:S(2)}) collective-permute-start(bf16[1280,128]{1,0:T(8,128)(2,1)S(1)} %slice.18), channel_id=1, source_target_pairs={{0,32},{4,12},{8,40},{12,20},{16,48},{20,28},{24,56},{28,4},{32,64... | collective-permute-start | bytes 983048 | tf_op jit(solution)/shard_map/far_b/ppermute | solution.py:319
  35.7 0.5 %collective-permute-start.13 = (bf16[2560,128]{1,0:T(8,128)(2,1)S(1)}, bf16[2560,128]{1,0:T(8,128)(2,1)S(1)}, u32[]{:S(2)}, u32[]{:S(2)}) collective-permute-start(bf16[2560,128]{1,0:T(8,128)(2,1)S(1)} %collective-permute-done.4.refs_2_), channel_id=1, source_target_pairs={{0,4},{4,0},{8,12},{12,8},{16,20},{20,16},{24,28},{28,24},{32,36},... | collective-permute-start | bytes 1966088 | tf_op jit(solution)/shard_map/swap_side/ppermute | solution.py:319
  36.3 1.9 %collective-permute-start.18 = (bf16[32,4096]{1,0:T(8,128)(2,1)S(1)}, bf16[32,4096]{1,0:T(8,128)(2,1)S(1)}, u32[]{:S(2)}, u32[]{:S(2)}) collective-permute-start(bf16[32,4096]{1,0:T(8,128)(2,1)S(1)} %shard_map.103), channel_id=1, source_target_pairs={{0,3},{1,2},{2,1},{3,0},{4,5},{5,4},{6,7},{7,6},{8,11},{9,10},{10,... | collective-permute-start | bytes 786440 | tf_op jit(solution)/shard_map/near_last/ppermute | solution.py:324
  38.3 2.5 %collective-permute-done.10.refs_4_ = bf16[1280,128]{1,0:T(8,128)(2,1)S(1)} collective-permute-done((bf16[1280,128]{1,0:T(8,128)(2,1)S(1)}, bf16[1280,128]{1,0:T(8,128)(2,1)S(1)}, u32[]{:S(2)}, u32[]{:S(2)}) %collective-permute-start.10) | collective-permute-done | bytes 327712 | tf_op jit(solution)/shard_map/far_a/ppermute | solution.py:319
  40.8 1.3 %collective-permute-done.9.refs_3_ = bf16[1280,128]{1,0:T(8,128)(2,1)S(1)} collective-permute-done((bf16[1280,128]{1,0:T(8,128)(2,1)S(1)}, bf16[1280,128]{1,0:T(8,128)(2,1)S(1)}, u32[]{:S(2)}, u32[]{:S(2)}) %collective-permute-start.9) | collective-permute-done | bytes 327712 | tf_op jit(solution)/shard_map/far_b/ppermute | solution.py:319
  42.2 0.5 %collective-permute-start.14 = (bf16[640,128]{1,0:T(8,128)(2,1)S(1)}, bf16[640,128]{1,0:T(8,128)(2,1)S(1)}, u32[]{:S(2)}, u32[]{:S(2)}) collective-permute-start(bf16[640,128]{1,0:T(8,128)(2,1)S(1)} %get-tuple-element.38), channel_id=1, source_target_pairs={{0,4},{4,0},{8,12},{12,8},{16,20},{20,16},{24,28},{28,24},{32,36},... | collective-permute-start | bytes 491528 | tf_op jit(solution)/shard_map/swap_far/ppermute | solution.py:319
  42.9 0.4 collective-permute-start.16
  43.8 0.4 collective-permute-done.17.refs_11_
  44.5 3.7 %shard_map.104.down = bf16[32,2048]{1,0:T(8,128)(2,1)S(1)} custom-call(s32[8,32]{1,0:T(8,128)S(1)} %get-tuple-element.20.leaf_codes, s32[8,8]{1,0:T(8,128)S(1)} %get-tuple-element.21.par_codes, bf16[2560,128]{1,0:T(8,128)(2,1)S(1)} %shard_map.101.refs_0_, bf16[2560,128]{1,0:T(8,128)(2,1)S(1)} %collective-permute-done.3.refs_1_, ...), custom_call_target="tpu_custom_call" | custom-call | tf_op jit(solution)/shard_map/pallas_call | solution.py:258
  48.1 1.0 %shard_map.105 = bf16[32,4096]{1,0:T(8,128)(2,1)} custom-call(bf16[32,2048]{1,0:T(8,128)(2,1)S(1)} %shard_map.104.down, bf16[32,64,128]{2,1,0:T(8,128)(2,1)S(1)} %bitcast.7, bf16[32,4096]{1,0:T(8,128)(2,1)S(1)} %get-tuple-element.34.keep, bf16[64,4096]{1,0:T(8,128)(2,1)S(1)} %collective-permute-done.11.taken, bf16[32,4096]{1,0:T(8,128)(2,1)S(1)} %collective-permute-done.18.passed), custom_call_target="tpu_custom_call" | custom-call | tf_op jit(solution)/shard_map/pallas_call | solution.py:281
  (34 shorter events, 1.7 us)
Async XLA Ops:
  1.1 10.2 %collective-permute-start.6 = (bf16[64,4096]{1,0:T(8,128)(2,1)S(1)}, bf16[64,4096]{1,0:T(8,128)(2,1)S(1)}, u32[]{:S(2)}, u32[]{:S(2)}) collective-permute-start(bf16[64,4096]{1,0:T(8,128)(2,1)S(1)} %constant_dynamic-slice_fusion), channel_id=1, source_target_pairs={{0,124},{4,8},{8,4},{12,16},{16,12},{20,24},{24,20},{28,32},{32,28... | collective-permute-start | bytes 1572872 | tf_op jit(solution)/shard_map/halo/ppermute | solution.py:319
  1.4 20.3 %collective-permute-start.5 = (bf16[128,4096]{1,0:T(8,128)(2,1)}, bf16[128,4096]{1,0:T(8,128)(2,1)S(1)}, u32[]{:S(2)}, u32[]{:S(2)}) collective-permute-start(bf16[128,4096]{1,0:T(8,128)(2,1)} %refs_0_.1), channel_id=1, source_target_pairs={{0,4},{4,0},{8,12},{12,8},{16,20},{20,16},{24,28},{28,24},{32,36},... | collective-permute-start | bytes 3145736 | tf_op jit(solution)/shard_map/sibling/ppermute | solution.py:319
  6.5 7.0 %collective-permute-start.2 = (bf16[640,128]{1,0:T(8,128)(2,1)S(1)}, bf16[640,128]{1,0:T(8,128)(2,1)S(1)}, u32[]{:S(2)}, u32[]{:S(2)}) collective-permute-start(bf16[640,128]{1,0:T(8,128)(2,1)S(1)} %get-tuple-element.22.refs_0_), channel_id=1, source_target_pairs={{0,16},{4,68},{8,24},{12,76},{16,0},{20,84},{24,8},{28,92},{32,48}... | collective-permute-start | bytes 491528 | tf_op jit(solution)/shard_map/across/ppermute | solution.py:319
  8.0 8.9 %collective-permute-start.1 = (bf16[640,128]{1,0:T(8,128)(2,1)S(1)}, bf16[640,128]{1,0:T(8,128)(2,1)S(1)}, u32[]{:S(2)}, u32[]{:S(2)}) collective-permute-start(bf16[640,128]{1,0:T(8,128)(2,1)S(1)} %get-tuple-element.22.refs_0_), channel_id=1, source_target_pairs={{0,24},{4,100},{8,0},{12,108},{16,8},{20,116},{24,16},{28,124},{32... | collective-permute-start | bytes 491528 | tf_op jit(solution)/shard_map/after/ppermute | solution.py:319
  11.0 6.0 %collective-permute-start = (bf16[640,128]{1,0:T(8,128)(2,1)S(1)}, bf16[640,128]{1,0:T(8,128)(2,1)S(1)}, u32[]{:S(2)}, u32[]{:S(2)}) collective-permute-start(bf16[640,128]{1,0:T(8,128)(2,1)S(1)} %get-tuple-element.22.refs_0_), channel_id=1, source_target_pairs={{0,8},{4,36},{8,16},{12,44},{16,24},{20,52},{24,0},{28,60},{32,40}... | collective-permute-start | bytes 491528 | tf_op jit(solution)/shard_map/before/ppermute | solution.py:319
  11.3 10.5 %collective-permute-start.7 = (bf16[64,4096]{1,0:T(8,128)(2,1)S(1)}, bf16[64,4096]{1,0:T(8,128)(2,1)S(1)}, u32[]{:S(2)}, u32[]{:S(2)}) collective-permute-start(bf16[64,4096]{1,0:T(8,128)(2,1)S(1)} %collective-permute-done.6.far_mine), channel_id=1, source_target_pairs={{0,1},{1,0},{2,3},{3,2},{4,7},{5,6},{6,5},{7,4},{8,9},{9,8},{10,11... | collective-permute-start | bytes 1572872 | tf_op jit(solution)/shard_map/halo_half/ppermute | solution.py:324
  17.0 8.3 %collective-permute-start.8 = (bf16[2560,128]{1,0:T(8,128)(2,1)S(1)}, bf16[2560,128]{1,0:T(8,128)(2,1)S(1)}, u32[]{:S(2)}, u32[]{:S(2)}) collective-permute-start(bf16[2560,128]{1,0:T(8,128)(2,1)S(1)} %shard_map.101.refs_0_), channel_id=1, source_target_pairs={{0,4},{4,0},{8,12},{12,8},{16,20},{20,16},{24,28},{28,24},{32,36},... | collective-permute-start | bytes 1966088 | tf_op jit(solution)/shard_map/swap_own/ppermute | solution.py:319
  17.1 12.8 %collective-permute-start.4 = (bf16[2560,128]{1,0:T(8,128)(2,1)S(1)}, bf16[2560,128]{1,0:T(8,128)(2,1)S(1)}, u32[]{:S(2)}, u32[]{:S(2)}) collective-permute-start(bf16[2560,128]{1,0:T(8,128)(2,1)S(1)} %shard_map.101.refs_0_), channel_id=1, source_target_pairs={{0,96},{4,28},{8,104},{12,4},{16,112},{20,12},{24,120},{28,20},{32... | collective-permute-start | bytes 1966088 | tf_op jit(solution)/shard_map/side_a/ppermute | solution.py:319
  21.8 11.8 %collective-permute-start.3 = (bf16[2560,128]{1,0:T(8,128)(2,1)S(1)}, bf16[2560,128]{1,0:T(8,128)(2,1)S(1)}, u32[]{:S(2)}, u32[]{:S(2)}) collective-permute-start(bf16[2560,128]{1,0:T(8,128)(2,1)S(1)} %shard_map.101.refs_0_), channel_id=1, source_target_pairs={{0,32},{4,12},{8,40},{12,20},{16,48},{20,28},{24,56},{28,4},{32,64... | collective-permute-start | bytes 1966088 | tf_op jit(solution)/shard_map/side_b/ppermute | solution.py:319
  24.7 11.6 %collective-permute-start.11 = (bf16[64,4096]{1,0:T(8,128)(2,1)S(1)}, bf16[64,4096]{1,0:T(8,128)(2,1)S(1)}, u32[]{:S(2)}, u32[]{:S(2)}) collective-permute-start(bf16[64,4096]{1,0:T(8,128)(2,1)S(1)} %get-tuple-element.30), channel_id=1, source_target_pairs={{0,1},{1,0},{2,3},{3,2},{4,7},{5,6},{6,5},{7,4},{8,9},{9,8},{10,11... | collective-permute-start | bytes 1572872 | tf_op jit(solution)/shard_map/near_pairs/ppermute | solution.py:324
  33.6 10.8 %copy-start.1 = (bf16[8,8,64,64]{3,2,1,0:T(8,128)(2,1)S(1)}, bf16[8,8,64,64]{3,2,1,0:T(8,128)(2,1)}, u32[]{:S(2)}) copy-start(bf16[8,8,64,64]{3,2,1,0:T(8,128)(2,1)} %refs_13_.1) | copy-start | bytes 1572868
  33.6 10.8 %copy-start.2 = (bf16[32,64,64]{2,1,0:T(8,128)(2,1)S(1)}, bf16[32,64,64]{2,1,0:T(8,128)(2,1)}, u32[]{:S(2)}) copy-start(bf16[32,64,64]{2,1,0:T(8,128)(2,1)} %refs_14_.1) | copy-start | bytes 786436
  33.6 7.1 %collective-permute-start.10 = (bf16[1280,128]{1,0:T(8,128)(2,1)S(1)}, bf16[1280,128]{1,0:T(8,128)(2,1)S(1)}, u32[]{:S(2)}, u32[]{:S(2)}) collective-permute-start(bf16[1280,128]{1,0:T(8,128)(2,1)S(1)} %slice.19), channel_id=1, source_target_pairs={{0,96},{4,28},{8,104},{12,4},{16,112},{20,12},{24,120},{28,20},{32... | collective-permute-start | bytes 983048 | tf_op jit(solution)/shard_map/far_a/ppermute | solution.py:319
  33.7 8.4 %collective-permute-start.9 = (bf16[1280,128]{1,0:T(8,128)(2,1)S(1)}, bf16[1280,128]{1,0:T(8,128)(2,1)S(1)}, u32[]{:S(2)}, u32[]{:S(2)}) collective-permute-start(bf16[1280,128]{1,0:T(8,128)(2,1)S(1)} %slice.18), channel_id=1, source_target_pairs={{0,32},{4,12},{8,40},{12,20},{16,48},{20,28},{24,56},{28,4},{32,64... | collective-permute-start | bytes 983048 | tf_op jit(solution)/shard_map/far_b/ppermute | solution.py:319
  35.7 7.0 %collective-permute-start.12 = (bf16[2560,128]{1,0:T(8,128)(2,1)S(1)}, bf16[2560,128]{1,0:T(8,128)(2,1)S(1)}, u32[]{:S(2)}, u32[]{:S(2)}) collective-permute-start(bf16[2560,128]{1,0:T(8,128)(2,1)S(1)} %collective-permute-done.3.refs_1_), channel_id=1, source_target_pairs={{0,4},{4,0},{8,12},{12,8},{16,20},{20,16},{24,28},{28,24},{32,36},... | collective-permute-start | bytes 1966088 | tf_op jit(solution)/shard_map/swap_side/ppermute | solution.py:319
  35.7 7.2 %collective-permute-start.13 = (bf16[2560,128]{1,0:T(8,128)(2,1)S(1)}, bf16[2560,128]{1,0:T(8,128)(2,1)S(1)}, u32[]{:S(2)}, u32[]{:S(2)}) collective-permute-start(bf16[2560,128]{1,0:T(8,128)(2,1)S(1)} %collective-permute-done.4.refs_2_), channel_id=1, source_target_pairs={{0,4},{4,0},{8,12},{12,8},{16,20},{20,16},{24,28},{28,24},{32,36},... | collective-permute-start | bytes 1966088 | tf_op jit(solution)/shard_map/swap_side/ppermute | solution.py:319
  36.2 8.2 %copy-start = (bf16[32,8,64,64]{3,2,1,0:T(8,128)(2,1)S(1)}, bf16[32,8,64,64]{3,2,1,0:T(8,128)(2,1)}, u32[]{:S(2)}) copy-start(bf16[32,8,64,64]{3,2,1,0:T(8,128)(2,1)} %refs_12_.1) | copy-start | bytes 6291460
  36.3 11.8 %collective-permute-start.18 = (bf16[32,4096]{1,0:T(8,128)(2,1)S(1)}, bf16[32,4096]{1,0:T(8,128)(2,1)S(1)}, u32[]{:S(2)}, u32[]{:S(2)}) collective-permute-start(bf16[32,4096]{1,0:T(8,128)(2,1)S(1)} %shard_map.103), channel_id=1, source_target_pairs={{0,3},{1,2},{2,1},{3,0},{4,5},{5,4},{6,7},{7,6},{8,11},{9,10},{10,... | collective-permute-start | bytes 786440 | tf_op jit(solution)/shard_map/near_last/ppermute | solution.py:324
  42.1 1.5 %collective-permute-start.15 = (bf16[640,128]{1,0:T(8,128)(2,1)S(1)}, bf16[640,128]{1,0:T(8,128)(2,1)S(1)}, u32[]{:S(2)}, u32[]{:S(2)}) collective-permute-start(bf16[640,128]{1,0:T(8,128)(2,1)S(1)} %get-tuple-element.37), channel_id=1, source_target_pairs={{0,4},{4,0},{8,12},{12,8},{16,20},{20,16},{24,28},{28,24},{32,36},... | collective-permute-start | bytes 491528 | tf_op jit(solution)/shard_map/swap_far/ppermute | solution.py:319
  42.2 1.6 %collective-permute-start.14 = (bf16[640,128]{1,0:T(8,128)(2,1)S(1)}, bf16[640,128]{1,0:T(8,128)(2,1)S(1)}, u32[]{:S(2)}, u32[]{:S(2)}) collective-permute-start(bf16[640,128]{1,0:T(8,128)(2,1)S(1)} %get-tuple-element.38), channel_id=1, source_target_pairs={{0,4},{4,0},{8,12},{12,8},{16,20},{20,16},{24,28},{28,24},{32,36},... | collective-permute-start | bytes 491528 | tf_op jit(solution)/shard_map/swap_far/ppermute | solution.py:319
  42.7 1.5 %collective-permute-start.17 = (bf16[640,128]{1,0:T(8,128)(2,1)S(1)}, bf16[640,128]{1,0:T(8,128)(2,1)S(1)}, u32[]{:S(2)}, u32[]{:S(2)}) collective-permute-start(bf16[640,128]{1,0:T(8,128)(2,1)S(1)} %get-tuple-element.35), channel_id=1, source_target_pairs={{0,4},{4,0},{8,12},{12,8},{16,20},{20,16},{24,28},{28,24},{32,36},... | collective-permute-start | bytes 491528 | tf_op jit(solution)/shard_map/swap_far/ppermute | solution.py:319
  42.9 1.5 %collective-permute-start.16 = (bf16[640,128]{1,0:T(8,128)(2,1)S(1)}, bf16[640,128]{1,0:T(8,128)(2,1)S(1)}, u32[]{:S(2)}, u32[]{:S(2)}) collective-permute-start(bf16[640,128]{1,0:T(8,128)(2,1)S(1)} %get-tuple-element.36), channel_id=1, source_target_pairs={{0,4},{4,0},{8,12},{12,8},{16,20},{20,16},{24,28},{28,24},{32,36},... | collective-permute-start | bytes 491528 | tf_op jit(solution)/shard_map/swap_far/ppermute | solution.py:319
  44.4 3.7 %copy-start.3 = (bf16[32,128,64]{1,2,0:T(8,128)(2,1)S(1)}, bf16[32,128,64]{1,2,0:T(8,128)(2,1)}, u32[]{:S(2)}) copy-start(bf16[32,128,64]{1,2,0:T(8,128)(2,1)} %param.11) | copy-start | bytes 1572868

commit v7 on v6

--- a/solution.py
+++ b/solution.py
@@ -72,14 +72,6 @@
         copy.wait()
     for copy in copies[7:]:
         copy.start()
-    for copy in copies[3:7]:
-        copy.wait()
-    y, x, core = clus >> 3, (clus >> 1) & 3, clus & 1
-    leaf_codes[...] = codes_of(leaf_here[...], 5, 0, y, x, core)
-    par_codes[...] = codes_of(par_here[...], 3, 512, y, x, core)
-    slot = z * 2 + lax.broadcasted_iota(jnp.int32, (2, LEAVES), 0)
-    place = jnp.clip(list_here[...] - (clus - 1) * LEAVES, 0, 3 * LEAVES - 1)
-    near_codes[...] = jnp.where(slot < count_here[...], place, -1)
     pairs = []
     for m in range(LEAVES // 2):
         weights = diagonal(basis_here[2 * m], basis_here[2 * m + 1])
@@ -94,6 +86,14 @@
             weights = transfer_here[4 * q : 4 * q + 4].reshape(256, 64)
             halves.append(jnp.dot(children, weights, preferred_element_type=F32))
         out[512 + 32 * n : 512 + 32 * (n + 1), :] = side_by_side(*halves).astype(BF16)
+    for copy in copies[3:7]:
+        copy.wait()
+    y, x, core = clus >> 3, (clus >> 1) & 3, clus & 1
+    leaf_codes[...] = codes_of(leaf_here[...], 5, 0, y, x, core)
+    par_codes[...] = codes_of(par_here[...], 3, 512, y, x, core)
+    slot = z * 2 + lax.broadcasted_iota(jnp.int32, (2, LEAVES), 0)
+    place = jnp.clip(list_here[...] - (clus - 1) * LEAVES, 0, 3 * LEAVES - 1)
+    near_codes[...] = jnp.where(slot < count_here[...], place, -1)
     for copy in copies[7:]:
         copy.wait()
 
@@ -218,9 +218,8 @@
 def far_kernel(leaf_codes, par_codes, *refs):
     coupling, par_coupling, transfer, out, held = refs[-5:]
     fill(held, refs[:-5])
-    lane = lax.broadcasted_iota(jnp.int32, (1, 128), 1)
-    low = (lane < 64).astype(F32).astype(BF16)
-    high = (lane >= 64).astype(F32).astype(BF16)
+    lane = lax.broadcasted_iota(jnp.int32, (32, 128), 1)
+    first = lane < 64
 
     def turned(code, wanted):
         pair = held[pl.ds(pl.multiple_of(code & ~31, 32), 32), :]
@@ -230,7 +229,7 @@
     def couple(codes, blocks):
         terms, weights = [], []
         for i in range(0, 8, 2):
-            terms.append(turned(codes[i], 0) * low + turned(codes[i + 1], 1) * high)
+            terms.append(jnp.where(first, turned(codes[i], 0), turned(codes[i + 1], 1)))
             weights.append(side_by_side(blocks(i), blocks(i + 1)))
         return dot_nt(jnp.concatenate(terms, axis=1), jnp.concatenate(weights, axis=1))
 

time: 49.7 us -> 49.7 us (level)
  no operation moved by 1% of the time
where the time goes in v7:
time: 49.7 us; the launch traced here: 49.1 us
  starting transfers between devices  19.5 us (39%)
  waiting for transfers between devices  16.9 us (34%)
  Pallas kernels  11.3 us (23%)
  local copies, waits for them, and re-layouts  1.19 us (2%)
    ppermute x16, waiting for transfers between devices, send(): return lax.ppermute(value, 'clus', pairs)  16.9 us
    ppermute x16, starting transfers between devices, send(): return lax.ppermute(value, 'clus', pairs)  14.9 us
    ppermute x3, starting transfers between devices, trade(): return lax.ppermute(value, ('clus', 'rhs'), partners(first))  4.54 us
    pallas_call x1, Pallas kernels, coefficients(): pl.pallas_call(coef_kernel, out_shape=[pltpu.VMEM((ROWS, 128), BF16)] + [...  3.69 us
    pallas_call x1, Pallas kernels, far_down(): pl.pallas_call(far_kernel, out_shape=jax.ShapeDtypeStruct((32, 2048), BF1...  3.63 us
    pallas_call x1, Pallas kernels, near_partials(): pl.pallas_call(near_kernel, out_shape=[jax.ShapeDtypeStruct((n, 4096), BF...  2.89 us
    dynamic_slice x1, local copies, waits for them, and re-layouts, per_device(): half = lax.dynamic_slice_in_dim(sources, (rhs & 1) * 64, 64, 0)  1.08 us
  transfers between devices with their start and end apart: 19, of which 10 were waited for; matrix products, arithmetic and copies ran while one was open for 0% of the time, Pallas kernels for 21%

profile of v7, /device:TPU:6, one launch (start us, length us, event | category | flops | bytes accessed | tf_op | source)
XLA Modules:
  0.0 49.1 jit_solution(7894019733969394827)
XLA Ops:
  0.0 1.1 %constant_dynamic-slice_fusion = bf16[64,4096]{1,0:T(8,128)(2,1)S(1)} fusion(bf16[128,4096]{1,0:T(8,128)(2,1)} %refs_0_.1, s32[]{:T(128)S(6)} %select_n.3), kind=kLoop, calls=%fused_computation.1 | loop fusion | bytes 1048580 | tf_op jit(solution)/shard_map/dynamic_slice | solution.py:341
  1.1 0.3 collective-permute-start.6
  1.4 1.3 %collective-permute-start.5 = (bf16[128,4096]{1,0:T(8,128)(2,1)}, bf16[128,4096]{1,0:T(8,128)(2,1)S(1)}, u32[]{:S(2)}, u32[]{:S(2)}) collective-permute-start(bf16[128,4096]{1,0:T(8,128)(2,1)} %refs_0_.1), channel_id=1, source_target_pairs={{0,4},{4,0},{8,12},{12,8},{16,20},{20,16},{24,28},{28,24},{32,36},... | collective-permute-start | bytes 3145736 | tf_op jit(solution)/shard_map/sibling/ppermute | solution.py:318
  2.8 3.7 %shard_map.100 = (bf16[640,128]{1,0:T(8,128)(2,1)S(1)}, s32[8,32]{1,0:T(8,128)S(1)}, s32[8,8]{1,0:T(8,128)S(1)}, s32[2,32]{1,0:T(2,128)S(1)}, bf16[128,4096]{1,0...) custom-call(s32[2]{0:T(128)S(1)} %pad_add_fusion.meta, bf16[128,4096]{1,0:T(8,128)(2,1)} %refs_0_.1, ...), custom_call_target="tpu_custom_call" | custom-call | flops 3000000000 | bytes 9000000 | tf_op jit(solution)/shard_map/pallas_call | solution.py:105
  6.5 1.5 %collective-permute-start.2 = (bf16[640,128]{1,0:T(8,128)(2,1)S(1)}, bf16[640,128]{1,0:T(8,128)(2,1)S(1)}, u32[]{:S(2)}, u32[]{:S(2)}) collective-permute-start(bf16[640,128]{1,0:T(8,128)(2,1)S(1)} %get-tuple-element.22.refs_0_), channel_id=1, source_target_pairs={{0,16},{4,68},{8,24},{12,76},{16,0},{20,84},{24,8},{28,92},{32,48}... | collective-permute-start | bytes 491528 | tf_op jit(solution)/shard_map/across/ppermute | solution.py:318
  8.0 3.0 %collective-permute-start.1 = (bf16[640,128]{1,0:T(8,128)(2,1)S(1)}, bf16[640,128]{1,0:T(8,128)(2,1)S(1)}, u32[]{:S(2)}, u32[]{:S(2)}) collective-permute-start(bf16[640,128]{1,0:T(8,128)(2,1)S(1)} %get-tuple-element.22.refs_0_), channel_id=1, source_target_pairs={{0,24},{4,100},{8,0},{12,108},{16,8},{20,116},{24,16},{28,124},{32... | collective-permute-start | bytes 491528 | tf_op jit(solution)/shard_map/after/ppermute | solution.py:318
  11.3 1.9 %collective-permute-start.7 = (bf16[64,4096]{1,0:T(8,128)(2,1)S(1)}, bf16[64,4096]{1,0:T(8,128)(2,1)S(1)}, u32[]{:S(2)}, u32[]{:S(2)}) collective-permute-start(bf16[64,4096]{1,0:T(8,128)(2,1)S(1)} %collective-permute-done.6.far_mine), channel_id=1, source_target_pairs={{0,1},{1,0},{2,3},{3,2},{4,7},{5,6},{6,5},{7,4},{8,9},{9,8},{10,11... | collective-permute-start | bytes 1572872 | tf_op jit(solution)/shard_map/halo_half/ppermute | solution.py:323
  13.2 0.4 collective-permute-done.2.refs_3_
  13.5 3.4 %collective-permute-done.1.refs_2_ = bf16[640,128]{1,0:T(8,128)(2,1)S(1)} collective-permute-done((bf16[640,128]{1,0:T(8,128)(2,1)S(1)}, bf16[640,128]{1,0:T(8,128)(2,1)S(1)}, u32[]{:S(2)}, u32[]{:S(2)}) %collective-permute-start.1) | collective-permute-done | bytes 163872 | tf_op jit(solution)/shard_map/after/ppermute | solution.py:318
  17.1 4.7 %collective-permute-start.4 = (bf16[2560,128]{1,0:T(8,128)(2,1)S(1)}, bf16[2560,128]{1,0:T(8,128)(2,1)S(1)}, u32[]{:S(2)}, u32[]{:S(2)}) collective-permute-start(bf16[2560,128]{1,0:T(8,128)(2,1)S(1)} %shard_map.101.refs_0_), channel_id=1, source_target_pairs={{0,96},{4,28},{8,104},{12,4},{16,112},{20,12},{24,120},{28,20},{32... | collective-permute-start | bytes 1966088 | tf_op jit(solution)/shard_map/side_a/ppermute | solution.py:318
  21.8 2.9 %shard_map.102 = (bf16[32,4096]{1,0:T(8,128)(2,1)S(1)}, bf16[32,4096]{1,0:T(8,128)(2,1)S(1)}, bf16[64,4096]{1,0:T(8,128)(2,1)S(1)}) custom-call(s32[2]{0:T(128)S(1)} %pad_add_fusion.meta, s32[2,32]{1,0:T(2,128)S(1)} %get-tuple-element.23.near_codes, bf16[128,4096]{1,0:T(8,128)(2,1)S(1)} %get-tuple-element.24.own, ...), custom_call_target="tpu_custom_call" | custom-call | flops 3000000000 | bytes 9000000 | tf_op jit(solution)/shard_map/pallas_call | solution.py:191
  24.7 0.7 %collective-permute-start.11 = (bf16[64,4096]{1,0:T(8,128)(2,1)S(1)}, bf16[64,4096]{1,0:T(8,128)(2,1)S(1)}, u32[]{:S(2)}, u32[]{:S(2)}) collective-permute-start(bf16[64,4096]{1,0:T(8,128)(2,1)S(1)} %get-tuple-element.30), channel_id=1, source_target_pairs={{0,1},{1,0},{2,3},{3,2},{4,7},{5,6},{6,5},{7,4},{8,9},{9,8},{10,11... | collective-permute-start | bytes 1572872 | tf_op jit(solution)/shard_map/near_pairs/ppermute | solution.py:323
  25.3 4.5 %collective-permute-done.4.refs_2_ = bf16[2560,128]{1,0:T(8,128)(2,1)S(1)} collective-permute-done((bf16[2560,128]{1,0:T(8,128)(2,1)S(1)}, bf16[2560,128]{1,0:T(8,128)(2,1)S(1)}, u32[]{:S(2)}, u32[]{:S(2)}) %collective-permute-start.4) | collective-permute-done | bytes 655392 | tf_op jit(solution)/shard_map/side_a/ppermute | solution.py:318
  29.9 3.7 %collective-permute-done.3.refs_1_ = bf16[2560,128]{1,0:T(8,128)(2,1)S(1)} collective-permute-done((bf16[2560,128]{1,0:T(8,128)(2,1)S(1)}, bf16[2560,128]{1,0:T(8,128)(2,1)S(1)}, u32[]{:S(2)}, u32[]{:S(2)}) %collective-permute-start.3) | collective-permute-done | bytes 655392 | tf_op jit(solution)/shard_map/side_b/ppermute | solution.py:318
  33.7 2.0 %collective-permute-start.9 = (bf16[1280,128]{1,0:T(8,128)(2,1)S(1)}, bf16[1280,128]{1,0:T(8,128)(2,1)S(1)}, u32[]{:S(2)}, u32[]{:S(2)}) collective-permute-start(bf16[1280,128]{1,0:T(8,128)(2,1)S(1)} %slice.18), channel_id=1, source_target_pairs={{0,32},{4,12},{8,40},{12,20},{16,48},{20,28},{24,56},{28,4},{32,64... | collective-permute-start | bytes 983048 | tf_op jit(solution)/shard_map/far_b/ppermute | solution.py:318
  35.7 0.5 %collective-permute-start.13 = (bf16[2560,128]{1,0:T(8,128)(2,1)S(1)}, bf16[2560,128]{1,0:T(8,128)(2,1)S(1)}, u32[]{:S(2)}, u32[]{:S(2)}) collective-permute-start(bf16[2560,128]{1,0:T(8,128)(2,1)S(1)} %collective-permute-done.4.refs_2_), channel_id=1, source_target_pairs={{0,4},{4,0},{8,12},{12,8},{16,20},{20,16},{24,28},{28,24},{32,36},... | collective-permute-start | bytes 1966088 | tf_op jit(solution)/shard_map/swap_side/ppermute | solution.py:318
  36.3 1.9 %collective-permute-start.18 = (bf16[32,4096]{1,0:T(8,128)(2,1)S(1)}, bf16[32,4096]{1,0:T(8,128)(2,1)S(1)}, u32[]{:S(2)}, u32[]{:S(2)}) collective-permute-start(bf16[32,4096]{1,0:T(8,128)(2,1)S(1)} %shard_map.103), channel_id=1, source_target_pairs={{0,3},{1,2},{2,1},{3,0},{4,5},{5,4},{6,7},{7,6},{8,11},{9,10},{10,... | collective-permute-start | bytes 786440 | tf_op jit(solution)/shard_map/near_last/ppermute | solution.py:323
  38.3 2.5 %collective-permute-done.10.refs_4_ = bf16[1280,128]{1,0:T(8,128)(2,1)S(1)} collective-permute-done((bf16[1280,128]{1,0:T(8,128)(2,1)S(1)}, bf16[1280,128]{1,0:T(8,128)(2,1)S(1)}, u32[]{:S(2)}, u32[]{:S(2)}) %collective-permute-start.10) | collective-permute-done | bytes 327712 | tf_op jit(solution)/shard_map/far_a/ppermute | solution.py:318
  40.8 1.3 %collective-permute-done.9.refs_3_ = bf16[1280,128]{1,0:T(8,128)(2,1)S(1)} collective-permute-done((bf16[1280,128]{1,0:T(8,128)(2,1)S(1)}, bf16[1280,128]{1,0:T(8,128)(2,1)S(1)}, u32[]{:S(2)}, u32[]{:S(2)}) %collective-permute-start.9) | collective-permute-done | bytes 327712 | tf_op jit(solution)/shard_map/far_b/ppermute | solution.py:318
  42.2 0.5 %collective-permute-start.14 = (bf16[640,128]{1,0:T(8,128)(2,1)S(1)}, bf16[640,128]{1,0:T(8,128)(2,1)S(1)}, u32[]{:S(2)}, u32[]{:S(2)}) collective-permute-start(bf16[640,128]{1,0:T(8,128)(2,1)S(1)} %get-tuple-element.38), channel_id=1, source_target_pairs={{0,4},{4,0},{8,12},{12,8},{16,20},{20,16},{24,28},{28,24},{32,36},... | collective-permute-start | bytes 491528 | tf_op jit(solution)/shard_map/swap_far/ppermute | solution.py:318
  42.9 0.4 collective-permute-start.16
  43.8 0.4 collective-permute-done.17.refs_11_
  44.5 3.6 %shard_map.104.down = bf16[32,2048]{1,0:T(8,128)(2,1)S(1)} custom-call(s32[8,32]{1,0:T(8,128)S(1)} %get-tuple-element.20.leaf_codes, s32[8,8]{1,0:T(8,128)S(1)} %get-tuple-element.21.par_codes, bf16[2560,128]{1,0:T(8,128)(2,1)S(1)} %shard_map.101.refs_0_, bf16[2560,128]{1,0:T(8,128)(2,1)S(1)} %collective-permute-done.3.refs_1_, ...), custom_call_target="tpu_custom_call" | custom-call | tf_op jit(solution)/shard_map/pallas_call | solution.py:257
  48.1 1.0 %shard_map.105 = bf16[32,4096]{1,0:T(8,128)(2,1)} custom-call(bf16[32,2048]{1,0:T(8,128)(2,1)S(1)} %shard_map.104.down, bf16[32,64,128]{2,1,0:T(8,128)(2,1)S(1)} %bitcast.7, bf16[32,4096]{1,0:T(8,128)(2,1)S(1)} %get-tuple-element.34.keep, bf16[64,4096]{1,0:T(8,128)(2,1)S(1)} %collective-permute-done.11.taken, bf16[32,4096]{1,0:T(8,128)(2,1)S(1)} %collective-permute-done.18.passed), custom_call_target="tpu_custom_call" | custom-call | tf_op jit(solution)/shard_map/pallas_call | solution.py:280
  (34 shorter events, 1.7 us)
Async XLA Ops:
  1.1 10.2 %collective-permute-start.6 = (bf16[64,4096]{1,0:T(8,128)(2,1)S(1)}, bf16[64,4096]{1,0:T(8,128)(2,1)S(1)}, u32[]{:S(2)}, u32[]{:S(2)}) collective-permute-start(bf16[64,4096]{1,0:T(8,128)(2,1)S(1)} %constant_dynamic-slice_fusion), channel_id=1, source_target_pairs={{0,124},{4,8},{8,4},{12,16},{16,12},{20,24},{24,20},{28,32},{32,28... | collective-permute-start | bytes 1572872 | tf_op jit(solution)/shard_map/halo/ppermute | solution.py:318
  1.4 20.3 %collective-permute-start.5 = (bf16[128,4096]{1,0:T(8,128)(2,1)}, bf16[128,4096]{1,0:T(8,128)(2,1)S(1)}, u32[]{:S(2)}, u32[]{:S(2)}) collective-permute-start(bf16[128,4096]{1,0:T(8,128)(2,1)} %refs_0_.1), channel_id=1, source_target_pairs={{0,4},{4,0},{8,12},{12,8},{16,20},{20,16},{24,28},{28,24},{32,36},... | collective-permute-start | bytes 3145736 | tf_op jit(solution)/shard_map/sibling/ppermute | solution.py:318
  6.5 7.0 %collective-permute-start.2 = (bf16[640,128]{1,0:T(8,128)(2,1)S(1)}, bf16[640,128]{1,0:T(8,128)(2,1)S(1)}, u32[]{:S(2)}, u32[]{:S(2)}) collective-permute-start(bf16[640,128]{1,0:T(8,128)(2,1)S(1)} %get-tuple-element.22.refs_0_), channel_id=1, source_target_pairs={{0,16},{4,68},{8,24},{12,76},{16,0},{20,84},{24,8},{28,92},{32,48}... | collective-permute-start | bytes 491528 | tf_op jit(solution)/shard_map/across/ppermute | solution.py:318
  8.0 8.9 %collective-permute-start.1 = (bf16[640,128]{1,0:T(8,128)(2,1)S(1)}, bf16[640,128]{1,0:T(8,128)(2,1)S(1)}, u32[]{:S(2)}, u32[]{:S(2)}) collective-permute-start(bf16[640,128]{1,0:T(8,128)(2,1)S(1)} %get-tuple-element.22.refs_0_), channel_id=1, source_target_pairs={{0,24},{4,100},{8,0},{12,108},{16,8},{20,116},{24,16},{28,124},{32... | collective-permute-start | bytes 491528 | tf_op jit(solution)/shard_map/after/ppermute | solution.py:318
  11.0 6.0 %collective-permute-start = (bf16[640,128]{1,0:T(8,128)(2,1)S(1)}, bf16[640,128]{1,0:T(8,128)(2,1)S(1)}, u32[]{:S(2)}, u32[]{:S(2)}) collective-permute-start(bf16[640,128]{1,0:T(8,128)(2,1)S(1)} %get-tuple-element.22.refs_0_), channel_id=1, source_target_pairs={{0,8},{4,36},{8,16},{12,44},{16,24},{20,52},{24,0},{28,60},{32,40}... | collective-permute-start | bytes 491528 | tf_op jit(solution)/shard_map/before/ppermute | solution.py:318
  11.3 10.5 %collective-permute-start.7 = (bf16[64,4096]{1,0:T(8,128)(2,1)S(1)}, bf16[64,4096]{1,0:T(8,128)(2,1)S(1)}, u32[]{:S(2)}, u32[]{:S(2)}) collective-permute-start(bf16[64,4096]{1,0:T(8,128)(2,1)S(1)} %collective-permute-done.6.far_mine), channel_id=1, source_target_pairs={{0,1},{1,0},{2,3},{3,2},{4,7},{5,6},{6,5},{7,4},{8,9},{9,8},{10,11... | collective-permute-start | bytes 1572872 | tf_op jit(solution)/shard_map/halo_half/ppermute | solution.py:323
  17.0 8.3 %collective-permute-start.8 = (bf16[2560,128]{1,0:T(8,128)(2,1)S(1)}, bf16[2560,128]{1,0:T(8,128)(2,1)S(1)}, u32[]{:S(2)}, u32[]{:S(2)}) collective-permute-start(bf16[2560,128]{1,0:T(8,128)(2,1)S(1)} %shard_map.101.refs_0_), channel_id=1, source_target_pairs={{0,4},{4,0},{8,12},{12,8},{16,20},{20,16},{24,28},{28,24},{32,36},... | collective-permute-start | bytes 1966088 | tf_op jit(solution)/shard_map/swap_own/ppermute | solution.py:318
  17.1 12.8 %collective-permute-start.4 = (bf16[2560,128]{1,0:T(8,128)(2,1)S(1)}, bf16[2560,128]{1,0:T(8,128)(2,1)S(1)}, u32[]{:S(2)}, u32[]{:S(2)}) collective-permute-start(bf16[2560,128]{1,0:T(8,128)(2,1)S(1)} %shard_map.101.refs_0_), channel_id=1, source_target_pairs={{0,96},{4,28},{8,104},{12,4},{16,112},{20,12},{24,120},{28,20},{32... | collective-permute-start | bytes 1966088 | tf_op jit(solution)/shard_map/side_a/ppermute | solution.py:318
  21.8 11.8 %collective-permute-start.3 = (bf16[2560,128]{1,0:T(8,128)(2,1)S(1)}, bf16[2560,128]{1,0:T(8,128)(2,1)S(1)}, u32[]{:S(2)}, u32[]{:S(2)}) collective-permute-start(bf16[2560,128]{1,0:T(8,128)(2,1)S(1)} %shard_map.101.refs_0_), channel_id=1, source_target_pairs={{0,32},{4,12},{8,40},{12,20},{16,48},{20,28},{24,56},{28,4},{32,64... | collective-permute-start | bytes 1966088 | tf_op jit(solution)/shard_map/side_b/ppermute | solution.py:318
  24.7 11.6 %collective-permute-start.11 = (bf16[64,4096]{1,0:T(8,128)(2,1)S(1)}, bf16[64,4096]{1,0:T(8,128)(2,1)S(1)}, u32[]{:S(2)}, u32[]{:S(2)}) collective-permute-start(bf16[64,4096]{1,0:T(8,128)(2,1)S(1)} %get-tuple-element.30), channel_id=1, source_target_pairs={{0,1},{1,0},{2,3},{3,2},{4,7},{5,6},{6,5},{7,4},{8,9},{9,8},{10,11... | collective-permute-start | bytes 1572872 | tf_op jit(solution)/shard_map/near_pairs/ppermute | solution.py:323
  33.6 10.8 %copy-start.1 = (bf16[8,8,64,64]{3,2,1,0:T(8,128)(2,1)S(1)}, bf16[8,8,64,64]{3,2,1,0:T(8,128)(2,1)}, u32[]{:S(2)}) copy-start(bf16[8,8,64,64]{3,2,1,0:T(8,128)(2,1)} %refs_13_.1) | copy-start | bytes 1572868
  33.6 10.8 %copy-start.2 = (bf16[32,64,64]{2,1,0:T(8,128)(2,1)S(1)}, bf16[32,64,64]{2,1,0:T(8,128)(2,1)}, u32[]{:S(2)}) copy-start(bf16[32,64,64]{2,1,0:T(8,128)(2,1)} %refs_14_.1) | copy-start | bytes 786436
  33.6 7.1 %collective-permute-start.10 = (bf16[1280,128]{1,0:T(8,128)(2,1)S(1)}, bf16[1280,128]{1,0:T(8,128)(2,1)S(1)}, u32[]{:S(2)}, u32[]{:S(2)}) collective-permute-start(bf16[1280,128]{1,0:T(8,128)(2,1)S(1)} %slice.19), channel_id=1, source_target_pairs={{0,96},{4,28},{8,104},{12,4},{16,112},{20,12},{24,120},{28,20},{32... | collective-permute-start | bytes 983048 | tf_op jit(solution)/shard_map/far_a/ppermute | solution.py:318
  33.7 8.4 %collective-permute-start.9 = (bf16[1280,128]{1,0:T(8,128)(2,1)S(1)}, bf16[1280,128]{1,0:T(8,128)(2,1)S(1)}, u32[]{:S(2)}, u32[]{:S(2)}) collective-permute-start(bf16[1280,128]{1,0:T(8,128)(2,1)S(1)} %slice.18), channel_id=1, source_target_pairs={{0,32},{4,12},{8,40},{12,20},{16,48},{20,28},{24,56},{28,4},{32,64... | collective-permute-start | bytes 983048 | tf_op jit(solution)/shard_map/far_b/ppermute | solution.py:318
  35.7 7.0 %collective-permute-start.12 = (bf16[2560,128]{1,0:T(8,128)(2,1)S(1)}, bf16[2560,128]{1,0:T(8,128)(2,1)S(1)}, u32[]{:S(2)}, u32[]{:S(2)}) collective-permute-start(bf16[2560,128]{1,0:T(8,128)(2,1)S(1)} %collective-permute-done.3.refs_1_), channel_id=1, source_target_pairs={{0,4},{4,0},{8,12},{12,8},{16,20},{20,16},{24,28},{28,24},{32,36},... | collective-permute-start | bytes 1966088 | tf_op jit(solution)/shard_map/swap_side/ppermute | solution.py:318
  35.7 7.2 %collective-permute-start.13 = (bf16[2560,128]{1,0:T(8,128)(2,1)S(1)}, bf16[2560,128]{1,0:T(8,128)(2,1)S(1)}, u32[]{:S(2)}, u32[]{:S(2)}) collective-permute-start(bf16[2560,128]{1,0:T(8,128)(2,1)S(1)} %collective-permute-done.4.refs_2_), channel_id=1, source_target_pairs={{0,4},{4,0},{8,12},{12,8},{16,20},{20,16},{24,28},{28,24},{32,36},... | collective-permute-start | bytes 1966088 | tf_op jit(solution)/shard_map/swap_side/ppermute | solution.py:318
  36.2 8.2 %copy-start = (bf16[32,8,64,64]{3,2,1,0:T(8,128)(2,1)S(1)}, bf16[32,8,64,64]{3,2,1,0:T(8,128)(2,1)}, u32[]{:S(2)}) copy-start(bf16[32,8,64,64]{3,2,1,0:T(8,128)(2,1)} %refs_12_.1) | copy-start | bytes 6291460
  36.3 11.8 %collective-permute-start.18 = (bf16[32,4096]{1,0:T(8,128)(2,1)S(1)}, bf16[32,4096]{1,0:T(8,128)(2,1)S(1)}, u32[]{:S(2)}, u32[]{:S(2)}) collective-permute-start(bf16[32,4096]{1,0:T(8,128)(2,1)S(1)} %shard_map.103), channel_id=1, source_target_pairs={{0,3},{1,2},{2,1},{3,0},{4,5},{5,4},{6,7},{7,6},{8,11},{9,10},{10,... | collective-permute-start | bytes 786440 | tf_op jit(solution)/shard_map/near_last/ppermute | solution.py:323
  42.1 1.5 %collective-permute-start.15 = (bf16[640,128]{1,0:T(8,128)(2,1)S(1)}, bf16[640,128]{1,0:T(8,128)(2,1)S(1)}, u32[]{:S(2)}, u32[]{:S(2)}) collective-permute-start(bf16[640,128]{1,0:T(8,128)(2,1)S(1)} %get-tuple-element.37), channel_id=1, source_target_pairs={{0,4},{4,0},{8,12},{12,8},{16,20},{20,16},{24,28},{28,24},{32,36},... | collective-permute-start | bytes 491528 | tf_op jit(solution)/shard_map/swap_far/ppermute | solution.py:318
  42.2 1.6 %collective-permute-start.14 = (bf16[640,128]{1,0:T(8,128)(2,1)S(1)}, bf16[640,128]{1,0:T(8,128)(2,1)S(1)}, u32[]{:S(2)}, u32[]{:S(2)}) collective-permute-start(bf16[640,128]{1,0:T(8,128)(2,1)S(1)} %get-tuple-element.38), channel_id=1, source_target_pairs={{0,4},{4,0},{8,12},{12,8},{16,20},{20,16},{24,28},{28,24},{32,36},... | collective-permute-start | bytes 491528 | tf_op jit(solution)/shard_map/swap_far/ppermute | solution.py:318
  42.7 1.5 %collective-permute-start.17 = (bf16[640,128]{1,0:T(8,128)(2,1)S(1)}, bf16[640,128]{1,0:T(8,128)(2,1)S(1)}, u32[]{:S(2)}, u32[]{:S(2)}) collective-permute-start(bf16[640,128]{1,0:T(8,128)(2,1)S(1)} %get-tuple-element.35), channel_id=1, source_target_pairs={{0,4},{4,0},{8,12},{12,8},{16,20},{20,16},{24,28},{28,24},{32,36},... | collective-permute-start | bytes 491528 | tf_op jit(solution)/shard_map/swap_far/ppermute | solution.py:318
  42.9 1.5 %collective-permute-start.16 = (bf16[640,128]{1,0:T(8,128)(2,1)S(1)}, bf16[640,128]{1,0:T(8,128)(2,1)S(1)}, u32[]{:S(2)}, u32[]{:S(2)}) collective-permute-start(bf16[640,128]{1,0:T(8,128)(2,1)S(1)} %get-tuple-element.36), channel_id=1, source_target_pairs={{0,4},{4,0},{8,12},{12,8},{16,20},{20,16},{24,28},{28,24},{32,36},... | collective-permute-start | bytes 491528 | tf_op jit(solution)/shard_map/swap_far/ppermute | solution.py:318
  44.4 3.7 %copy-start.3 = (bf16[32,128,64]{1,2,0:T(8,128)(2,1)S(1)}, bf16[32,128,64]{1,2,0:T(8,128)(2,1)}, u32[]{:S(2)}) copy-start(bf16[32,128,64]{1,2,0:T(8,128)(2,1)} %param.11) | copy-start | bytes 1572868
